TPU v7x, 512 devices: a whole 4x4x16 slice. The times are simulated.
512 devices in a mesh: dp: 32 (over z, y_hi), tensor: 16 (over x, y_lo, core).
Axes of the slice: x: 4, y: 4 (y_hi: 2, y_lo: 2; y = y_hi * 2 + y_lo), z: 16, core: 2. Of those that a mesh axis runs over, the one named last changes fastest.
Arguments:
- gradient: bfloat16 [8192, 28672], P('dp', 'tensor'), may hold values from -5 to 5
- left_codes: bfloat16 [32, 1024, 1024], P('dp', 'tensor'), may hold values from -1 to 1
- left_scales: float32 [32, 1024, 8], P('dp', 'tensor'), may hold values from 0.05 to 0.5
Outputs:
- new_codes: bfloat16 [32, 1024, 1024], P('dp', 'tensor')
- new_scales: float32 [32, 1024, 8], P('dp', 'tensor')
All inputs are finite; a program needn't handle non-finite values. Where the computation divides by a largest or mean magnitude, that divisor is 1e-20 or more.
Results may differ from a plain program's by a relative error of at most 0.001.
Values may be sent and summed in bfloat16 or wider, within the bound.
No kernel may reach another device: no remote copies, remote signals or barrier semaphores. Data moves between devices by JAX's collectives and lax.ppermute only.
A program may use at most 64 MiB of HBM per device.

v0:
```python
import math

import jax
import jax.numpy as jnp
from jax import lax
from jax.sharding import PartitionSpec as P

GROUP = 128
BLOCKS = 2


def swapped(array, axis, distance):
    return lax.ppermute(array, axis, [(i, i ^ 1 << distance) for i in range(lax.axis_size(axis))])


def hadamard_table(matrix_order):
    index_row = lax.broadcasted_iota(jnp.int32, (matrix_order, matrix_order), 0)
    index_col = lax.broadcasted_iota(jnp.int32, (matrix_order, matrix_order), 1)
    parity = jnp.zeros((matrix_order, matrix_order), jnp.int32)
    for bit_pos in range(matrix_order.bit_length() - 1):
        parity = parity + jnp.right_shift(index_row, bit_pos) % 2 * (
            jnp.right_shift(index_col, bit_pos) % 2
        )
    signs = 1.0 - 2.0 * (parity % 2).astype(jnp.float32)
    return signs / jnp.sqrt(jnp.float32(matrix_order))


def rotate(values, hadamard):
    group_size = hadamard.shape[0]
    row_total, col_total = values.shape
    grouped = values.reshape(row_total, col_total // group_size, group_size)
    turned = jnp.einsum("rkn,nm->rkm", grouped, hadamard, precision=lax.Precision.HIGHEST)
    return turned.reshape(row_total, col_total)


def refresh(old_codes, old_scales, gram, hadamard):
    group_size = hadamard.shape[0]
    row_total, col_total = gram.shape
    grouped = old_codes.astype(jnp.float32).reshape(row_total, col_total // group_size, group_size)
    dequant = (grouped * old_scales[:, :, None]).reshape(row_total, col_total)
    old_factor = rotate(dequant, hadamard)
    blended = 0.95 * old_factor + 0.05 * gram
    rotated = rotate(blended, hadamard).reshape(row_total, col_total // group_size, group_size)
    fresh_scales = jnp.max(jnp.abs(rotated), axis=2)
    fresh_codes = (rotated / (fresh_scales[:, :, None] + 1e-06)).reshape(row_total, col_total)
    return (fresh_codes.astype(jnp.bfloat16), fresh_scales)


def join_halves(held_rows, partner, bit_pos):
    is_upper = jnp.right_shift(lax.axis_index("dp"), bit_pos) % 2 == 1
    lower_half = jnp.where(is_upper, partner, held_rows)
    upper_half = jnp.where(is_upper, held_rows, partner)
    return jnp.concatenate([lower_half, upper_half], axis=0)


def per_device(gradient, left_codes, left_scales):
    side_len = math.isqrt(lax.axis_size("dp") // BLOCKS)
    side_bits = side_len.bit_length() - 1
    tile_rows = gradient
    for depth_no in range(side_bits):
        partner = swapped(tile_rows, "dp", depth_no)
        tile_rows = join_halves(tile_rows, partner, depth_no)
    tile_cols = gradient
    for depth_no in range(side_bits):
        partner = swapped(tile_cols, "dp", side_bits + depth_no)
        tile_cols = join_halves(tile_cols, partner, side_bits + depth_no)
    gram = lax.psum_scatter(
        lax.dot_general(
            tile_rows, tile_cols, (((1,), (1,)), ((), ())), preferred_element_type=jnp.float32
        ),
        "tensor",
        scatter_dimension=0,
        tiled=True,
    )
    fresh_codes, fresh_scales = refresh(left_codes[0], left_scales[0], gram, hadamard_table(GROUP))
    return (fresh_codes[None], fresh_scales[None])


def solution(mesh):
    return jax.shard_map(
        per_device,
        mesh=mesh,
        in_specs=(P("dp", "tensor"), P("dp", "tensor", None), P("dp", "tensor", None)),
        out_specs=(P("dp", "tensor", None), P("dp", "tensor", None)),
        check_vma=False,
    )
```

profile of v0, /device:TPU:7, one launch (start us, length us, event | category | flops | bytes accessed | tf_op | source)
XLA Modules:
  0.0 318.1 jit_solution(7847173273732428976)
XLA Ops:
  7.2 0.0 reduce-scatter.2.cloned.1.call-start
  7.2 4.8 %collective-permute-start = (bf16[256,1792]{1,0:T(8,128)(2,1)}, bf16[256,1792]{1,0:T(8,128)(2,1)S(1)}, u32[]{:S(2)}, u32[]{:S(2)}) collective-permute-start(bf16[256,1792]{1,0:T(8,128)(2,1)} %param.3), channel_id=1, source_target_pairs={{0,16},{16,0},{32,48},{48,32},{64,80},{80,64},{96,112},{112,96},{1... | collective-permute-start | bytes 2752520 | tf_op jit(solution)/shard_map/ppermute | solution.py:13
  12.0 4.9 %collective-permute-start.2 = (bf16[256,1792]{1,0:T(8,128)(2,1)}, bf16[256,1792]{1,0:T(8,128)(2,1)}, u32[]{:S(2)}, u32[]{:S(2)}) collective-permute-start(bf16[256,1792]{1,0:T(8,128)(2,1)} %param.3), channel_id=1, source_target_pairs={{0,64},{16,80},{32,96},{48,112},{64,0},{80,16},{96,32},{112,48},{1... | collective-permute-start | bytes 2752520 | tf_op jit(solution)/shard_map/ppermute | solution.py:13
  17.0 15.1 %collective-permute-done = bf16[256,1792]{1,0:T(8,128)(2,1)S(1)} collective-permute-done((bf16[256,1792]{1,0:T(8,128)(2,1)}, bf16[256,1792]{1,0:T(8,128)(2,1)S(1)}, u32[]{:S(2)}, u32[]{:S(2)}) %collective-permute-start) | collective-permute-done | bytes 917536 | tf_op jit(solution)/shard_map/ppermute | solution.py:13
  32.0 0.0 copy-start.1
  32.0 1.0 copy-done.1
  33.0 23.7 %collective-permute-done.2 = bf16[256,1792]{1,0:T(8,128)(2,1)} collective-permute-done((bf16[256,1792]{1,0:T(8,128)(2,1)}, bf16[256,1792]{1,0:T(8,128)(2,1)}, u32[]{:S(2)}, u32[]{:S(2)}) %collective-permute-start.2) | collective-permute-done | bytes 917536 | tf_op jit(solution)/shard_map/ppermute | solution.py:13
  56.7 2.0 broadcast_select_fusion.5
  58.6 0.0 copy-start
  58.7 1.5 pad_maximum_fusion.1
  60.1 0.0 copy-done
  60.2 8.8 %collective-permute-start.3 = (bf16[512,1792]{1,0:T(8,128)(2,1)}, bf16[512,1792]{1,0:T(8,128)(2,1)}, u32[]{:S(2)}, u32[]{:S(2)}) collective-permute-start(bf16[512,1792]{1,0:T(8,128)(2,1)} %pad_maximum_fusion.1), channel_id=1, source_target_pairs={{0,128},{16,144},{32,160},{48,176},{64,192},{80,208},{96,224},{112... | collective-permute-start | bytes 5505032 | tf_op jit(solution)/shard_map/ppermute | solution.py:13
  69.0 1.4 pad_maximum_fusion
  70.4 3.4 %collective-permute-start.1 = (bf16[512,1792]{1,0:T(8,128)(2,1)}, bf16[512,1792]{1,0:T(8,128)(2,1)}, u32[]{:S(2)}, u32[]{:S(2)}) collective-permute-start(bf16[512,1792]{1,0:T(8,128)(2,1)} %pad_maximum_fusion), channel_id=1, source_target_pairs={{0,32},{16,48},{32,0},{48,16},{64,96},{80,112},{96,64},{112,80},{1... | collective-permute-start | bytes 5505032 | tf_op jit(solution)/shard_map/ppermute | solution.py:13
  73.8 153.0 %collective-permute-done.3 = bf16[512,1792]{1,0:T(8,128)(2,1)} collective-permute-done((bf16[512,1792]{1,0:T(8,128)(2,1)}, bf16[512,1792]{1,0:T(8,128)(2,1)}, u32[]{:S(2)}, u32[]{:S(2)}) %collective-permute-start.3) | collective-permute-done | bytes 1835040 | tf_op jit(solution)/shard_map/ppermute | solution.py:13
  226.8 2.4 broadcast_select_fusion.1
  229.1 0.0 collective-permute-done.1
  229.2 2.2 broadcast_select_fusion.3
  231.3 5.9 %fusion = f32[1024,1024]{1,0:T(8,128)} fusion(bf16[512,1792]{1,0:T(8,128)(2,1)S(1)} %get-tuple-element.7, bf16[512,1792]{1,0:T(8,128)(2,1)S(1)} %get-tuple-element.6, bf16[512,1792]{1,0:T(8,128)(2,1)S(1)} %get-tuple-element.5, bf16[512,1792]{1,0:T(8,128)(2,1)S(1)} %get-tuple-element.4), kind=kOutput, calls=%fused_computation | convolution fusion | flops 3772776448 | bytes 11534336 | tf_op jit(solution)/shard_map/dot_general | solution.py:68
  237.2 0.0 copy-start.2
  237.2 0.0 copy-start.3
  237.2 0.0 reduce-scatter.2.cloned.1.call-update
  237.3 0.9 copy-done.2
  238.2 0.0 copy-done.3
  238.2 0.1 copy.7
  238.5 0.1 bitcast_multiply_fusion
  238.6 0.8 convolution_multiply_fusion
  239.4 68.4 %reduce-scatter.2.cloned.1.call-done = f32[64,1024]{1,0:T(8,128)} async-done(((f32[1024,1024]{1,0:T(8,128)}), f32[64,1024]{1,0:T(8,128)}) %reduce-scatter.2.cloned.1.call-update) | async-done | bytes 262160 | tf_op jit(solution)/shard_map/reduce_scatter | solution.py:67
  307.8 1.0 fusion.7
  308.9 0.9 abs_reduce_fusion
  309.8 0.1 divide_convert_fusion
  309.9 0.7 convert_element_type.29
  310.6 0.7 copy.8
  (15 shorter events, 0.2 us)
Async XLA Ops:
  7.2 300.7 %reduce-scatter.2.cloned.1.call-start = ((), (), s32[]{:S(2)}) async-start(), calls=%async_computation.1 | async-start | bytes 4456448 | tf_op jit(solution)/shard_map/reduce_scatter | solution.py:67
  7.2 24.8 %collective-permute-start = (bf16[256,1792]{1,0:T(8,128)(2,1)}, bf16[256,1792]{1,0:T(8,128)(2,1)S(1)}, u32[]{:S(2)}, u32[]{:S(2)}) collective-permute-start(bf16[256,1792]{1,0:T(8,128)(2,1)} %param.3), channel_id=1, source_target_pairs={{0,16},{16,0},{32,48},{48,32},{64,80},{80,64},{96,112},{112,96},{1... | collective-permute-start | bytes 2752520 | tf_op jit(solution)/shard_map/ppermute | solution.py:13
  12.0 44.6 %collective-permute-start.2 = (bf16[256,1792]{1,0:T(8,128)(2,1)}, bf16[256,1792]{1,0:T(8,128)(2,1)}, u32[]{:S(2)}, u32[]{:S(2)}) collective-permute-start(bf16[256,1792]{1,0:T(8,128)(2,1)} %param.3), channel_id=1, source_target_pairs={{0,64},{16,80},{32,96},{48,112},{64,0},{80,16},{96,32},{112,48},{1... | collective-permute-start | bytes 2752520 | tf_op jit(solution)/shard_map/ppermute | solution.py:13
  32.0 1.0 copy-start.1
  58.6 1.5 copy-start
  60.2 166.6 %collective-permute-start.3 = (bf16[512,1792]{1,0:T(8,128)(2,1)}, bf16[512,1792]{1,0:T(8,128)(2,1)}, u32[]{:S(2)}, u32[]{:S(2)}) collective-permute-start(bf16[512,1792]{1,0:T(8,128)(2,1)} %pad_maximum_fusion.1), channel_id=1, source_target_pairs={{0,128},{16,144},{32,160},{48,176},{64,192},{80,208},{96,224},{112... | collective-permute-start | bytes 5505032 | tf_op jit(solution)/shard_map/ppermute | solution.py:13
  70.4 158.8 %collective-permute-start.1 = (bf16[512,1792]{1,0:T(8,128)(2,1)}, bf16[512,1792]{1,0:T(8,128)(2,1)}, u32[]{:S(2)}, u32[]{:S(2)}) collective-permute-start(bf16[512,1792]{1,0:T(8,128)(2,1)} %pad_maximum_fusion), channel_id=1, source_target_pairs={{0,32},{16,48},{32,0},{48,16},{64,96},{80,112},{96,64},{112,80},{1... | collective-permute-start | bytes 5505032 | tf_op jit(solution)/shard_map/ppermute | solution.py:13
  237.2 0.9 copy-start.2
  237.2 1.0 copy-start.3
Sparse Core Ops, SparseCore 0:
  237.4 70.3 reduce-scatter.1
where the time goes:
time: 323 us; the launch traced here: 318 us
  waiting for transfers between devices  260 us (80%)
  starting transfers between devices  22 us (7%)
  between operations  14.2 us (4%)
  other arithmetic  10.8 us (3%)
  matrix products  7.59 us (2%)
  local copies, waits for them, and re-layouts  3.44 us (1%)
    ppermute x4, waiting for transfers between devices, swapped(): lax.ppermute(array, axis, [(i, i ^ 1 << distance) for i in range(lax.axis...  192 us
    reduce_scatter x1, waiting for transfers between devices, per_device(): lax.psum_scatter(lax.dot_general(tile_rows, tile_cols, (((1,), (1,)), (()...  68.4 us
    ppermute x4, starting transfers between devices, swapped(): lax.ppermute(array, axis, [(i, i ^ 1 << distance) for i in range(lax.axis...  21.9 us
    select_n x3, other arithmetic, join_halves(): lower_half = jnp.where(is_upper, partner, held_rows)  6.52 us
  transfers between devices with their start and end apart: 5, of which 4 were waited for; matrix products, arithmetic and copies ran while one was open for 2% of the time, Pallas kernels for 0%

commit v1 on v0

v1 whole, which is shorter than its diff:
```python
import jax
import jax.numpy as jnp
from jax import lax
from jax.sharding import PartitionSpec as P

GROUP = 128
AXES = ("dp", "tensor")
SUPERS = 4


def place(index):
    dp, tensor = divmod(index, 16)
    return dict(
        b=dp >> 4, g=(dp >> 2) & 3, h=dp & 3, x=tensor >> 2, yl=(tensor >> 1) & 1, c=tensor & 1
    )


def index_of(b, g, h, x, yl, c):
    return ((b << 4 | g << 2 | h) << 4) | x << 2 | yl << 1 | c


def permute(array, target, keep=lambda at: True):
    total = lax.axis_size("dp") * lax.axis_size("tensor")
    pairs = []
    for i in range(total):
        at = place(i)
        if keep(at):
            pairs.append((i, index_of(**{**at, **target(at)})))
    return lax.ppermute(array, AXES, pairs)


def reach(at):
    return at["g"] if at["c"] == 0 else SUPERS - 1 - at["g"]


def onward(at):
    return dict(g=at["g"] + (1 if at["c"] == 0 else -1))


def hadamard_table(matrix_order):
    index_row = lax.broadcasted_iota(jnp.int32, (matrix_order, matrix_order), 0)
    index_col = lax.broadcasted_iota(jnp.int32, (matrix_order, matrix_order), 1)
    parity = jnp.zeros((matrix_order, matrix_order), jnp.int32)
    for bit_pos in range(matrix_order.bit_length() - 1):
        parity = parity + jnp.right_shift(index_row, bit_pos) % 2 * (
            jnp.right_shift(index_col, bit_pos) % 2
        )
    signs = 1.0 - 2.0 * (parity % 2).astype(jnp.float32)
    return signs / jnp.sqrt(jnp.float32(matrix_order))


def refresh(old_codes, old_scales, gram, hadamard):
    rows, cols = gram.shape
    groups = cols // GROUP
    grouped = gram.reshape(rows, groups, GROUP)
    turned = jnp.einsum("rkn,nm->rkm", grouped, hadamard, precision=lax.Precision.HIGHEST)
    dequant = old_codes.astype(jnp.float32).reshape(rows, groups, GROUP) * old_scales[:, :, None]
    rotated = 0.95 * dequant + 0.05 * turned
    fresh_scales = jnp.max(jnp.abs(rotated), axis=2)
    fresh_codes = (rotated / (fresh_scales[:, :, None] + 1e-06)).reshape(rows, cols)
    return fresh_codes.astype(jnp.bfloat16), fresh_scales


def swap_if(flag, first, second):
    return jnp.where(flag, second, first), jnp.where(flag, first, second)


def per_device(gradient, left_codes, left_scales):
    dp, tensor = lax.axis_index("dp"), lax.axis_index("tensor")
    g, h = (dp >> 2) & 3, dp & 3
    x, yl, c = tensor >> 2, (tensor >> 1) & 1, tensor & 1
    block = gradient.shape[0]
    half, quarter = block // 2, block // 4

    passing = [gradient]
    for step in range(1, SUPERS):
        passing.append(
            permute(
                passing[-1],
                onward,
                lambda at, step=step: step - 1 <= reach(at) < SUPERS - 1,
            )
        )

    z_block = permute(gradient, lambda at: dict(h=at["h"] ^ 2))
    y_block = permute(gradient, lambda at: dict(h=at["h"] ^ 1))
    zy_block = permute(z_block, lambda at: dict(h=at["h"] ^ 1))
    turn = x ^ h
    low = swap_if(turn & 1 == 1, gradient, y_block)
    high = swap_if(turn & 1 == 1, z_block, zy_block)
    s0, s2 = swap_if(turn >> 1 == 1, low[0], high[0])
    s1, s3 = swap_if(turn >> 1 == 1, low[1], high[1])
    stationary = [s0, s1, s2, s3]

    def product(rows, cols):
        return lax.dot_general(
            rows, cols, (((1,), (1,)), ((), ())), preferred_element_type=jnp.float32
        )

    sums = [None] * SUPERS
    for steps in ((0, 1), (2,), (3,)):
        parts = [
            jnp.stack([product(rows, passing[step]) for step in steps]) for rows in stationary
        ]
        valid = lambda at, steps=steps: reach(at) >= steps[0]
        total = parts[0]
        for d in (1, 3, 2):
            total = total + permute(parts[d], lambda at, d=d: dict(x=at["x"] ^ d), valid)
        keep = lax.dynamic_slice_in_dim(total, yl * half, half, 1)
        give = lax.dynamic_slice_in_dim(total, (1 - yl) * half, half, 1)
        done = keep + permute(give, lambda at: dict(yl=at["yl"] ^ 1), valid)
        for k, step in enumerate(steps):
            sums[step] = done[k]

    every = jnp.stack(sums)
    own = lax.dynamic_slice_in_dim(every, c * quarter, quarter, 1)
    other = permute(
        lax.dynamic_slice_in_dim(every, (1 - c) * quarter, quarter, 1),
        lambda at: dict(c=at["c"] ^ 1),
    )
    first = c == 0
    offsets = [
        own[0] + other[0],
        jnp.where(first, other[1] + own[3], own[1] + other[3]),
        own[2] + other[2],
        jnp.where(first, own[1] + other[3], other[1] + own[3]),
    ]

    across = [None]
    for step in range(1, SUPERS):
        across.append(
            permute(
                sums[step],
                lambda at, step=step: dict(
                    g=at["g"] + (-step if at["c"] == 0 else step), h=at["x"], x=at["h"]
                ),
                lambda at, step=step: reach(at) >= step,
            )
        )
    flipped = jnp.stack(
        [
            jnp.where(first, across[1], across[3]).T,
            across[2].T,
            jnp.where(first, across[3], across[1]).T,
        ]
    )
    pieces = lax.all_to_all(
        flipped.reshape(3, 4, quarter, half),
        "tensor",
        1,
        1,
        axis_index_groups=[[4 * i + k for k in range(4)] for i in range(4)],
        tiled=True,
    ).reshape(3, 2, 2, quarter, half)
    pieces = pieces[:, :, 0] + pieces[:, :, 1]
    for step in range(1, SUPERS):
        offsets[step] = offsets[step] + jnp.concatenate(
            [pieces[step - 1, 0], pieces[step - 1, 1]], axis=1
        )
    around = jnp.concatenate(offsets + offsets[:-1], axis=1)
    gram = lax.dynamic_slice_in_dim(around, (SUPERS - g) % SUPERS * block, SUPERS * block, 1)
    fresh_codes, fresh_scales = refresh(left_codes[0], left_scales[0], gram, hadamard_table(GROUP))
    return fresh_codes[None], fresh_scales[None]


def solution(mesh):
    return jax.shard_map(
        per_device,
        mesh=mesh,
        in_specs=(P("dp", "tensor"), P("dp", "tensor", None), P("dp", "tensor", None)),
        out_specs=(P("dp", "tensor", None), P("dp", "tensor", None)),
        check_vma=False,
    )
```

time: 323 us -> 191 us (0.59); the launches traced: 318 us -> 190 us
  waiting for transfers between devices: 260 us -> 81.3 us
  starting transfers between devices: 22 us -> 83.8 us
  between operations: 14.2 us -> 1.41 us
  matrix products: 7.59 us -> 11 us
    ppermute x4 -> x22, waiting for transfers between devices: 192 us -> 74.8 us  [permute(): return lax.ppermute(array, AXES, pairs)]
    reduce_scatter x1 -> x0, waiting for transfers between devices: 68.4 us -> none  [per_device(): lax.psum_scatter(lax.dot_general(tile_rows, tile_cols, (((1,), (1,)), (()...]
    ppermute x4 -> x22, starting transfers between devices: 21.9 us -> 58 us  [permute(): return lax.ppermute(array, AXES, pairs)]
    all_to_all x0 -> x1, starting transfers between devices: none -> 25.8 us  [per_device(): lax.all_to_all(flipped.reshape(3, 4, quarter, half), 'tensor', 1, 1, axis...]
    all_to_all x0 -> x1, waiting for transfers between devices: none -> 6.55 us  [per_device(): lax.all_to_all(flipped.reshape(3, 4, quarter, half), 'tensor', 1, 1, axis...]
    select_n x3 -> x1, other arithmetic: 6.52 us -> 2.03 us  [swap_if(): return (jnp.where(flag, second, first), jnp.where(flag, first, second))]
    dot_general x3 -> x17, matrix products: 7.59 us -> 11 us  [the longest x16 10.2 us: product(): lax.dot_general(rows, cols, (((1,), (1,)), ((), ())), preferred_element_t...]
  transfers between devices with their start and end apart: 5 -> 23, of which waited for: 4 -> 11; matrix products, arithmetic and copies ran while one was open for 2% -> 9% of each run, Pallas kernels for 0% -> 0%
where the time goes in v1:
time: 191 us; the launch traced here: 190 us
  starting transfers between devices  83.8 us (44%)
  waiting for transfers between devices  81.3 us (43%)
  matrix products  11 us (6%)
  other arithmetic  8.42 us (4%)
  local copies, waits for them, and re-layouts  4.13 us (2%)
    ppermute x22, waiting for transfers between devices, permute(): return lax.ppermute(array, AXES, pairs)  74.8 us
    ppermute x22, starting transfers between devices, permute(): return lax.ppermute(array, AXES, pairs)  58 us
    all_to_all x1, starting transfers between devices, per_device(): lax.all_to_all(flipped.reshape(3, 4, quarter, half), 'tensor', 1, 1, axis...  25.8 us
    dot_general x16, matrix products, product(): lax.dot_general(rows, cols, (((1,), (1,)), ((), ())), preferred_element_t...  10.2 us
    all_to_all x1, waiting for transfers between devices, per_device(): lax.all_to_all(flipped.reshape(3, 4, quarter, half), 'tensor', 1, 1, axis...  6.55 us
  transfers between devices with their start and end apart: 23, of which 11 were waited for; matrix products, arithmetic and copies ran while one was open for 9% of the time, Pallas kernels for 0%

profile of v1, /device:TPU:7, one launch (start us, length us, event | category | flops | bytes accessed | tf_op | source)
XLA Modules:
  0.0 190.1 jit_solution(1060308872337849852)
XLA Ops:
  0.6 3.7 %collective-permute-start = (bf16[256,1792]{1,0:T(8,128)(2,1)}, bf16[256,1792]{1,0:T(8,128)(2,1)}, u32[]{:S(2)}, u32[]{:S(2)}) collective-permute-start(bf16[256,1792]{1,0:T(8,128)(2,1)} %param.3), channel_id=1, source_target_pairs={{0,32},{1,33},{2,34},{3,35},{4,36},{5,37},{6,38},{7,39},{8,40},{9,... | collective-permute-start | bytes 2752520 | tf_op jit(solution)/shard_map/ppermute | solution.py:29
  4.3 4.8 %collective-permute-start.2 = (bf16[256,1792]{1,0:T(8,128)(2,1)}, bf16[256,1792]{1,0:T(8,128)(2,1)}, u32[]{:S(2)}, u32[]{:S(2)}) collective-permute-start(bf16[256,1792]{1,0:T(8,128)(2,1)} %param.3), channel_id=1, source_target_pairs={{0,16},{1,17},{2,18},{3,19},{4,20},{5,21},{6,22},{7,23},{8,24},{9,... | collective-permute-start | bytes 2752520 | tf_op jit(solution)/shard_map/ppermute | solution.py:29
  9.2 1.3 collective-permute-start.3
  10.5 0.9 convert_bitcast_fusion
  11.4 23.0 %collective-permute-done = bf16[256,1792]{1,0:T(8,128)(2,1)} collective-permute-done((bf16[256,1792]{1,0:T(8,128)(2,1)}, bf16[256,1792]{1,0:T(8,128)(2,1)}, u32[]{:S(2)}, u32[]{:S(2)}) %collective-permute-start) | collective-permute-done | bytes 917536 | tf_op jit(solution)/shard_map/ppermute | solution.py:29
  34.4 4.8 %collective-permute-start.1 = (bf16[256,1792]{1,0:T(8,128)(2,1)}, bf16[256,1792]{1,0:T(8,128)(2,1)}, u32[]{:S(2)}, u32[]{:S(2)}) collective-permute-start(bf16[256,1792]{1,0:T(8,128)(2,1)} %collective-permute-done), channel_id=1, source_target_pairs={{0,16},{1,17},{2,18},{3,19},{4,20},{5,21},{6,22},{7,23},{8,24},{9,... | collective-permute-start | bytes 2752520 | tf_op jit(solution)/shard_map/ppermute | solution.py:29
  39.2 0.6 compare_select_fusion.8
  39.9 0.6 copy-done.1
  41.7 0.6 compare_and_fusion.2
  42.9 0.6 broadcast_add_fusion.2
  43.5 0.6 broadcast_add_fusion.4
  44.2 1.3 collective-permute-start.8
  45.5 13.1 %collective-permute-done.1 = bf16[256,1792]{1,0:T(8,128)(2,1)} collective-permute-done((bf16[256,1792]{1,0:T(8,128)(2,1)}, bf16[256,1792]{1,0:T(8,128)(2,1)}, u32[]{:S(2)}, u32[]{:S(2)}) %collective-permute-start.1) | collective-permute-done | bytes 917536 | tf_op jit(solution)/shard_map/ppermute | solution.py:29
  58.6 2.0 %broadcast_select_fusion.7 = (bf16[256,1792]{1,0:T(8,128)(2,1)S(1)}, bf16[256,1792]{1,0:T(8,128)(2,1)S(1)}, bf16[256,1792]{1,0:T(8,128)(2,1)S(1)}, bf16[256,1792]{1,0:T(8,128)(2,1)S(1)}) fusion(pred[]{:T(512)S(6)} %eq.29, bf16[256,1792]{1,0:T(8,128)(2,1)} %collective-permute-done.1, bf16[256,1792]{1,0:T(8,128)(2,1)} %collective-permute-done, pred[]{:T(512)S(6)} %eq.30, ...), kind=kLoop, calls=%fused_computation.31 | loop fusion | flops 3670016 | bytes 7340034 | tf_op jit(solution)/shard_map/jit(_where)/select_n | solution.py:65
  61.6 2.5 %collective-permute-start.4 = (f32[2,256,256]{2,1,0:T(8,128)S(1)}, f32[2,256,256]{2,1,0:T(8,128)S(1)}, u32[]{:S(2)}, u32[]{:S(2)}) collective-permute-start(f32[2,256,256]{2,1,0:T(8,128)S(1)} %pad_maximum_fusion), channel_id=1, source_target_pairs={{0,4},{1,5},{2,6},{3,7},{4,0},{5,1},{6,2},{7,3},{8,12},{9,13},{10,... | collective-permute-start | bytes 1572872 | tf_op jit(solution)/shard_map/ppermute | solution.py:29
  65.0 2.8 %collective-permute-start.5 = (f32[2,256,256]{2,1,0:T(8,128)S(1)}, f32[2,256,256]{2,1,0:T(8,128)S(1)}, u32[]{:S(2)}, u32[]{:S(2)}) collective-permute-start(f32[2,256,256]{2,1,0:T(8,128)S(1)} %pad_maximum_fusion.1), channel_id=1, source_target_pairs={{0,12},{1,13},{2,14},{3,15},{4,8},{5,9},{6,10},{7,11},{8,4},{9,5},... | collective-permute-start | bytes 1572872 | tf_op jit(solution)/shard_map/ppermute | solution.py:29
  68.2 1.5 collective-permute-done.8
  70.1 2.2 %collective-permute-start.10 = (f32[1,256,256]{2,1,0:T(8,128)S(1)}, f32[1,256,256]{2,1,0:T(8,128)S(1)}, u32[]{:S(2)}, u32[]{:S(2)}) collective-permute-start(f32[1,256,256]{2,1,0:T(8,128)S(1)} %convolution_bitcast_fusion.5), channel_id=1, source_target_pairs={{1,13},{3,15},{5,9},{7,11},{9,5},{11,7},{13,1},{15,3},{17,29},{19,... | collective-permute-start | bytes 786440 | tf_op jit(solution)/shard_map/ppermute | solution.py:29
  72.8 3.9 %collective-permute-start.11 = (f32[1,256,256]{2,1,0:T(8,128)S(1)}, f32[1,256,256]{2,1,0:T(8,128)S(1)}, u32[]{:S(2)}, u32[]{:S(2)}) collective-permute-start(f32[1,256,256]{2,1,0:T(8,128)S(1)} %convolution_bitcast_fusion.4), channel_id=1, source_target_pairs={{1,9},{3,11},{5,13},{7,15},{9,1},{11,3},{13,5},{15,7},{17,25},{19,... | collective-permute-start | bytes 786440 | tf_op jit(solution)/shard_map/ppermute | solution.py:29
  77.2 2.8 %collective-permute-start.9 = (f32[1,256,256]{2,1,0:T(8,128)S(1)}, f32[1,256,256]{2,1,0:T(8,128)S(1)}, u32[]{:S(2)}, u32[]{:S(2)}) collective-permute-start(f32[1,256,256]{2,1,0:T(8,128)S(1)} %convolution_bitcast_fusion.6), channel_id=1, source_target_pairs={{1,5},{3,7},{5,1},{7,3},{9,13},{11,15},{13,9},{15,11},{17,21},{19,... | collective-permute-start | bytes 786440 | tf_op jit(solution)/shard_map/ppermute | solution.py:29
  81.0 12.1 %collective-permute-done.10 = f32[1,256,256]{2,1,0:T(8,128)S(1)} collective-permute-done((f32[1,256,256]{2,1,0:T(8,128)S(1)}, f32[1,256,256]{2,1,0:T(8,128)S(1)}, u32[]{:S(2)}, u32[]{:S(2)}) %collective-permute-start.10) | collective-permute-done | bytes 262176 | tf_op jit(solution)/shard_map/ppermute | solution.py:29
  93.0 2.2 %collective-permute-start.6 = (f32[2,256,256]{2,1,0:T(8,128)S(1)}, f32[2,256,256]{2,1,0:T(8,128)S(1)}, u32[]{:S(2)}, u32[]{:S(2)}) collective-permute-start(f32[2,256,256]{2,1,0:T(8,128)S(1)} %pad_maximum_fusion.2), channel_id=1, source_target_pairs={{0,8},{1,9},{2,10},{3,11},{4,12},{5,13},{6,14},{7,15},{8,0},{9,1},... | collective-permute-start | bytes 1572872 | tf_op jit(solution)/shard_map/ppermute | solution.py:29
  95.2 1.3 collective-permute-start.13
  97.0 3.2 %collective-permute-start.12 = (f32[1,128,256]{2,1,0:T(8,128)S(1)}, f32[1,128,256]{2,1,0:T(8,128)S(1)}, u32[]{:S(2)}, u32[]{:S(2)}) collective-permute-start(f32[1,128,256]{2,1,0:T(8,128)S(1)} %constant_dynamic-slice_fusion.2), channel_id=1, source_target_pairs={{1,3},{3,1},{5,7},{7,5},{9,11},{11,9},{13,15},{15,13},{17,19},{19,... | collective-permute-start | bytes 393224 | tf_op jit(solution)/shard_map/ppermute | solution.py:29
  100.6 2.2 %collective-permute-done.12 = f32[1,128,256]{2,1,0:T(8,128)S(1)} collective-permute-done((f32[1,128,256]{2,1,0:T(8,128)S(1)}, f32[1,128,256]{2,1,0:T(8,128)S(1)}, u32[]{:S(2)}, u32[]{:S(2)}) %collective-permute-start.12) | collective-permute-done | bytes 131104 | tf_op jit(solution)/shard_map/ppermute | solution.py:29
  102.8 1.3 collective-permute-start.21
  104.6 3.2 %collective-permute-start.7 = (f32[2,128,256]{2,1,0:T(8,128)S(1)}, f32[2,128,256]{2,1,0:T(8,128)S(1)}, u32[]{:S(2)}, u32[]{:S(2)}) collective-permute-start(f32[2,128,256]{2,1,0:T(8,128)S(1)} %constant_dynamic-slice_fusion.3), channel_id=1, source_target_pairs={{0,2},{1,3},{2,0},{3,1},{4,6},{5,7},{6,4},{7,5},{8,10},{9,11},{10,... | collective-permute-start | bytes 786440 | tf_op jit(solution)/shard_map/ppermute | solution.py:29
  107.8 15.4 %collective-permute-done.13 = bf16[256,1792]{1,0:T(8,128)(2,1)S(1)} collective-permute-done((bf16[256,1792]{1,0:T(8,128)(2,1)S(1)}, bf16[256,1792]{1,0:T(8,128)(2,1)S(1)}, u32[]{:S(2)}, u32[]{:S(2)}) %collective-permute-start.13) | collective-permute-done | bytes 917536 | tf_op jit(solution)/shard_map/ppermute | solution.py:29
  123.2 1.1 convolution_bitcast_fusion.2
  124.3 2.8 %collective-permute-start.14 = (f32[1,256,256]{2,1,0:T(8,128)}, f32[1,256,256]{2,1,0:T(8,128)}, u32[]{:S(2)}, u32[]{:S(2)}) collective-permute-start(f32[1,256,256]{2,1,0:T(8,128)} %convolution_bitcast_fusion.2), channel_id=1, source_target_pairs={{1,5},{3,7},{5,1},{7,3},{9,13},{11,15},{13,9},{15,11},{17,21},{19,... | collective-permute-start | bytes 786440 | tf_op jit(solution)/shard_map/ppermute | solution.py:29
  127.1 1.2 convolution_bitcast_fusion.1
  128.2 4.1 %collective-permute-start.15 = (f32[1,256,256]{2,1,0:T(8,128)}, f32[1,256,256]{2,1,0:T(8,128)}, u32[]{:S(2)}, u32[]{:S(2)}) collective-permute-start(f32[1,256,256]{2,1,0:T(8,128)} %convolution_bitcast_fusion.1), channel_id=1, source_target_pairs={{1,13},{3,15},{5,9},{7,11},{9,5},{11,7},{13,1},{15,3},{17,29},{19,... | collective-permute-start | bytes 786440 | tf_op jit(solution)/shard_map/ppermute | solution.py:29
  132.4 1.1 convolution_bitcast_fusion
  133.5 2.0 %collective-permute-start.16 = (f32[1,256,256]{2,1,0:T(8,128)}, f32[1,256,256]{2,1,0:T(8,128)}, u32[]{:S(2)}, u32[]{:S(2)}) collective-permute-start(f32[1,256,256]{2,1,0:T(8,128)} %convolution_bitcast_fusion), channel_id=1, source_target_pairs={{1,9},{3,11},{5,13},{7,15},{9,1},{11,3},{13,5},{15,7},{17,25},{19,... | collective-permute-start | bytes 786440 | tf_op jit(solution)/shard_map/ppermute | solution.py:29
  135.6 0.6 broadcast_add_fusion.6
  136.9 5.6 %collective-permute-done.16 = f32[1,256,256]{2,1,0:T(8,128)} collective-permute-done((f32[1,256,256]{2,1,0:T(8,128)}, f32[1,256,256]{2,1,0:T(8,128)}, u32[]{:S(2)}, u32[]{:S(2)}) %collective-permute-start.16) | collective-permute-done | bytes 262176 | tf_op jit(solution)/shard_map/ppermute | solution.py:29
  142.4 1.5 fusion.6
  144.0 3.2 %collective-permute-start.17 = (f32[1,128,256]{2,1,0:T(8,128)S(1)}, f32[1,128,256]{2,1,0:T(8,128)S(1)}, u32[]{:S(2)}, u32[]{:S(2)}) collective-permute-start(f32[1,128,256]{2,1,0:T(8,128)S(1)} %constant_dynamic-slice_fusion.1), channel_id=1, source_target_pairs={{1,3},{3,1},{5,7},{7,5},{9,11},{11,9},{13,15},{15,13},{17,19},{19,... | collective-permute-start | bytes 393224 | tf_op jit(solution)/shard_map/ppermute | solution.py:29
  147.3 1.3 collective-permute-start.19
  148.6 1.1 collective-permute-done.17
  149.8 1.3 collective-permute-start.20
  151.1 1.9 %collective-permute-start.18 = (f32[4,64,256]{2,1,0:T(8,128)S(1)}, f32[4,64,256]{2,1,0:T(8,128)S(1)}, u32[]{:S(2)}, u32[]{:S(2)}) collective-permute-start(f32[4,64,256]{2,1,0:T(8,128)S(1)} %constant_dynamic-slice_fusion), channel_id=1, source_target_pairs={{0,1},{1,0},{2,3},{3,2},{4,5},{5,4},{6,7},{7,6},{8,9},{9,8},{10,11... | collective-permute-start | bytes 786440 | tf_op jit(solution)/shard_map/ppermute | solution.py:29
  153.3 0.8 copy.18
  154.1 25.8 %all-to-all-start = ((f32[3,4,64,128]{3,2,0,1:T(8,128)}), f32[3,4,64,128]{3,2,0,1:T(8,128)S(1)}, u32[]{:S(2)}, u32[]{:S(2)}) async-start(f32[3,4,64,128]{3,2,0,1:T(8,128)} %copy.18), calls=%async_computation | async-start | bytes 786432 | tf_op jit(solution)/shard_map/all_to_all | solution.py:147
  180.0 6.6 %all-to-all-done = f32[3,4,64,128]{3,2,0,1:T(8,128)S(1)} async-done(((f32[3,4,64,128]{3,2,0,1:T(8,128)}), f32[3,4,64,128]{3,2,0,1:T(8,128)S(1)}, u32[]{:S(2)}, u32[]{:S(2)}) %all-to-all-start) | async-done | bytes 393248 | tf_op jit(solution)/shard_map/all_to_all | solution.py:147
  187.7 0.9 abs_reduce_fusion
  188.7 0.7 convert_element_type.27
  189.4 0.7 copy.22
  (102 shorter events, 9.8 us)
Async XLA Ops:
  0.6 58.0 %copy-start = (bf16[256,1792]{1,0:T(8,128)(2,1)S(1)}, bf16[256,1792]{1,0:T(8,128)(2,1)}, u32[]{:S(2)}) copy-start(bf16[256,1792]{1,0:T(8,128)(2,1)} %param.3) | copy-start | bytes 2752516
  0.6 33.8 %collective-permute-start = (bf16[256,1792]{1,0:T(8,128)(2,1)}, bf16[256,1792]{1,0:T(8,128)(2,1)}, u32[]{:S(2)}, u32[]{:S(2)}) collective-permute-start(bf16[256,1792]{1,0:T(8,128)(2,1)} %param.3), channel_id=1, source_target_pairs={{0,32},{1,33},{2,34},{3,35},{4,36},{5,37},{6,38},{7,39},{8,40},{9,... | collective-permute-start | bytes 2752520 | tf_op jit(solution)/shard_map/ppermute | solution.py:29
  4.3 41.2 %collective-permute-start.2 = (bf16[256,1792]{1,0:T(8,128)(2,1)}, bf16[256,1792]{1,0:T(8,128)(2,1)}, u32[]{:S(2)}, u32[]{:S(2)}) collective-permute-start(bf16[256,1792]{1,0:T(8,128)(2,1)} %param.3), channel_id=1, source_target_pairs={{0,16},{1,17},{2,18},{3,19},{4,20},{5,21},{6,22},{7,23},{8,24},{9,... | collective-permute-start | bytes 2752520 | tf_op jit(solution)/shard_map/ppermute | solution.py:29
  9.2 35.0 %collective-permute-start.3 = (bf16[256,1792]{1,0:T(8,128)(2,1)}, bf16[256,1792]{1,0:T(8,128)(2,1)S(1)}, u32[]{:S(2)}, u32[]{:S(2)}) collective-permute-start(bf16[256,1792]{1,0:T(8,128)(2,1)} %param.3), channel_id=1, source_target_pairs={{0,64},{2,66},{4,68},{6,70},{8,72},{10,74},{12,76},{14,78},{16,80}... | collective-permute-start | bytes 2752520 | tf_op jit(solution)/shard_map/ppermute | solution.py:29
  34.4 24.2 %collective-permute-start.1 = (bf16[256,1792]{1,0:T(8,128)(2,1)}, bf16[256,1792]{1,0:T(8,128)(2,1)}, u32[]{:S(2)}, u32[]{:S(2)}) collective-permute-start(bf16[256,1792]{1,0:T(8,128)(2,1)} %collective-permute-done), channel_id=1, source_target_pairs={{0,16},{1,17},{2,18},{3,19},{4,20},{5,21},{6,22},{7,23},{8,24},{9,... | collective-permute-start | bytes 2752520 | tf_op jit(solution)/shard_map/ppermute | solution.py:29
  39.8 0.7 copy-start.1
  44.2 25.5 %collective-permute-start.8 = (bf16[256,1792]{1,0:T(8,128)(2,1)S(1)}, bf16[256,1792]{1,0:T(8,128)(2,1)S(1)}, u32[]{:S(2)}, u32[]{:S(2)}) collective-permute-start(bf16[256,1792]{1,0:T(8,128)(2,1)S(1)} %collective-permute-done.3), channel_id=1, source_target_pairs={{64,128},{65,1},{66,130},{67,3},{68,132},{69,5},{70,134},{71,7},{7... | collective-permute-start | bytes 2752520 | tf_op jit(solution)/shard_map/ppermute | solution.py:29
  61.6 42.6 %collective-permute-start.4 = (f32[2,256,256]{2,1,0:T(8,128)S(1)}, f32[2,256,256]{2,1,0:T(8,128)S(1)}, u32[]{:S(2)}, u32[]{:S(2)}) collective-permute-start(f32[2,256,256]{2,1,0:T(8,128)S(1)} %pad_maximum_fusion), channel_id=1, source_target_pairs={{0,4},{1,5},{2,6},{3,7},{4,0},{5,1},{6,2},{7,3},{8,12},{9,13},{10,... | collective-permute-start | bytes 1572872 | tf_op jit(solution)/shard_map/ppermute | solution.py:29
  65.0 39.2 %collective-permute-start.5 = (f32[2,256,256]{2,1,0:T(8,128)S(1)}, f32[2,256,256]{2,1,0:T(8,128)S(1)}, u32[]{:S(2)}, u32[]{:S(2)}) collective-permute-start(f32[2,256,256]{2,1,0:T(8,128)S(1)} %pad_maximum_fusion.1), channel_id=1, source_target_pairs={{0,12},{1,13},{2,14},{3,15},{4,8},{5,9},{6,10},{7,11},{8,4},{9,5},... | collective-permute-start | bytes 1572872 | tf_op jit(solution)/shard_map/ppermute | solution.py:29
  70.1 22.9 %collective-permute-start.10 = (f32[1,256,256]{2,1,0:T(8,128)S(1)}, f32[1,256,256]{2,1,0:T(8,128)S(1)}, u32[]{:S(2)}, u32[]{:S(2)}) collective-permute-start(f32[1,256,256]{2,1,0:T(8,128)S(1)} %convolution_bitcast_fusion.5), channel_id=1, source_target_pairs={{1,13},{3,15},{5,9},{7,11},{9,5},{11,7},{13,1},{15,3},{17,29},{19,... | collective-permute-start | bytes 786440 | tf_op jit(solution)/shard_map/ppermute | solution.py:29
  72.8 22.4 %collective-permute-start.11 = (f32[1,256,256]{2,1,0:T(8,128)S(1)}, f32[1,256,256]{2,1,0:T(8,128)S(1)}, u32[]{:S(2)}, u32[]{:S(2)}) collective-permute-start(f32[1,256,256]{2,1,0:T(8,128)S(1)} %convolution_bitcast_fusion.4), channel_id=1, source_target_pairs={{1,9},{3,11},{5,13},{7,15},{9,1},{11,3},{13,5},{15,7},{17,25},{19,... | collective-permute-start | bytes 786440 | tf_op jit(solution)/shard_map/ppermute | solution.py:29
  77.2 19.3 %collective-permute-start.9 = (f32[1,256,256]{2,1,0:T(8,128)S(1)}, f32[1,256,256]{2,1,0:T(8,128)S(1)}, u32[]{:S(2)}, u32[]{:S(2)}) collective-permute-start(f32[1,256,256]{2,1,0:T(8,128)S(1)} %convolution_bitcast_fusion.6), channel_id=1, source_target_pairs={{1,5},{3,7},{5,1},{7,3},{9,13},{11,15},{13,9},{15,11},{17,21},{19,... | collective-permute-start | bytes 786440 | tf_op jit(solution)/shard_map/ppermute | solution.py:29
  93.0 11.4 %collective-permute-start.6 = (f32[2,256,256]{2,1,0:T(8,128)S(1)}, f32[2,256,256]{2,1,0:T(8,128)S(1)}, u32[]{:S(2)}, u32[]{:S(2)}) collective-permute-start(f32[2,256,256]{2,1,0:T(8,128)S(1)} %pad_maximum_fusion.2), channel_id=1, source_target_pairs={{0,8},{1,9},{2,10},{3,11},{4,12},{5,13},{6,14},{7,15},{8,0},{9,1},... | collective-permute-start | bytes 1572872 | tf_op jit(solution)/shard_map/ppermute | solution.py:29
  95.2 28.0 %collective-permute-start.13 = (bf16[256,1792]{1,0:T(8,128)(2,1)S(1)}, bf16[256,1792]{1,0:T(8,128)(2,1)S(1)}, u32[]{:S(2)}, u32[]{:S(2)}) collective-permute-start(bf16[256,1792]{1,0:T(8,128)(2,1)S(1)} %collective-permute-done.8), channel_id=1, source_target_pairs={{65,1},{67,3},{69,5},{71,7},{73,9},{75,11},{77,13},{79,15},{81,17}... | collective-permute-start | bytes 2752520 | tf_op jit(solution)/shard_map/ppermute | solution.py:29
  97.0 5.8 %collective-permute-start.12 = (f32[1,128,256]{2,1,0:T(8,128)S(1)}, f32[1,128,256]{2,1,0:T(8,128)S(1)}, u32[]{:S(2)}, u32[]{:S(2)}) collective-permute-start(f32[1,128,256]{2,1,0:T(8,128)S(1)} %constant_dynamic-slice_fusion.2), channel_id=1, source_target_pairs={{1,3},{3,1},{5,7},{7,5},{9,11},{11,9},{13,15},{15,13},{17,19},{19,... | collective-permute-start | bytes 393224 | tf_op jit(solution)/shard_map/ppermute | solution.py:29
  102.8 33.3 %collective-permute-start.21 = (f32[128,256]{1,0:T(8,128)S(1)}, f32[128,256]{1,0:T(8,128)S(1)}, u32[]{:S(2)}, u32[]{:S(2)}) collective-permute-start(f32[128,256]{1,0:T(8,128)S(1)} %bitcast.143), channel_id=1, source_target_pairs={{1,129},{3,131},{5,145},{7,147},{9,161},{11,163},{13,177},{15,179}... | collective-permute-start | bytes 393224 | tf_op jit(solution)/shard_map/ppermute | solution.py:29
  104.6 31.7 %collective-permute-start.7 = (f32[2,128,256]{2,1,0:T(8,128)S(1)}, f32[2,128,256]{2,1,0:T(8,128)S(1)}, u32[]{:S(2)}, u32[]{:S(2)}) collective-permute-start(f32[2,128,256]{2,1,0:T(8,128)S(1)} %constant_dynamic-slice_fusion.3), channel_id=1, source_target_pairs={{0,2},{1,3},{2,0},{3,1},{4,6},{5,7},{6,4},{7,5},{8,10},{9,11},{10,... | collective-permute-start | bytes 786440 | tf_op jit(solution)/shard_map/ppermute | solution.py:29
  124.3 12.0 %collective-permute-start.14 = (f32[1,256,256]{2,1,0:T(8,128)}, f32[1,256,256]{2,1,0:T(8,128)}, u32[]{:S(2)}, u32[]{:S(2)}) collective-permute-start(f32[1,256,256]{2,1,0:T(8,128)} %convolution_bitcast_fusion.2), channel_id=1, source_target_pairs={{1,5},{3,7},{5,1},{7,3},{9,13},{11,15},{13,9},{15,11},{17,21},{19,... | collective-permute-start | bytes 786440 | tf_op jit(solution)/shard_map/ppermute | solution.py:29
  128.2 8.6 %collective-permute-start.15 = (f32[1,256,256]{2,1,0:T(8,128)}, f32[1,256,256]{2,1,0:T(8,128)}, u32[]{:S(2)}, u32[]{:S(2)}) collective-permute-start(f32[1,256,256]{2,1,0:T(8,128)} %convolution_bitcast_fusion.1), channel_id=1, source_target_pairs={{1,13},{3,15},{5,9},{7,11},{9,5},{11,7},{13,1},{15,3},{17,29},{19,... | collective-permute-start | bytes 786440 | tf_op jit(solution)/shard_map/ppermute | solution.py:29
  133.5 8.9 %collective-permute-start.16 = (f32[1,256,256]{2,1,0:T(8,128)}, f32[1,256,256]{2,1,0:T(8,128)}, u32[]{:S(2)}, u32[]{:S(2)}) collective-permute-start(f32[1,256,256]{2,1,0:T(8,128)} %convolution_bitcast_fusion), channel_id=1, source_target_pairs={{1,9},{3,11},{5,13},{7,15},{9,1},{11,3},{13,5},{15,7},{17,25},{19,... | collective-permute-start | bytes 786440 | tf_op jit(solution)/shard_map/ppermute | solution.py:29
  144.0 5.7 %collective-permute-start.17 = (f32[1,128,256]{2,1,0:T(8,128)S(1)}, f32[1,128,256]{2,1,0:T(8,128)S(1)}, u32[]{:S(2)}, u32[]{:S(2)}) collective-permute-start(f32[1,128,256]{2,1,0:T(8,128)S(1)} %constant_dynamic-slice_fusion.1), channel_id=1, source_target_pairs={{1,3},{3,1},{5,7},{7,5},{9,11},{11,9},{13,15},{15,13},{17,19},{19,... | collective-permute-start | bytes 393224 | tf_op jit(solution)/shard_map/ppermute | solution.py:29
  147.3 5.8 %collective-permute-start.19 = (f32[128,256]{1,0:T(8,128)S(1)}, f32[128,256]{1,0:T(8,128)S(1)}, u32[]{:S(2)}, u32[]{:S(2)}) collective-permute-start(f32[128,256]{1,0:T(8,128)S(1)} %slice_bitcast_fusion), channel_id=1, source_target_pairs={{1,65},{3,67},{5,81},{7,83},{9,97},{11,99},{13,113},{15,115},{17,6... | collective-permute-start | bytes 393224 | tf_op jit(solution)/shard_map/ppermute | solution.py:29
  149.8 3.3 %collective-permute-start.20 = (f32[128,256]{1,0:T(8,128)S(1)}, f32[128,256]{1,0:T(8,128)S(1)}, u32[]{:S(2)}, u32[]{:S(2)}) collective-permute-start(f32[128,256]{1,0:T(8,128)S(1)} %bitcast.144), channel_id=1, source_target_pairs={{1,193},{3,195},{5,209},{7,211},{9,225},{11,227},{13,241},{15,243}... | collective-permute-start | bytes 393224 | tf_op jit(solution)/shard_map/ppermute | solution.py:29
  151.1 28.8 %collective-permute-start.18 = (f32[4,64,256]{2,1,0:T(8,128)S(1)}, f32[4,64,256]{2,1,0:T(8,128)S(1)}, u32[]{:S(2)}, u32[]{:S(2)}) collective-permute-start(f32[4,64,256]{2,1,0:T(8,128)S(1)} %constant_dynamic-slice_fusion), channel_id=1, source_target_pairs={{0,1},{1,0},{2,3},{3,2},{4,5},{5,4},{6,7},{7,6},{8,9},{9,8},{10,11... | collective-permute-start | bytes 786440 | tf_op jit(solution)/shard_map/ppermute | solution.py:29
  154.1 32.4 %all-to-all-start = ((f32[3,4,64,128]{3,2,0,1:T(8,128)}), f32[3,4,64,128]{3,2,0,1:T(8,128)S(1)}, u32[]{:S(2)}, u32[]{:S(2)}) async-start(f32[3,4,64,128]{3,2,0,1:T(8,128)} %copy.18), calls=%async_computation | async-start | bytes 786432 | tf_op jit(solution)/shard_map/all_to_all | solution.py:147
  186.8 0.7 copy-start.5
  186.8 0.6 copy-start.6
  186.8 0.7 copy-start.7
  186.8 0.7 copy-start.8
  186.8 0.7 copy-start.9
  186.8 0.7 copy-start.10
  186.8 0.7 copy-start.11
  186.9 0.7 copy-start.12
  186.9 0.7 copy-start.13
  186.9 0.7 copy-start.14
  186.9 0.7 copy-start.15
  186.9 0.7 copy-start.16
  186.9 0.7 copy-start.17
  187.0 0.7 copy-start.2
  187.0 0.7 copy-start.3
  187.0 0.7 copy-start.4

commit v2 on v1

--- a/solution.py
+++ b/solution.py
@@ -97,8 +97,11 @@
             rows, cols, (((1,), (1,)), ((), ())), preferred_element_type=jnp.float32
         )
 
-    sums = [None] * SUPERS
-    for steps in ((0, 1), (2,), (3,)):
+    def half_of(array, flag, size, axis):
+        return lax.dynamic_slice_in_dim(array, flag * size, size, axis)
+
+    own, across = [None] * SUPERS, [None] * SUPERS
+    for steps in ((0, 1), (2, 3)):
         parts = [
             jnp.stack([product(rows, passing[step]) for step in steps]) for rows in stationary
         ]
@@ -106,57 +109,36 @@
         total = parts[0]
         for d in (1, 3, 2):
             total = total + permute(parts[d], lambda at, d=d: dict(x=at["x"] ^ d), valid)
-        keep = lax.dynamic_slice_in_dim(total, yl * half, half, 1)
-        give = lax.dynamic_slice_in_dim(total, (1 - yl) * half, half, 1)
-        done = keep + permute(give, lambda at: dict(yl=at["yl"] ^ 1), valid)
+        far = [k for k, step in enumerate(steps) if step]
+        both = jnp.stack(list(total) + [total[k].T for k in far])
+        done = half_of(both, yl, half, 1) + permute(
+            half_of(both, 1 - yl, half, 1), lambda at: dict(yl=at["yl"] ^ 1), valid
+        )
         for k, step in enumerate(steps):
-            sums[step] = done[k]
-
-    every = jnp.stack(sums)
-    own = lax.dynamic_slice_in_dim(every, c * quarter, quarter, 1)
-    other = permute(
-        lax.dynamic_slice_in_dim(every, (1 - c) * quarter, quarter, 1),
-        lambda at: dict(c=at["c"] ^ 1),
-    )
-    first = c == 0
-    offsets = [
-        own[0] + other[0],
-        jnp.where(first, other[1] + own[3], own[1] + other[3]),
-        own[2] + other[2],
-        jnp.where(first, own[1] + other[3], other[1] + own[3]),
-    ]
-
-    across = [None]
-    for step in range(1, SUPERS):
-        across.append(
-            permute(
-                sums[step],
+            own[step] = done[k]
+        for k, place_no in enumerate(far):
+            step = steps[place_no]
+            across[step] = permute(
+                done[len(steps) + k],
                 lambda at, step=step: dict(
                     g=at["g"] + (-step if at["c"] == 0 else step), h=at["x"], x=at["h"]
                 ),
                 lambda at, step=step: reach(at) >= step,
             )
-        )
-    flipped = jnp.stack(
+
+    first = c == 0
+    strips = jnp.stack(
         [
-            jnp.where(first, across[1], across[3]).T,
-            across[2].T,
-            jnp.where(first, across[3], across[1]).T,
+            own[0],
+            jnp.where(first, own[3] + across[1], own[1] + across[3]),
+            own[2] + across[2],
+            jnp.where(first, own[1] + across[3], own[3] + across[1]),
         ]
     )
-    pieces = lax.all_to_all(
-        flipped.reshape(3, 4, quarter, half),
-        "tensor",
-        1,
-        1,
-        axis_index_groups=[[4 * i + k for k in range(4)] for i in range(4)],
-        tiled=True,
-    ).reshape(3, 2, 2, quarter, half)
-    pieces = pieces[:, :, 0] + pieces[:, :, 1]
-    for step in range(1, SUPERS):
-        offsets[step] = offsets[step] + jnp.concatenate(
-            [pieces[step - 1, 0], pieces[step - 1, 1]], axis=1
-        )
+    offsets = half_of(strips, c, quarter, 1) + permute(
+        half_of(strips, 1 - c, quarter, 1), lambda at: dict(c=at["c"] ^ 1)
+    )
+    offsets = list(offsets)
     around = jnp.concatenate(offsets + offsets[:-1], axis=1)
     gram = lax.dynamic_slice_in_dim(around, (SUPERS - g) % SUPERS * block, SUPERS * block, 1)
     fresh_codes, fresh_scales = refresh(left_codes[0], left_scales[0], gram, hadamard_table(GROUP))

time: 191 us -> 164 us (0.86)
  starting transfers between devices: 83.8 us -> 68.8 us
  waiting for transfers between devices: 81.3 us -> 67.7 us
  other arithmetic: 8.42 us -> 13.7 us
  matrix products: 11 us -> 7.79 us
    all_to_all x1 -> x0, starting transfers between devices: 25.8 us -> none  [per_device(): lax.all_to_all(flipped.reshape(3, 4, quarter, half), 'tensor', 1, 1, axis...]
    ppermute x22 -> x18, starting transfers between devices: 58 us -> 68.8 us  [permute(): return lax.ppermute(array, AXES, pairs)]
    ppermute x22 -> x18, waiting for transfers between devices: 74.8 us -> 67.7 us  [permute(): return lax.ppermute(array, AXES, pairs)]
    all_to_all x1 -> x0, waiting for transfers between devices: 6.55 us -> none  [per_device(): lax.all_to_all(flipped.reshape(3, 4, quarter, half), 'tensor', 1, 1, axis...]
    dot_general x16, matrix products: 10.2 us -> 6.92 us  [product(): lax.dot_general(rows, cols, (((1,), (1,)), ((), ())), preferred_element_t...]
    another operation x3 -> x6, other arithmetic: 0.11 us -> 2.64 us  [per_device(): jnp.stack([product(rows, passing[step]) for step in steps])]
  transfers between devices with their start and end apart: 23 -> 18, of which waited for: 11 -> 9; matrix products, arithmetic and copies ran while one was open for 9% -> 13% of each run, Pallas kernels for 0% -> 0%
where the time goes in v2:
time: 164 us; the launch traced here: 163 us
  starting transfers between devices  68.8 us (42%)
  waiting for transfers between devices  67.7 us (41%)
  other arithmetic  13.7 us (8%)
  matrix products  7.79 us (5%)
  local copies, waits for them, and re-layouts  3.72 us (2%)
    ppermute x18, starting transfers between devices, permute(): return lax.ppermute(array, AXES, pairs)  68.8 us
    ppermute x18, waiting for transfers between devices, permute(): return lax.ppermute(array, AXES, pairs)  67.7 us
    dot_general x16, matrix products, product(): lax.dot_general(rows, cols, (((1,), (1,)), ((), ())), preferred_element_t...  6.92 us
  transfers between devices with their start and end apart: 18, of which 9 were waited for; matrix products, arithmetic and copies ran while one was open for 13% of the time, Pallas kernels for 0%

profile of v2, /device:TPU:7, one launch (start us, length us, event | category | flops | bytes accessed | tf_op | source)
XLA Modules:
  0.0 163.1 jit_solution(1693558960543817119)
XLA Ops:
  0.6 3.5 %collective-permute-start = (bf16[256,1792]{1,0:T(8,128)(2,1)}, bf16[256,1792]{1,0:T(8,128)(2,1)S(1)}, u32[]{:S(2)}, u32[]{:S(2)}) collective-permute-start(bf16[256,1792]{1,0:T(8,128)(2,1)} %param.3), channel_id=1, source_target_pairs={{0,32},{1,33},{2,34},{3,35},{4,36},{5,37},{6,38},{7,39},{8,40},{9,... | collective-permute-start | bytes 2752520 | tf_op jit(solution)/shard_map/ppermute | solution.py:29
  4.2 4.8 %collective-permute-start.2 = (bf16[256,1792]{1,0:T(8,128)(2,1)}, bf16[256,1792]{1,0:T(8,128)(2,1)S(1)}, u32[]{:S(2)}, u32[]{:S(2)}) collective-permute-start(bf16[256,1792]{1,0:T(8,128)(2,1)} %param.3), channel_id=1, source_target_pairs={{0,16},{1,17},{2,18},{3,19},{4,20},{5,21},{6,22},{7,23},{8,24},{9,... | collective-permute-start | bytes 2752520 | tf_op jit(solution)/shard_map/ppermute | solution.py:29
  9.0 1.3 collective-permute-start.3
  10.3 23.9 %collective-permute-done = bf16[256,1792]{1,0:T(8,128)(2,1)S(1)} collective-permute-done((bf16[256,1792]{1,0:T(8,128)(2,1)}, bf16[256,1792]{1,0:T(8,128)(2,1)S(1)}, u32[]{:S(2)}, u32[]{:S(2)}) %collective-permute-start) | collective-permute-done | bytes 917536 | tf_op jit(solution)/shard_map/ppermute | solution.py:29
  34.2 4.8 %collective-permute-start.1 = (bf16[256,1792]{1,0:T(8,128)(2,1)S(1)}, bf16[256,1792]{1,0:T(8,128)(2,1)}, u32[]{:S(2)}, u32[]{:S(2)}) collective-permute-start(bf16[256,1792]{1,0:T(8,128)(2,1)S(1)} %collective-permute-done), channel_id=1, source_target_pairs={{0,16},{1,17},{2,18},{3,19},{4,20},{5,21},{6,22},{7,23},{8,24},{9,... | collective-permute-start | bytes 2752520 | tf_op jit(solution)/shard_map/ppermute | solution.py:29
  39.0 0.5 broadcast_add_fusion.2
  39.6 0.6 compare_select_fusion.4
  40.1 0.5 broadcast_add_fusion.4
  40.7 0.6 compare_select_fusion.8
  41.3 0.6 broadcast_add_fusion.6
  41.8 1.6 convert_bitcast_fusion
  43.5 1.4 collective-permute-start.8
  44.9 0.9 copy-done.2
  45.8 12.4 %collective-permute-done.1 = bf16[256,1792]{1,0:T(8,128)(2,1)} collective-permute-done((bf16[256,1792]{1,0:T(8,128)(2,1)S(1)}, bf16[256,1792]{1,0:T(8,128)(2,1)}, u32[]{:S(2)}, u32[]{:S(2)}) %collective-permute-start.1) | collective-permute-done | bytes 917536 | tf_op jit(solution)/shard_map/ppermute | solution.py:29
  58.2 2.0 %broadcast_select_fusion.7 = (bf16[256,1792]{1,0:T(8,128)(2,1)S(1)}, bf16[256,1792]{1,0:T(8,128)(2,1)S(1)}, bf16[256,1792]{1,0:T(8,128)(2,1)S(1)}, bf16[256,1792]{1,0:T(8,128)(2,1)S(1)}) fusion(pred[]{:T(512)S(6)} %eq.29, bf16[256,1792]{1,0:T(8,128)(2,1)} %collective-permute-done.1, bf16[256,1792]{1,0:T(8,128)(2,1)S(1)} %collective-permute-done, ...), kind=kLoop, calls=%fused_computation.28 | loop fusion | flops 3670016 | bytes 7340034 | tf_op jit(solution)/shard_map/jit(_where)/select_n | solution.py:65
  60.2 0.4 convolution_bitcast_fusion.9
  61.1 3.0 %collective-permute-start.6 = (f32[2,256,256]{2,1,0:T(8,128)S(1)}, f32[2,256,256]{2,1,0:T(8,128)S(1)}, u32[]{:S(2)}, u32[]{:S(2)}) collective-permute-start(f32[2,256,256]{2,1,0:T(8,128)S(1)} %pad_maximum_fusion.3), channel_id=1, source_target_pairs={{0,8},{1,9},{2,10},{3,11},{4,12},{5,13},{6,14},{7,15},{8,0},{9,1},... | collective-permute-start | bytes 1572872 | tf_op jit(solution)/shard_map/ppermute | solution.py:29
  65.1 3.7 %collective-permute-start.5 = (f32[2,256,256]{2,1,0:T(8,128)S(1)}, f32[2,256,256]{2,1,0:T(8,128)S(1)}, u32[]{:S(2)}, u32[]{:S(2)}) collective-permute-start(f32[2,256,256]{2,1,0:T(8,128)S(1)} %pad_maximum_fusion.2), channel_id=1, source_target_pairs={{0,12},{1,13},{2,14},{3,15},{4,8},{5,9},{6,10},{7,11},{8,4},{9,5},... | collective-permute-start | bytes 1572872 | tf_op jit(solution)/shard_map/ppermute | solution.py:29
  69.8 1.9 %collective-permute-start.4 = (f32[2,256,256]{2,1,0:T(8,128)S(1)}, f32[2,256,256]{2,1,0:T(8,128)S(1)}, u32[]{:S(2)}, u32[]{:S(2)}) collective-permute-start(f32[2,256,256]{2,1,0:T(8,128)S(1)} %pad_maximum_fusion.1), channel_id=1, source_target_pairs={{0,4},{1,5},{2,6},{3,7},{4,0},{5,1},{6,2},{7,3},{8,12},{9,13},{10,... | collective-permute-start | bytes 1572872 | tf_op jit(solution)/shard_map/ppermute | solution.py:29
  72.1 1.3 collective-permute-start.9
  75.7 21.4 %collective-permute-done.9 = bf16[256,1792]{1,0:T(8,128)(2,1)S(1)} collective-permute-done((bf16[256,1792]{1,0:T(8,128)(2,1)S(1)}, bf16[256,1792]{1,0:T(8,128)(2,1)S(1)}, u32[]{:S(2)}, u32[]{:S(2)}) %collective-permute-start.9) | collective-permute-done | bytes 917536 | tf_op jit(solution)/shard_map/ppermute | solution.py:29
  97.0 0.4 convolution_bitcast_fusion
  97.5 0.8 pad_maximum_fusion.6
  98.3 3.9 %collective-permute-start.12 = (f32[2,256,256]{1,2,0:T(8,128)}, f32[2,256,256]{1,2,0:T(8,128)}, u32[]{:S(2)}, u32[]{:S(2)}) collective-permute-start(f32[2,256,256]{1,2,0:T(8,128)} %pad_maximum_fusion.6), channel_id=1, source_target_pairs={{1,9},{3,11},{5,13},{7,15},{9,1},{11,3},{13,5},{15,7},{17,25},{19,... | collective-permute-start | bytes 1572872 | tf_op jit(solution)/shard_map/ppermute | solution.py:29
  102.7 0.8 pad_maximum_fusion.5
  103.5 3.7 %collective-permute-start.11 = (f32[2,256,256]{1,2,0:T(8,128)}, f32[2,256,256]{1,2,0:T(8,128)}, u32[]{:S(2)}, u32[]{:S(2)}) collective-permute-start(f32[2,256,256]{1,2,0:T(8,128)} %pad_maximum_fusion.5), channel_id=1, source_target_pairs={{1,13},{3,15},{5,9},{7,11},{9,5},{11,7},{13,1},{15,3},{17,29},{19,... | collective-permute-start | bytes 1572872 | tf_op jit(solution)/shard_map/ppermute | solution.py:29
  107.7 0.8 pad_maximum_fusion.4
  108.5 1.9 %collective-permute-start.10 = (f32[2,256,256]{1,2,0:T(8,128)}, f32[2,256,256]{1,2,0:T(8,128)}, u32[]{:S(2)}, u32[]{:S(2)}) collective-permute-start(f32[2,256,256]{1,2,0:T(8,128)} %pad_maximum_fusion.4), channel_id=1, source_target_pairs={{1,5},{3,7},{5,1},{7,3},{9,13},{11,15},{13,9},{15,11},{17,21},{19,... | collective-permute-start | bytes 1572872 | tf_op jit(solution)/shard_map/ppermute | solution.py:29
  110.8 0.8 fusion.5
  111.6 3.2 %collective-permute-start.7 = (f32[3,128,256]{2,1,0:T(8,128)}, f32[3,128,256]{2,1,0:T(8,128)}, u32[]{:S(2)}, u32[]{:S(2)}) collective-permute-start(f32[3,128,256]{2,1,0:T(8,128)} %fusion.5), channel_id=1, source_target_pairs={{0,2},{1,3},{2,0},{3,1},{4,6},{5,7},{6,4},{7,5},{8,10},{9,11},{10,... | collective-permute-start | bytes 1179656 | tf_op jit(solution)/shard_map/ppermute | solution.py:29
  115.2 0.4 collective-permute-done.11
  115.7 3.1 %collective-permute-done.10 = f32[2,256,256]{1,2,0:T(8,128)} collective-permute-done((f32[2,256,256]{1,2,0:T(8,128)}, f32[2,256,256]{1,2,0:T(8,128)}, u32[]{:S(2)}, u32[]{:S(2)}) %collective-permute-start.10) | collective-permute-done | bytes 524320 | tf_op jit(solution)/shard_map/ppermute | solution.py:29
  118.8 1.5 fusion.4
  120.7 3.2 %collective-permute-start.13 = (f32[4,128,256]{2,1,0:T(8,128)S(1)}, f32[4,128,256]{2,1,0:T(8,128)S(1)}, u32[]{:S(2)}, u32[]{:S(2)}) collective-permute-start(f32[4,128,256]{2,1,0:T(8,128)S(1)} %constant_dynamic-slice_fusion.1), channel_id=1, source_target_pairs={{1,3},{3,1},{5,7},{7,5},{9,11},{11,9},{13,15},{15,13},{17,19},{19,... | collective-permute-start | bytes 1572872 | tf_op jit(solution)/shard_map/ppermute | solution.py:29
  123.9 0.6 compare_and_fusion
  124.5 1.0 fusion.7
  125.5 1.3 collective-permute-start.14
  126.8 3.7 %collective-permute-done.13 = f32[4,128,256]{2,1,0:T(8,128)S(1)} collective-permute-done((f32[4,128,256]{2,1,0:T(8,128)S(1)}, f32[4,128,256]{2,1,0:T(8,128)S(1)}, u32[]{:S(2)}, u32[]{:S(2)}) %collective-permute-start.13) | collective-permute-done | bytes 524320 | tf_op jit(solution)/shard_map/ppermute | solution.py:29
  130.7 1.3 collective-permute-start.15
  132.0 1.3 collective-permute-start.16
  133.3 0.6 collective-permute-done.15
  133.9 1.4 collective-permute-done.16
  135.4 23.1 %collective-permute-start.17 = (f32[4,64,256]{2,1,0:T(8,128)S(1)}, f32[4,64,256]{2,1,0:T(8,128)S(1)}, u32[]{:S(2)}, u32[]{:S(2)}) collective-permute-start(f32[4,64,256]{2,1,0:T(8,128)S(1)} %constant_dynamic-slice_fusion), channel_id=1, source_target_pairs={{0,1},{1,0},{2,3},{3,2},{4,5},{5,4},{6,7},{7,6},{8,9},{9,8},{10,11... | collective-permute-start | bytes 786440 | tf_op jit(solution)/shard_map/ppermute | solution.py:29
  158.8 0.8 collective-permute-done.17
  160.0 0.4 copy-done.7
  160.7 0.9 abs_reduce_fusion
  161.7 0.7 convert_element_type.27
  162.4 0.7 copy.28
  (89 shorter events, 7.9 us)
Async XLA Ops:
  0.6 33.5 %collective-permute-start = (bf16[256,1792]{1,0:T(8,128)(2,1)}, bf16[256,1792]{1,0:T(8,128)(2,1)S(1)}, u32[]{:S(2)}, u32[]{:S(2)}) collective-permute-start(bf16[256,1792]{1,0:T(8,128)(2,1)} %param.3), channel_id=1, source_target_pairs={{0,32},{1,33},{2,34},{3,35},{4,36},{5,37},{6,38},{7,39},{8,40},{9,... | collective-permute-start | bytes 2752520 | tf_op jit(solution)/shard_map/ppermute | solution.py:29
  4.2 40.7 %collective-permute-start.2 = (bf16[256,1792]{1,0:T(8,128)(2,1)}, bf16[256,1792]{1,0:T(8,128)(2,1)S(1)}, u32[]{:S(2)}, u32[]{:S(2)}) collective-permute-start(bf16[256,1792]{1,0:T(8,128)(2,1)} %param.3), channel_id=1, source_target_pairs={{0,16},{1,17},{2,18},{3,19},{4,20},{5,21},{6,22},{7,23},{8,24},{9,... | collective-permute-start | bytes 2752520 | tf_op jit(solution)/shard_map/ppermute | solution.py:29
  9.0 34.4 %collective-permute-start.3 = (bf16[256,1792]{1,0:T(8,128)(2,1)}, bf16[256,1792]{1,0:T(8,128)(2,1)S(1)}, u32[]{:S(2)}, u32[]{:S(2)}) collective-permute-start(bf16[256,1792]{1,0:T(8,128)(2,1)} %param.3), channel_id=1, source_target_pairs={{0,64},{2,66},{4,68},{6,70},{8,72},{10,74},{12,76},{14,78},{16,80}... | collective-permute-start | bytes 2752520 | tf_op jit(solution)/shard_map/ppermute | solution.py:29
  34.2 24.0 %collective-permute-start.1 = (bf16[256,1792]{1,0:T(8,128)(2,1)S(1)}, bf16[256,1792]{1,0:T(8,128)(2,1)}, u32[]{:S(2)}, u32[]{:S(2)}) collective-permute-start(bf16[256,1792]{1,0:T(8,128)(2,1)S(1)} %collective-permute-done), channel_id=1, source_target_pairs={{0,16},{1,17},{2,18},{3,19},{4,20},{5,21},{6,22},{7,23},{8,24},{9,... | collective-permute-start | bytes 2752520 | tf_op jit(solution)/shard_map/ppermute | solution.py:29
  43.5 16.8 %copy-start = (bf16[256,1792]{1,0:T(8,128)(2,1)S(1)}, bf16[256,1792]{1,0:T(8,128)(2,1)}, u32[]{:S(2)}) copy-start(bf16[256,1792]{1,0:T(8,128)(2,1)} %param.3) | copy-start | bytes 2752516
  43.5 28.7 %collective-permute-start.8 = (bf16[256,1792]{1,0:T(8,128)(2,1)S(1)}, bf16[256,1792]{1,0:T(8,128)(2,1)S(1)}, u32[]{:S(2)}, u32[]{:S(2)}) collective-permute-start(bf16[256,1792]{1,0:T(8,128)(2,1)S(1)} %collective-permute-done.3), channel_id=1, source_target_pairs={{64,128},{65,1},{66,130},{67,3},{68,132},{69,5},{70,134},{71,7},{7... | collective-permute-start | bytes 2752520 | tf_op jit(solution)/shard_map/ppermute | solution.py:29
  44.9 0.9 copy-start.2
  61.1 47.4 %collective-permute-start.6 = (f32[2,256,256]{2,1,0:T(8,128)S(1)}, f32[2,256,256]{2,1,0:T(8,128)S(1)}, u32[]{:S(2)}, u32[]{:S(2)}) collective-permute-start(f32[2,256,256]{2,1,0:T(8,128)S(1)} %pad_maximum_fusion.3), channel_id=1, source_target_pairs={{0,8},{1,9},{2,10},{3,11},{4,12},{5,13},{6,14},{7,15},{8,0},{9,1},... | collective-permute-start | bytes 1572872 | tf_op jit(solution)/shard_map/ppermute | solution.py:29
  65.1 45.4 %collective-permute-start.5 = (f32[2,256,256]{2,1,0:T(8,128)S(1)}, f32[2,256,256]{2,1,0:T(8,128)S(1)}, u32[]{:S(2)}, u32[]{:S(2)}) collective-permute-start(f32[2,256,256]{2,1,0:T(8,128)S(1)} %pad_maximum_fusion.2), channel_id=1, source_target_pairs={{0,12},{1,13},{2,14},{3,15},{4,8},{5,9},{6,10},{7,11},{8,4},{9,5},... | collective-permute-start | bytes 1572872 | tf_op jit(solution)/shard_map/ppermute | solution.py:29
  69.8 40.7 %collective-permute-start.4 = (f32[2,256,256]{2,1,0:T(8,128)S(1)}, f32[2,256,256]{2,1,0:T(8,128)S(1)}, u32[]{:S(2)}, u32[]{:S(2)}) collective-permute-start(f32[2,256,256]{2,1,0:T(8,128)S(1)} %pad_maximum_fusion.1), channel_id=1, source_target_pairs={{0,4},{1,5},{2,6},{3,7},{4,0},{5,1},{6,2},{7,3},{8,12},{9,13},{10,... | collective-permute-start | bytes 1572872 | tf_op jit(solution)/shard_map/ppermute | solution.py:29
  72.1 24.9 %collective-permute-start.9 = (bf16[256,1792]{1,0:T(8,128)(2,1)S(1)}, bf16[256,1792]{1,0:T(8,128)(2,1)S(1)}, u32[]{:S(2)}, u32[]{:S(2)}) collective-permute-start(bf16[256,1792]{1,0:T(8,128)(2,1)S(1)} %collective-permute-done.8), channel_id=1, source_target_pairs={{65,1},{67,3},{69,5},{71,7},{73,9},{75,11},{77,13},{79,15},{81,17}... | collective-permute-start | bytes 2752520 | tf_op jit(solution)/shard_map/ppermute | solution.py:29
  98.3 16.9 %collective-permute-start.12 = (f32[2,256,256]{1,2,0:T(8,128)}, f32[2,256,256]{1,2,0:T(8,128)}, u32[]{:S(2)}, u32[]{:S(2)}) collective-permute-start(f32[2,256,256]{1,2,0:T(8,128)} %pad_maximum_fusion.6), channel_id=1, source_target_pairs={{1,9},{3,11},{5,13},{7,15},{9,1},{11,3},{13,5},{15,7},{17,25},{19,... | collective-permute-start | bytes 1572872 | tf_op jit(solution)/shard_map/ppermute | solution.py:29
  103.5 12.1 %collective-permute-start.11 = (f32[2,256,256]{1,2,0:T(8,128)}, f32[2,256,256]{1,2,0:T(8,128)}, u32[]{:S(2)}, u32[]{:S(2)}) collective-permute-start(f32[2,256,256]{1,2,0:T(8,128)} %pad_maximum_fusion.5), channel_id=1, source_target_pairs={{1,13},{3,15},{5,9},{7,11},{9,5},{11,7},{13,1},{15,3},{17,29},{19,... | collective-permute-start | bytes 1572872 | tf_op jit(solution)/shard_map/ppermute | solution.py:29
  108.5 10.2 %collective-permute-start.10 = (f32[2,256,256]{1,2,0:T(8,128)}, f32[2,256,256]{1,2,0:T(8,128)}, u32[]{:S(2)}, u32[]{:S(2)}) collective-permute-start(f32[2,256,256]{1,2,0:T(8,128)} %pad_maximum_fusion.4), channel_id=1, source_target_pairs={{1,5},{3,7},{5,1},{7,3},{9,13},{11,15},{13,9},{15,11},{17,21},{19,... | collective-permute-start | bytes 1572872 | tf_op jit(solution)/shard_map/ppermute | solution.py:29
  111.6 12.9 %collective-permute-start.7 = (f32[3,128,256]{2,1,0:T(8,128)}, f32[3,128,256]{2,1,0:T(8,128)}, u32[]{:S(2)}, u32[]{:S(2)}) collective-permute-start(f32[3,128,256]{2,1,0:T(8,128)} %fusion.5), channel_id=1, source_target_pairs={{0,2},{1,3},{2,0},{3,1},{4,6},{5,7},{6,4},{7,5},{8,10},{9,11},{10,... | collective-permute-start | bytes 1179656 | tf_op jit(solution)/shard_map/ppermute | solution.py:29
  120.7 9.9 %collective-permute-start.13 = (f32[4,128,256]{2,1,0:T(8,128)S(1)}, f32[4,128,256]{2,1,0:T(8,128)S(1)}, u32[]{:S(2)}, u32[]{:S(2)}) collective-permute-start(f32[4,128,256]{2,1,0:T(8,128)S(1)} %constant_dynamic-slice_fusion.1), channel_id=1, source_target_pairs={{1,3},{3,1},{5,7},{7,5},{9,11},{11,9},{13,15},{15,13},{17,19},{19,... | collective-permute-start | bytes 1572872 | tf_op jit(solution)/shard_map/ppermute | solution.py:29
  125.5 7.8 %collective-permute-start.14 = (f32[128,256]{1,0:T(8,128)S(1)}, f32[128,256]{1,0:T(8,128)S(1)}, u32[]{:S(2)}, u32[]{:S(2)}) collective-permute-start(f32[128,256]{1,0:T(8,128)S(1)} %get-tuple-element.16), channel_id=1, source_target_pairs={{1,65},{3,67},{5,81},{7,83},{9,97},{11,99},{13,113},{15,115},{17,6... | collective-permute-start | bytes 393224 | tf_op jit(solution)/shard_map/ppermute | solution.py:29
  130.7 3.2 %collective-permute-start.15 = (f32[128,256]{1,0:T(8,128)S(1)}, f32[128,256]{1,0:T(8,128)S(1)}, u32[]{:S(2)}, u32[]{:S(2)}) collective-permute-start(f32[128,256]{1,0:T(8,128)S(1)} %get-tuple-element.12), channel_id=1, source_target_pairs={{1,193},{3,195},{5,209},{7,211},{9,225},{11,227},{13,241},{15,243}... | collective-permute-start | bytes 393224 | tf_op jit(solution)/shard_map/ppermute | solution.py:29
  132.0 3.3 %collective-permute-start.16 = (f32[128,256]{1,0:T(8,128)S(1)}, f32[128,256]{1,0:T(8,128)S(1)}, u32[]{:S(2)}, u32[]{:S(2)}) collective-permute-start(f32[128,256]{1,0:T(8,128)S(1)} %get-tuple-element.11), channel_id=1, source_target_pairs={{1,129},{3,131},{5,145},{7,147},{9,161},{11,163},{13,177},{15,179}... | collective-permute-start | bytes 393224 | tf_op jit(solution)/shard_map/ppermute | solution.py:29
  135.4 23.2 %copy-start.1 = (f32[8,8,8,128]{3,1,2,0:T(8,128)S(1)}, f32[8,8,8,128]{3,1,2,0:T(8,128)}, u32[]{:S(2)}) copy-start(f32[8,8,8,128]{3,1,2,0:T(8,128)} %convert_bitcast_fusion) | copy-start | bytes 786436
  135.4 23.2 %copy-start.3 = (f32[1,64,8]{1,2,0:T(8,128)S(1)}, f32[1,64,8]{1,2,0:T(8,128)}, u32[]{:S(2)}) copy-start(f32[1,64,8]{1,2,0:T(8,128)} %param.5) | copy-start | bytes 6148
  135.4 24.2 %collective-permute-start.17 = (f32[4,64,256]{2,1,0:T(8,128)S(1)}, f32[4,64,256]{2,1,0:T(8,128)S(1)}, u32[]{:S(2)}, u32[]{:S(2)}) collective-permute-start(f32[4,64,256]{2,1,0:T(8,128)S(1)} %constant_dynamic-slice_fusion), channel_id=1, source_target_pairs={{0,1},{1,0},{2,3},{3,2},{4,5},{5,4},{6,7},{7,6},{8,9},{9,8},{10,11... | collective-permute-start | bytes 786440 | tf_op jit(solution)/shard_map/ppermute | solution.py:29
  159.8 0.7 copy-start.7
  159.8 0.7 copy-start.8
  159.8 0.6 copy-start.9
  159.8 0.7 copy-start.10
  159.8 0.7 copy-start.11
  159.9 0.7 copy-start.12
  159.9 0.7 copy-start.13
  159.9 0.7 copy-start.14
  159.9 0.7 copy-start.15
  160.0 0.7 copy-start.4
  160.0 0.7 copy-start.5
  160.0 0.7 copy-start.6

commit v3 on v2

--- a/solution.py
+++ b/solution.py
@@ -101,7 +101,7 @@
         return lax.dynamic_slice_in_dim(array, flag * size, size, axis)
 
     own, across = [None] * SUPERS, [None] * SUPERS
-    for steps in ((0, 1), (2, 3)):
+    for steps in ((0, 1), (2,), (3,)):
         parts = [
             jnp.stack([product(rows, passing[step]) for step in steps]) for rows in stationary
         ]
@@ -109,6 +109,9 @@
         total = parts[0]
         for d in (1, 3, 2):
             total = total + permute(parts[d], lambda at, d=d: dict(x=at["x"] ^ d), valid)
+        if steps[-1] < SUPERS - 1:
+            ahead = steps[-1] + 1
+            passing[ahead], total = lax.optimization_barrier((passing[ahead], total))
         far = [k for k, step in enumerate(steps) if step]
         both = jnp.stack(list(total) + [total[k].T for k in far])
         done = half_of(both, yl, half, 1) + permute(

time: 164 us -> 183 us (1.12)
  matrix products: 7.79 us -> 24.4 us
  waiting for transfers between devices: 67.7 us -> 52.7 us
  starting transfers between devices: 68.8 us -> 81.5 us
  local copies, waits for them, and re-layouts: 3.72 us -> 6.31 us
    dot_general x16, matrix products: 6.92 us -> 23.5 us  [product(): lax.dot_general(rows, cols, (((1,), (1,)), ((), ())), preferred_element_t...]
    ppermute x18 -> x22, waiting for transfers between devices: 67.7 us -> 52.7 us  [permute(): return lax.ppermute(array, AXES, pairs)]
    ppermute x18 -> x22, starting transfers between devices: 68.8 us -> 81.5 us  [permute(): return lax.ppermute(array, AXES, pairs)]
    another operation x6 -> x3, other arithmetic: 2.64 us -> 0.11 us  [per_device(): jnp.stack([product(rows, passing[step]) for step in steps])]
    optimization_barrier x0 -> x2, local copies, waits for them, and re-layouts: none -> 1.87 us  [per_device(): passing[ahead], total = lax.optimization_barrier((passing[ahead], total))]
  transfers between devices with their start and end apart: 18 -> 22, of which waited for: 9 -> 7; matrix products, arithmetic and copies ran while one was open for 13% -> 23% of each run, Pallas kernels for 0% -> 0%
where the time goes in v3:
time: 183 us; the launch traced here: 181 us
  starting transfers between devices  81.5 us (45%)
  waiting for transfers between devices  52.7 us (29%)
  matrix products  24.4 us (13%)
  other arithmetic  14.9 us (8%)
  local copies, waits for them, and re-layouts  6.31 us (3%)
    ppermute x22, starting transfers between devices, permute(): return lax.ppermute(array, AXES, pairs)  81.5 us
    ppermute x22, waiting for transfers between devices, permute(): return lax.ppermute(array, AXES, pairs)  52.7 us
    dot_general x16, matrix products, product(): lax.dot_general(rows, cols, (((1,), (1,)), ((), ())), preferred_element_t...  23.5 us
  transfers between devices with their start and end apart: 22, of which 7 were waited for; matrix products, arithmetic and copies ran while one was open for 23% of the time, Pallas kernels for 0%

profile of v3, /device:TPU:7, one launch (start us, length us, event | category | flops | bytes accessed | tf_op | source)
XLA Modules:
  0.0 181.3 jit_solution(14612963294956455568)
XLA Ops:
  0.6 3.5 %collective-permute-start.2 = (bf16[256,1792]{1,0:T(8,128)(2,1)}, bf16[256,1792]{1,0:T(8,128)(2,1)S(1)}, u32[]{:S(2)}, u32[]{:S(2)}) collective-permute-start(bf16[256,1792]{1,0:T(8,128)(2,1)} %param.3), channel_id=1, source_target_pairs={{0,32},{1,33},{2,34},{3,35},{4,36},{5,37},{6,38},{7,39},{8,40},{9,... | collective-permute-start | bytes 2752520 | tf_op jit(solution)/shard_map/ppermute | solution.py:29
  4.2 4.8 %collective-permute-start.4 = (bf16[256,1792]{1,0:T(8,128)(2,1)}, bf16[256,1792]{1,0:T(8,128)(2,1)S(1)}, u32[]{:S(2)}, u32[]{:S(2)}) collective-permute-start(bf16[256,1792]{1,0:T(8,128)(2,1)} %param.3), channel_id=1, source_target_pairs={{0,16},{1,17},{2,18},{3,19},{4,20},{5,21},{6,22},{7,23},{8,24},{9,... | collective-permute-start | bytes 2752520 | tf_op jit(solution)/shard_map/ppermute | solution.py:29
  9.0 1.3 collective-permute-start
  10.3 23.8 %collective-permute-done.2 = bf16[256,1792]{1,0:T(8,128)(2,1)S(1)} collective-permute-done((bf16[256,1792]{1,0:T(8,128)(2,1)}, bf16[256,1792]{1,0:T(8,128)(2,1)S(1)}, u32[]{:S(2)}, u32[]{:S(2)}) %collective-permute-start.2) | collective-permute-done | bytes 917536 | tf_op jit(solution)/shard_map/ppermute | solution.py:29
  34.2 4.8 %collective-permute-start.3 = (bf16[256,1792]{1,0:T(8,128)(2,1)S(1)}, bf16[256,1792]{1,0:T(8,128)(2,1)}, u32[]{:S(2)}, u32[]{:S(2)}) collective-permute-start(bf16[256,1792]{1,0:T(8,128)(2,1)S(1)} %collective-permute-done.2), channel_id=1, source_target_pairs={{0,16},{1,17},{2,18},{3,19},{4,20},{5,21},{6,22},{7,23},{8,24},{9,... | collective-permute-start | bytes 2752520 | tf_op jit(solution)/shard_map/ppermute | solution.py:29
  43.0 1.6 convert_bitcast_fusion
  44.6 1.4 collective-permute-start.1
  46.1 0.9 copy-done.7
  47.0 11.2 %collective-permute-done.3 = bf16[256,1792]{1,0:T(8,128)(2,1)} collective-permute-done((bf16[256,1792]{1,0:T(8,128)(2,1)S(1)}, bf16[256,1792]{1,0:T(8,128)(2,1)}, u32[]{:S(2)}, u32[]{:S(2)}) %collective-permute-start.3) | collective-permute-done | bytes 917536 | tf_op jit(solution)/shard_map/ppermute | solution.py:29
  58.2 2.3 %broadcast_select_fusion.7 = (bf16[256,1792]{1,0:T(8,128)(2,1)S(1)}, bf16[256,1792]{1,0:T(8,128)(2,1)S(1)}, bf16[256,1792]{1,0:T(8,128)(2,1)S(1)}, bf16[256,1792]{1,0:T(8,128)(2,1)S(1)}) fusion(pred[]{:T(512)S(6)} %eq.29, bf16[256,1792]{1,0:T(8,128)(2,1)} %collective-permute-done.3, bf16[256,1792]{1,0:T(8,128)(2,1)} %copy-done.6, pred[]{:T(512)S(6)} %eq.30, ...), kind=kLoop, calls=%fused_computation.29 | loop fusion | flops 3670016 | bytes 7340034 | tf_op jit(solution)/shard_map/jit(_where)/select_n | solution.py:65
  60.9 1.6 convolution_bitcast_fusion.12
  62.6 2.5 %collective-permute-start.5 = (f32[2,256,256]{2,1,0:T(8,128)S(1)}, f32[2,256,256]{2,1,0:T(8,128)S(1)}, u32[]{:S(2)}, u32[]{:S(2)}) collective-permute-start(f32[2,256,256]{2,1,0:T(8,128)S(1)} %pad_maximum_fusion), channel_id=1, source_target_pairs={{0,4},{1,5},{2,6},{3,7},{4,0},{5,1},{6,2},{7,3},{8,12},{9,13},{10,... | collective-permute-start | bytes 1572872 | tf_op jit(solution)/shard_map/ppermute | solution.py:29
  65.5 1.6 convolution_bitcast_fusion.10
  67.2 2.8 %collective-permute-start.6 = (f32[2,256,256]{2,1,0:T(8,128)S(1)}, f32[2,256,256]{2,1,0:T(8,128)S(1)}, u32[]{:S(2)}, u32[]{:S(2)}) collective-permute-start(f32[2,256,256]{2,1,0:T(8,128)S(1)} %pad_maximum_fusion.1), channel_id=1, source_target_pairs={{0,12},{1,13},{2,14},{3,15},{4,8},{5,9},{6,10},{7,11},{8,4},{9,5},... | collective-permute-start | bytes 1572872 | tf_op jit(solution)/shard_map/ppermute | solution.py:29
  70.4 1.6 convolution_bitcast_fusion.8
  72.1 3.7 %collective-permute-start.7 = (f32[2,256,256]{2,1,0:T(8,128)S(1)}, f32[2,256,256]{2,1,0:T(8,128)S(1)}, u32[]{:S(2)}, u32[]{:S(2)}) collective-permute-start(f32[2,256,256]{2,1,0:T(8,128)S(1)} %pad_maximum_fusion.2), channel_id=1, source_target_pairs={{0,8},{1,9},{2,10},{3,11},{4,12},{5,13},{6,14},{7,15},{8,0},{9,1},... | collective-permute-start | bytes 1572872 | tf_op jit(solution)/shard_map/ppermute | solution.py:29
  76.4 1.3 collective-permute-start.9
  78.1 1.6 convolution_bitcast_fusion.14
  79.8 12.6 %collective-permute-done.6 = f32[2,256,256]{2,1,0:T(8,128)S(1)} collective-permute-done((f32[2,256,256]{2,1,0:T(8,128)S(1)}, f32[2,256,256]{2,1,0:T(8,128)S(1)}, u32[]{:S(2)}, u32[]{:S(2)}) %collective-permute-start.6) | collective-permute-done | bytes 524320 | tf_op jit(solution)/shard_map/ppermute | solution.py:29
  92.5 2.3 %convolution_bitcast_fusion.6 = f32[1,256,256]{1,2,0:T(8,128)} fusion(bf16[256,1792]{1,0:T(8,128)(2,1)S(1)} %get-tuple-element.13, bf16[256,1792]{1,0:T(8,128)(2,1)} %collective-permute-done.1), kind=kOutput, calls=%fused_computation.8 | convolution fusion | flops 234881024 | bytes 2097152 | tf_op jit(solution)/shard_map/dot_general | solution.py:96
  94.9 2.3 %convolution_bitcast_fusion.5 = f32[1,256,256]{1,2,0:T(8,128)} fusion(bf16[256,1792]{1,0:T(8,128)(2,1)S(1)} %get-tuple-element.14, bf16[256,1792]{1,0:T(8,128)(2,1)} %collective-permute-done.1), kind=kOutput, calls=%fused_computation.7 | convolution fusion | flops 234881024 | bytes 2097152 | tf_op jit(solution)/shard_map/dot_general | solution.py:96
  97.2 2.4 %convolution_bitcast_fusion.4 = f32[1,256,256]{1,2,0:T(8,128)} fusion(bf16[256,1792]{1,0:T(8,128)(2,1)S(1)} %get-tuple-element.15, bf16[256,1792]{1,0:T(8,128)(2,1)} %collective-permute-done.1), kind=kOutput, calls=%fused_computation.6 | convolution fusion | flops 234881024 | bytes 2097152 | tf_op jit(solution)/shard_map/dot_general | solution.py:96
  99.6 1.9 %collective-permute-start.10 = (f32[1,256,256]{1,2,0:T(8,128)}, f32[1,256,256]{1,2,0:T(8,128)S(1)}, u32[]{:S(2)}, u32[]{:S(2)}) collective-permute-start(f32[1,256,256]{1,2,0:T(8,128)} %convolution_bitcast_fusion.6), channel_id=1, source_target_pairs={{1,5},{3,7},{5,1},{7,3},{9,13},{11,15},{13,9},{15,11},{17,21},{19,... | collective-permute-start | bytes 786440 | tf_op jit(solution)/shard_map/ppermute | solution.py:29
  101.5 2.8 %collective-permute-start.11 = (f32[1,256,256]{1,2,0:T(8,128)}, f32[1,256,256]{1,2,0:T(8,128)}, u32[]{:S(2)}, u32[]{:S(2)}) collective-permute-start(f32[1,256,256]{1,2,0:T(8,128)} %convolution_bitcast_fusion.5), channel_id=1, source_target_pairs={{1,13},{3,15},{5,9},{7,11},{9,5},{11,7},{13,1},{15,3},{17,29},{19,... | collective-permute-start | bytes 786440 | tf_op jit(solution)/shard_map/ppermute | solution.py:29
  104.3 4.3 %collective-permute-start.12 = (f32[1,256,256]{1,2,0:T(8,128)}, f32[1,256,256]{1,2,0:T(8,128)}, u32[]{:S(2)}, u32[]{:S(2)}) collective-permute-start(f32[1,256,256]{1,2,0:T(8,128)} %convolution_bitcast_fusion.4), channel_id=1, source_target_pairs={{1,9},{3,11},{5,13},{7,15},{9,1},{11,3},{13,5},{15,7},{17,25},{19,... | collective-permute-start | bytes 786440 | tf_op jit(solution)/shard_map/ppermute | solution.py:29
  108.6 1.0 copy.19
  109.6 1.0 slice_bitcast_fusion
  111.4 3.2 %collective-permute-start.8 = (f32[3,128,256]{2,1,0:T(8,128)}, f32[3,128,256]{2,1,0:T(8,128)}, u32[]{:S(2)}, u32[]{:S(2)}) collective-permute-start(f32[3,128,256]{2,1,0:T(8,128)} %fusion.5), channel_id=1, source_target_pairs={{0,2},{1,3},{2,0},{3,1},{4,6},{5,7},{6,4},{7,5},{8,10},{9,11},{10,... | collective-permute-start | bytes 1179656 | tf_op jit(solution)/shard_map/ppermute | solution.py:29
  114.6 1.6 fusion.1
  116.3 1.1 add_add_fusion.1
  118.2 1.6 fusion.8
  119.9 2.1 %collective-permute-start.19 = (f32[2,128,256]{2,1,0:T(8,128)}, f32[2,128,256]{2,1,0:T(8,128)}, u32[]{:S(2)}, u32[]{:S(2)}) collective-permute-start(f32[2,128,256]{2,1,0:T(8,128)} %fusion.8), channel_id=1, source_target_pairs={{1,3},{3,1},{5,7},{7,5},{9,11},{11,9},{13,15},{15,13},{17,19},{19,... | collective-permute-start | bytes 786440 | tf_op jit(solution)/shard_map/ppermute | solution.py:29
  121.9 1.9 %convolution_bitcast_fusion.1 = f32[1,256,256]{1,2,0:T(8,128)S(1)} fusion(bf16[256,1792]{1,0:T(8,128)(2,1)} %copy-done.1, bf16[256,1792]{1,0:T(8,128)(2,1)} %collective-permute-done.9), kind=kOutput, calls=%fused_computation.3 | convolution fusion | flops 234881024 | bytes 2097152 | tf_op jit(solution)/shard_map/dot_general | solution.py:96
  123.8 2.8 %collective-permute-start.14 = (f32[1,256,256]{1,2,0:T(8,128)S(1)}, f32[1,256,256]{1,2,0:T(8,128)S(1)}, u32[]{:S(2)}, u32[]{:S(2)}) collective-permute-start(f32[1,256,256]{1,2,0:T(8,128)S(1)} %convolution_bitcast_fusion.1), channel_id=1, source_target_pairs={{1,13},{3,15},{5,9},{7,11},{9,5},{11,7},{13,1},{15,3},{17,29},{19,... | collective-permute-start | bytes 786440 | tf_op jit(solution)/shard_map/ppermute | solution.py:29
  126.6 1.6 convolution_bitcast_fusion.2
  128.2 2.1 %collective-permute-start.13 = (f32[1,256,256]{1,2,0:T(8,128)S(1)}, f32[1,256,256]{1,2,0:T(8,128)S(1)}, u32[]{:S(2)}, u32[]{:S(2)}) collective-permute-start(f32[1,256,256]{1,2,0:T(8,128)S(1)} %convolution_bitcast_fusion.2), channel_id=1, source_target_pairs={{1,5},{3,7},{5,1},{7,3},{9,13},{11,15},{13,9},{15,11},{17,21},{19,... | collective-permute-start | bytes 786440 | tf_op jit(solution)/shard_map/ppermute | solution.py:29
  130.3 1.6 convolution_bitcast_fusion
  131.9 4.9 %collective-permute-start.15 = (f32[1,256,256]{1,2,0:T(8,128)S(1)}, f32[1,256,256]{1,2,0:T(8,128)S(1)}, u32[]{:S(2)}, u32[]{:S(2)}) collective-permute-start(f32[1,256,256]{1,2,0:T(8,128)S(1)} %convolution_bitcast_fusion), channel_id=1, source_target_pairs={{1,9},{3,11},{5,13},{7,15},{9,1},{11,3},{13,5},{15,7},{17,25},{19,... | collective-permute-start | bytes 786440 | tf_op jit(solution)/shard_map/ppermute | solution.py:29
  136.8 1.1 fusion.7
  137.9 1.3 collective-permute-start.17
  139.2 1.6 fusion.2
  141.8 3.3 %collective-permute-start.16 = (f32[2,128,256]{2,1,0:T(8,128)S(1)}, f32[2,128,256]{2,1,0:T(8,128)S(1)}, u32[]{:S(2)}, u32[]{:S(2)}) collective-permute-start(f32[2,128,256]{2,1,0:T(8,128)S(1)} %fusion.11), channel_id=1, source_target_pairs={{1,3},{3,1},{5,7},{7,5},{9,11},{11,9},{13,15},{15,13},{17,19},{19,... | collective-permute-start | bytes 786440 | tf_op jit(solution)/shard_map/ppermute | solution.py:29
  145.1 1.0 fusion.10
  146.1 1.3 collective-permute-start.20
  147.4 1.6 collective-permute-done.16
  149.1 1.3 collective-permute-start.18
  150.4 1.9 %collective-permute-done.18 = f32[128,256]{1,0:T(8,128)S(1)} collective-permute-done((f32[128,256]{1,0:T(8,128)S(1)}, f32[128,256]{1,0:T(8,128)S(1)}, u32[]{:S(2)}, u32[]{:S(2)}) %collective-permute-start.18) | collective-permute-done | bytes 131104 | tf_op jit(solution)/shard_map/ppermute | solution.py:29
  152.5 24.3 %collective-permute-start.21 = (f32[4,64,256]{2,1,0:T(8,128)S(1)}, f32[4,64,256]{2,1,0:T(8,128)S(1)}, u32[]{:S(2)}, u32[]{:S(2)}) collective-permute-start(f32[4,64,256]{2,1,0:T(8,128)S(1)} %constant_dynamic-slice_fusion), channel_id=1, source_target_pairs={{0,1},{1,0},{2,3},{3,2},{4,5},{5,4},{6,7},{7,6},{8,9},{9,8},{10,11... | collective-permute-start | bytes 786440 | tf_op jit(solution)/shard_map/ppermute | solution.py:29
  (116 shorter events, 13.7 us)
Async XLA Ops:
  0.6 33.5 %collective-permute-start.2 = (bf16[256,1792]{1,0:T(8,128)(2,1)}, bf16[256,1792]{1,0:T(8,128)(2,1)S(1)}, u32[]{:S(2)}, u32[]{:S(2)}) collective-permute-start(bf16[256,1792]{1,0:T(8,128)(2,1)} %param.3), channel_id=1, source_target_pairs={{0,32},{1,33},{2,34},{3,35},{4,36},{5,37},{6,38},{7,39},{8,40},{9,... | collective-permute-start | bytes 2752520 | tf_op jit(solution)/shard_map/ppermute | solution.py:29
  4.2 41.8 %collective-permute-start.4 = (bf16[256,1792]{1,0:T(8,128)(2,1)}, bf16[256,1792]{1,0:T(8,128)(2,1)S(1)}, u32[]{:S(2)}, u32[]{:S(2)}) collective-permute-start(bf16[256,1792]{1,0:T(8,128)(2,1)} %param.3), channel_id=1, source_target_pairs={{0,16},{1,17},{2,18},{3,19},{4,20},{5,21},{6,22},{7,23},{8,24},{9,... | collective-permute-start | bytes 2752520 | tf_op jit(solution)/shard_map/ppermute | solution.py:29
  9.0 35.6 %collective-permute-start = (bf16[256,1792]{1,0:T(8,128)(2,1)}, bf16[256,1792]{1,0:T(8,128)(2,1)}, u32[]{:S(2)}, u32[]{:S(2)}) collective-permute-start(bf16[256,1792]{1,0:T(8,128)(2,1)} %param.3), channel_id=1, source_target_pairs={{0,64},{2,66},{4,68},{6,70},{8,72},{10,74},{12,76},{14,78},{16,80}... | collective-permute-start | bytes 2752520 | tf_op jit(solution)/shard_map/ppermute | solution.py:29
  34.2 11.9 %copy-start.6 = (bf16[256,1792]{1,0:T(8,128)(2,1)}, bf16[256,1792]{1,0:T(8,128)(2,1)S(1)}, u32[]{:S(2)}) copy-start(bf16[256,1792]{1,0:T(8,128)(2,1)S(1)} %collective-permute-done.2) | copy-start | bytes 2752516
  34.2 24.0 %collective-permute-start.3 = (bf16[256,1792]{1,0:T(8,128)(2,1)S(1)}, bf16[256,1792]{1,0:T(8,128)(2,1)}, u32[]{:S(2)}, u32[]{:S(2)}) collective-permute-start(bf16[256,1792]{1,0:T(8,128)(2,1)S(1)} %collective-permute-done.2), channel_id=1, source_target_pairs={{0,16},{1,17},{2,18},{3,19},{4,20},{5,21},{6,22},{7,23},{8,24},{9,... | collective-permute-start | bytes 2752520 | tf_op jit(solution)/shard_map/ppermute | solution.py:29
  44.6 15.9 %copy-start = (bf16[256,1792]{1,0:T(8,128)(2,1)S(1)}, bf16[256,1792]{1,0:T(8,128)(2,1)}, u32[]{:S(2)}) copy-start(bf16[256,1792]{1,0:T(8,128)(2,1)} %param.3) | copy-start | bytes 2752516
  44.6 31.8 %collective-permute-start.1 = (bf16[256,1792]{1,0:T(8,128)(2,1)}, bf16[256,1792]{1,0:T(8,128)(2,1)}, u32[]{:S(2)}, u32[]{:S(2)}) collective-permute-start(bf16[256,1792]{1,0:T(8,128)(2,1)} %collective-permute-done), channel_id=1, source_target_pairs={{64,128},{65,1},{66,130},{67,3},{68,132},{69,5},{70,134},{71,7},{7... | collective-permute-start | bytes 2752520 | tf_op jit(solution)/shard_map/ppermute | solution.py:29
  46.0 0.9 copy-start.7
  60.5 34.4 %copy-start.1 = (bf16[256,1792]{1,0:T(8,128)(2,1)}, bf16[256,1792]{1,0:T(8,128)(2,1)S(1)}, u32[]{:S(2)}) copy-start(bf16[256,1792]{1,0:T(8,128)(2,1)S(1)} %get-tuple-element.14) | copy-start | bytes 2752516
  62.6 17.1 %collective-permute-start.5 = (f32[2,256,256]{2,1,0:T(8,128)S(1)}, f32[2,256,256]{2,1,0:T(8,128)S(1)}, u32[]{:S(2)}, u32[]{:S(2)}) collective-permute-start(f32[2,256,256]{2,1,0:T(8,128)S(1)} %pad_maximum_fusion), channel_id=1, source_target_pairs={{0,4},{1,5},{2,6},{3,7},{4,0},{5,1},{6,2},{7,3},{8,12},{9,13},{10,... | collective-permute-start | bytes 1572872 | tf_op jit(solution)/shard_map/ppermute | solution.py:29
  67.2 25.2 %collective-permute-start.6 = (f32[2,256,256]{2,1,0:T(8,128)S(1)}, f32[2,256,256]{2,1,0:T(8,128)S(1)}, u32[]{:S(2)}, u32[]{:S(2)}) collective-permute-start(f32[2,256,256]{2,1,0:T(8,128)S(1)} %pad_maximum_fusion.1), channel_id=1, source_target_pairs={{0,12},{1,13},{2,14},{3,15},{4,8},{5,9},{6,10},{7,11},{8,4},{9,5},... | collective-permute-start | bytes 1572872 | tf_op jit(solution)/shard_map/ppermute | solution.py:29
  72.1 20.3 %collective-permute-start.7 = (f32[2,256,256]{2,1,0:T(8,128)S(1)}, f32[2,256,256]{2,1,0:T(8,128)S(1)}, u32[]{:S(2)}, u32[]{:S(2)}) collective-permute-start(f32[2,256,256]{2,1,0:T(8,128)S(1)} %pad_maximum_fusion.2), channel_id=1, source_target_pairs={{0,8},{1,9},{2,10},{3,11},{4,12},{5,13},{6,14},{7,15},{8,0},{9,1},... | collective-permute-start | bytes 1572872 | tf_op jit(solution)/shard_map/ppermute | solution.py:29
  76.4 40.9 %collective-permute-start.9 = (bf16[256,1792]{1,0:T(8,128)(2,1)}, bf16[256,1792]{1,0:T(8,128)(2,1)}, u32[]{:S(2)}, u32[]{:S(2)}) collective-permute-start(bf16[256,1792]{1,0:T(8,128)(2,1)} %collective-permute-done.1), channel_id=1, source_target_pairs={{65,1},{67,3},{69,5},{71,7},{73,9},{75,11},{77,13},{79,15},{81,17}... | collective-permute-start | bytes 2752520 | tf_op jit(solution)/shard_map/ppermute | solution.py:29
  99.6 15.0 %collective-permute-start.10 = (f32[1,256,256]{1,2,0:T(8,128)}, f32[1,256,256]{1,2,0:T(8,128)S(1)}, u32[]{:S(2)}, u32[]{:S(2)}) collective-permute-start(f32[1,256,256]{1,2,0:T(8,128)} %convolution_bitcast_fusion.6), channel_id=1, source_target_pairs={{1,5},{3,7},{5,1},{7,3},{9,13},{11,15},{13,9},{15,11},{17,21},{19,... | collective-permute-start | bytes 786440 | tf_op jit(solution)/shard_map/ppermute | solution.py:29
  101.5 14.7 %collective-permute-start.11 = (f32[1,256,256]{1,2,0:T(8,128)}, f32[1,256,256]{1,2,0:T(8,128)}, u32[]{:S(2)}, u32[]{:S(2)}) collective-permute-start(f32[1,256,256]{1,2,0:T(8,128)} %convolution_bitcast_fusion.5), channel_id=1, source_target_pairs={{1,13},{3,15},{5,9},{7,11},{9,5},{11,7},{13,1},{15,3},{17,29},{19,... | collective-permute-start | bytes 786440 | tf_op jit(solution)/shard_map/ppermute | solution.py:29
  104.3 12.0 %collective-permute-start.12 = (f32[1,256,256]{1,2,0:T(8,128)}, f32[1,256,256]{1,2,0:T(8,128)}, u32[]{:S(2)}, u32[]{:S(2)}) collective-permute-start(f32[1,256,256]{1,2,0:T(8,128)} %convolution_bitcast_fusion.4), channel_id=1, source_target_pairs={{1,9},{3,11},{5,13},{7,15},{9,1},{11,3},{13,5},{15,7},{17,25},{19,... | collective-permute-start | bytes 786440 | tf_op jit(solution)/shard_map/ppermute | solution.py:29
  110.5 0.9 copy-start.3
  111.4 25.4 %collective-permute-start.8 = (f32[3,128,256]{2,1,0:T(8,128)}, f32[3,128,256]{2,1,0:T(8,128)}, u32[]{:S(2)}, u32[]{:S(2)}) collective-permute-start(f32[3,128,256]{2,1,0:T(8,128)} %fusion.5), channel_id=1, source_target_pairs={{0,2},{1,3},{2,0},{3,1},{4,6},{5,7},{6,4},{7,5},{8,10},{9,11},{10,... | collective-permute-start | bytes 1179656 | tf_op jit(solution)/shard_map/ppermute | solution.py:29
  119.9 25.2 %collective-permute-start.19 = (f32[2,128,256]{2,1,0:T(8,128)}, f32[2,128,256]{2,1,0:T(8,128)}, u32[]{:S(2)}, u32[]{:S(2)}) collective-permute-start(f32[2,128,256]{2,1,0:T(8,128)} %fusion.8), channel_id=1, source_target_pairs={{1,3},{3,1},{5,7},{7,5},{9,11},{11,9},{13,15},{15,13},{17,19},{19,... | collective-permute-start | bytes 786440 | tf_op jit(solution)/shard_map/ppermute | solution.py:29
  123.8 17.0 %collective-permute-start.14 = (f32[1,256,256]{1,2,0:T(8,128)S(1)}, f32[1,256,256]{1,2,0:T(8,128)S(1)}, u32[]{:S(2)}, u32[]{:S(2)}) collective-permute-start(f32[1,256,256]{1,2,0:T(8,128)S(1)} %convolution_bitcast_fusion.1), channel_id=1, source_target_pairs={{1,13},{3,15},{5,9},{7,11},{9,5},{11,7},{13,1},{15,3},{17,29},{19,... | collective-permute-start | bytes 786440 | tf_op jit(solution)/shard_map/ppermute | solution.py:29
  128.2 8.6 %copy-start.4 = (f32[1,256,256]{2,1,0:T(8,128)S(1)}, f32[1,256,256]{2,1,0:T(8,128)}, u32[]{:S(2)}) copy-start(f32[1,256,256]{2,1,0:T(8,128)} %copy-done.3) | copy-start | bytes 786436
  128.2 11.0 %collective-permute-start.13 = (f32[1,256,256]{1,2,0:T(8,128)S(1)}, f32[1,256,256]{1,2,0:T(8,128)S(1)}, u32[]{:S(2)}, u32[]{:S(2)}) collective-permute-start(f32[1,256,256]{1,2,0:T(8,128)S(1)} %convolution_bitcast_fusion.2), channel_id=1, source_target_pairs={{1,5},{3,7},{5,1},{7,3},{9,13},{11,15},{13,9},{15,11},{17,21},{19,... | collective-permute-start | bytes 786440 | tf_op jit(solution)/shard_map/ppermute | solution.py:29
  131.9 9.6 %collective-permute-start.15 = (f32[1,256,256]{1,2,0:T(8,128)S(1)}, f32[1,256,256]{1,2,0:T(8,128)S(1)}, u32[]{:S(2)}, u32[]{:S(2)}) collective-permute-start(f32[1,256,256]{1,2,0:T(8,128)S(1)} %convolution_bitcast_fusion), channel_id=1, source_target_pairs={{1,9},{3,11},{5,13},{7,15},{9,1},{11,3},{13,5},{15,7},{17,25},{19,... | collective-permute-start | bytes 786440 | tf_op jit(solution)/shard_map/ppermute | solution.py:29
  137.9 12.5 %collective-permute-start.17 = (f32[128,256]{1,0:T(8,128)S(1)}, f32[128,256]{1,0:T(8,128)S(1)}, u32[]{:S(2)}, u32[]{:S(2)}) collective-permute-start(f32[128,256]{1,0:T(8,128)S(1)} %get-tuple-element.19), channel_id=1, source_target_pairs={{1,65},{3,67},{5,81},{7,83},{9,97},{11,99},{13,113},{15,115},{17,6... | collective-permute-start | bytes 393224 | tf_op jit(solution)/shard_map/ppermute | solution.py:29
  141.7 3.4 %copy-start.2 = (f32[1,256,256]{2,1,0:T(8,128)S(1)}, f32[1,256,256]{2,1,0:T(8,128)}, u32[]{:S(2)}) copy-start(f32[1,256,256]{2,1,0:T(8,128)} %copy.29) | copy-start | bytes 786436
  141.8 7.2 %collective-permute-start.16 = (f32[2,128,256]{2,1,0:T(8,128)S(1)}, f32[2,128,256]{2,1,0:T(8,128)S(1)}, u32[]{:S(2)}, u32[]{:S(2)}) collective-permute-start(f32[2,128,256]{2,1,0:T(8,128)S(1)} %fusion.11), channel_id=1, source_target_pairs={{1,3},{3,1},{5,7},{7,5},{9,11},{11,9},{13,15},{15,13},{17,19},{19,... | collective-permute-start | bytes 786440 | tf_op jit(solution)/shard_map/ppermute | solution.py:29
  146.1 4.3 %collective-permute-start.20 = (f32[128,256]{1,0:T(8,128)S(1)}, f32[128,256]{1,0:T(8,128)S(1)}, u32[]{:S(2)}, u32[]{:S(2)}) collective-permute-start(f32[128,256]{1,0:T(8,128)S(1)} %slice_bitcast_fusion.1), channel_id=1, source_target_pairs={{1,129},{3,131},{5,145},{7,147},{9,161},{11,163},{13,177},{15,179}... | collective-permute-start | bytes 393224 | tf_op jit(solution)/shard_map/ppermute | solution.py:29
  149.1 3.2 %collective-permute-start.18 = (f32[128,256]{1,0:T(8,128)S(1)}, f32[128,256]{1,0:T(8,128)S(1)}, u32[]{:S(2)}, u32[]{:S(2)}) collective-permute-start(f32[128,256]{1,0:T(8,128)S(1)} %slice_bitcast_fusion.3), channel_id=1, source_target_pairs={{1,193},{3,195},{5,209},{7,211},{9,225},{11,227},{13,241},{15,243}... | collective-permute-start | bytes 393224 | tf_op jit(solution)/shard_map/ppermute | solution.py:29
  152.4 24.4 %copy-start.5 = (f32[8,8,8,128]{3,1,2,0:T(8,128)S(1)}, f32[8,8,8,128]{3,1,2,0:T(8,128)}, u32[]{:S(2)}) copy-start(f32[8,8,8,128]{3,1,2,0:T(8,128)} %convert_bitcast_fusion) | copy-start | bytes 786436
  152.4 24.4 %copy-start.8 = (f32[1,64,8]{1,2,0:T(8,128)S(1)}, f32[1,64,8]{1,2,0:T(8,128)}, u32[]{:S(2)}) copy-start(f32[1,64,8]{1,2,0:T(8,128)} %param.5) | copy-start | bytes 6148
  152.5 25.4 %collective-permute-start.21 = (f32[4,64,256]{2,1,0:T(8,128)S(1)}, f32[4,64,256]{2,1,0:T(8,128)S(1)}, u32[]{:S(2)}, u32[]{:S(2)}) collective-permute-start(f32[4,64,256]{2,1,0:T(8,128)S(1)} %constant_dynamic-slice_fusion), channel_id=1, source_target_pairs={{0,1},{1,0},{2,3},{3,2},{4,5},{5,4},{6,7},{7,6},{8,9},{9,8},{10,11... | collective-permute-start | bytes 786440 | tf_op jit(solution)/shard_map/ppermute | solution.py:29
  178.0 0.7 copy-start.12
  178.0 0.6 copy-start.13
  178.0 0.6 copy-start.14
  178.0 0.7 copy-start.15
  178.1 0.7 copy-start.16
  178.1 0.7 copy-start.17
  178.1 0.7 copy-start.18
  178.1 0.7 copy-start.19
  178.1 0.7 copy-start.20
  178.1 0.7 copy-start.21
  178.1 0.7 copy-start.22
  178.2 0.6 copy-start.23
  178.2 0.7 copy-start.24
  178.2 0.6 copy-start.9
  178.2 0.7 copy-start.10
  178.3 0.7 copy-start.11

commit v4 on v3

v4 whole, which is shorter than its diff:
```python
import functools

import jax
import jax.numpy as jnp
from jax import lax
from jax.experimental import pallas as pl
from jax.experimental.pallas import tpu as pltpu
from jax.sharding import PartitionSpec as P

GROUP = 128
AXES = ("dp", "tensor")
SUPERS = 4
VMEM = pl.BlockSpec(memory_space=pltpu.VMEM)
SMEM = pl.BlockSpec(memory_space=pltpu.SMEM)


def place(index):
    dp, tensor = divmod(index, 16)
    return dict(
        b=dp >> 4, g=(dp >> 2) & 3, h=dp & 3, x=tensor >> 2, yl=(tensor >> 1) & 1, c=tensor & 1
    )


def index_of(b, g, h, x, yl, c):
    return ((b << 4 | g << 2 | h) << 4) | x << 2 | yl << 1 | c


def permute(array, target, keep=lambda at: True):
    total = lax.axis_size("dp") * lax.axis_size("tensor")
    pairs = []
    for i in range(total):
        at = place(i)
        if keep(at):
            pairs.append((i, index_of(**{**at, **target(at)})))
    return lax.ppermute(array, AXES, pairs)


def reach(at):
    return at["g"] if at["c"] == 0 else SUPERS - 1 - at["g"]


def onward(at):
    return dict(g=at["g"] + (1 if at["c"] == 0 else -1))


def call(kernel, name, outs, flops, *operands):
    in_specs = [SMEM if op.dtype == jnp.int32 else VMEM for op in operands]
    moved = sum(op.size * op.dtype.itemsize for op in (*operands, *outs))
    return pl.pallas_call(
        kernel,
        out_shape=outs,
        in_specs=in_specs,
        out_specs=[VMEM] * len(outs),
        compiler_params=pltpu.CompilerParams(vmem_limit_bytes=40 * 1024 * 1024),
        cost_estimate=pl.CostEstimate(flops=flops, bytes_accessed=moved, transcendentals=0),
        name=name,
    )(*operands)


def floats(*shape):
    return jax.ShapeDtypeStruct(shape, jnp.float32)


def products_kernel(where, *refs):
    rows, cols, outs = refs[:4], refs[4:-4], refs[-4:]
    for turn in range(4):

        @pl.when(where[0] == turn)
        def _():
            for d in range(4):
                for k, col in enumerate(cols):
                    outs[d][k] = lax.dot_general(
                        rows[d ^ turn][...],
                        col[...],
                        (((1,), (1,)), ((), ())),
                        preferred_element_type=jnp.float32,
                    )


def products(where, rows, cols):
    size, depth = rows[0].shape
    count = len(cols)
    return call(
        products_kernel,
        "block_products",
        [floats(count, size, size)] * 4,
        8 * count * size * size * depth,
        where,
        *rows,
        *cols,
    )


def halves_kernel(far, where, first, second, third, fourth, keep, give):
    count, size, _ = first.shape
    half = size // 2
    upper = where[1] == 1
    totals = [first[k] + second[k] + third[k] + fourth[k] for k in range(count)]
    for k, total in enumerate(totals + [totals[k].T for k in far]):
        keep[k] = jnp.where(upper, total[half:], total[:half])
        give[k] = jnp.where(upper, total[:half], total[half:])


def halves(where, far, parts):
    count, size, _ = parts[0].shape
    shape = floats(count + len(far), size // 2, size)
    return call(
        functools.partial(halves_kernel, far), "halves", [shape, shape], 0, where, *parts
    )


def strips_kernel(where, *refs):
    own, across, keep, give = refs[:4], (None, *refs[4:7]), refs[7], refs[8]
    half = keep.shape[1]
    second = where[2] == 1
    back = own[3][...] + across[1][...], own[1][...] + across[3][...]
    strips = [
        own[0][...],
        jnp.where(second, back[1], back[0]),
        own[2][...] + across[2][...],
        jnp.where(second, back[0], back[1]),
    ]
    for k, strip in enumerate(strips):
        keep[k] = jnp.where(second, strip[half:], strip[:half])
        give[k] = jnp.where(second, strip[:half], strip[half:])


def strips(where, own, across):
    rows, cols = own[0].shape
    shape = floats(SUPERS, rows // 2, cols)
    return call(strips_kernel, "strips", [shape, shape], 0, where, *own, *across)


def refresh_kernel(where, mine, other, codes, scales, new_codes, new_scales):
    bits = lax.broadcasted_iota(jnp.int32, (GROUP, GROUP), 0) & lax.broadcasted_iota(
        jnp.int32, (GROUP, GROUP), 1
    )
    for shift in (4, 2, 1):
        bits = bits ^ (bits >> shift)
    signs = 1.0 - 2.0 * (bits & 1).astype(jnp.float32)
    unit = 1.0 / (GROUP**0.5)
    per_block = mine.shape[2] // GROUP
    largest = []
    for j in range(SUPERS):
        offset = (j + SUPERS - where[3]) & (SUPERS - 1)
        block = mine[offset] + other[offset]
        for k in range(per_block):
            group = j * per_block + k
            at = slice(group * GROUP, (group + 1) * GROUP)
            turned = jnp.dot(
                block[:, k * GROUP : (k + 1) * GROUP],
                signs,
                precision=lax.Precision.HIGHEST,
                preferred_element_type=jnp.float32,
            )
            old = codes[:, at].astype(jnp.float32) * scales[:, group : group + 1]
            rotated = 0.95 * old + 0.05 * (turned * unit)
            peak = jnp.max(jnp.abs(rotated), axis=1, keepdims=True)
            new_codes[:, at] = (rotated / (peak + 1e-06)).astype(jnp.bfloat16)
            largest.append(peak)
    new_scales[...] = jnp.concatenate(largest, axis=1)


def refresh(where, mine, other, codes, scales):
    return call(
        refresh_kernel,
        "refresh",
        [
            jax.ShapeDtypeStruct(codes.shape, jnp.bfloat16),
            jax.ShapeDtypeStruct(scales.shape, jnp.float32),
        ],
        2 * codes.size * GROUP,
        where,
        mine,
        other,
        codes,
        scales,
    )


def per_device(gradient, left_codes, left_scales):
    dp, tensor = lax.axis_index("dp"), lax.axis_index("tensor")
    where = jnp.stack(
        [(tensor >> 2) ^ (dp & 3), (tensor >> 1) & 1, tensor & 1, (dp >> 2) & 3]
    ).astype(jnp.int32)

    z_block = permute(gradient, lambda at: dict(h=at["h"] ^ 2))
    y_block = permute(gradient, lambda at: dict(h=at["h"] ^ 1))
    z_block, y_block, sent = lax.optimization_barrier((z_block, y_block, gradient))
    zy_block = permute(z_block, lambda at: dict(h=at["h"] ^ 1))
    rows = [gradient, y_block, z_block, zy_block]

    def onwards(block, step):
        return permute(block, onward, lambda at: step - 1 <= reach(at) < SUPERS - 1)

    passing = [sent, onwards(sent, 1)]
    passing[1], rows[3] = lax.optimization_barrier((passing[1], rows[3]))
    passing.append(onwards(passing[1], 2))

    own, across = [None] * SUPERS, [None] * SUPERS
    for steps in ((0, 1), (2,), (3,)):
        parts = list(products(where, rows, [passing[step] for step in steps]))
        valid = lambda at, steps=steps: reach(at) >= steps[0]
        parts[1:] = [
            permute(parts[d], lambda at, d=d: dict(x=at["x"] ^ d), valid) for d in (1, 2, 3)
        ]
        if steps[0] == 0:
            passing[2], *parts = lax.optimization_barrier((passing[2], *parts))
            passing.append(onwards(passing[2], 3))
        far = [k for k, step in enumerate(steps) if step]
        keep, give = halves(where, far, parts)
        if steps[-1] < SUPERS - 1:
            ahead = steps[-1] + 1
            passing[ahead], keep, give = lax.optimization_barrier((passing[ahead], keep, give))
        came = permute(give, lambda at: dict(yl=at["yl"] ^ 1), valid)
        for k, step in enumerate(steps):
            own[step] = keep[k] + came[k]
        for k, place_no in enumerate(far, len(steps)):
            step = steps[place_no]
            across[step] = permute(
                keep[k] + came[k],
                lambda at, step=step: dict(
                    g=at["g"] + (-step if at["c"] == 0 else step), h=at["x"], x=at["h"]
                ),
                lambda at, step=step: reach(at) >= step,
            )

    mine, given = strips(where, own, across[1:])
    other = permute(given, lambda at: dict(c=at["c"] ^ 1))
    fresh_codes, fresh_scales = refresh(where, mine, other, left_codes[0], left_scales[0])
    return fresh_codes[None], fresh_scales[None]


def solution(mesh):
    return jax.shard_map(
        per_device,
        mesh=mesh,
        in_specs=(P("dp", "tensor"), P("dp", "tensor", None), P("dp", "tensor", None)),
        out_specs=(P("dp", "tensor", None), P("dp", "tensor", None)),
        check_vma=False,
    )
```

time: 183 us -> 179 us (0.978)
  matrix products: 24.4 us -> 0 us
  waiting for transfers between devices: 52.7 us -> 70.6 us
  other arithmetic: 14.9 us -> 0.2 us
  Pallas kernels: 0 us -> 11.9 us
  starting transfers between devices: 81.5 us -> 92.5 us
  local copies, waits for them, and re-layouts: 6.31 us -> 1.94 us
    dot_general x17 -> x0, matrix products: 24.4 us -> none  [the longest x16 23.5 us: product(): lax.dot_general(rows, cols, (((1,), (1,)), ((), ())), preferred_element_t...]
    ppermute x22, waiting for transfers between devices: 52.7 us -> 70.6 us  [permute(): return lax.ppermute(array, AXES, pairs)]
    pallas_call x0 -> x8, Pallas kernels: none -> 11.9 us  [call(): pl.pallas_call(kernel, out_shape=outs, in_specs=in_specs, out_specs=[VMEM...]
    ppermute x22, starting transfers between devices: 81.5 us -> 92.5 us  [permute(): return lax.ppermute(array, AXES, pairs)]
    add x11 -> x3, other arithmetic: 5.09 us -> 0.12 us  [per_device(): keep[k] + came[k]]
    another operation x9 -> x1, other arithmetic: 2.71 us -> 0.08 us  [per_device(): jnp.stack([tensor >> 2 ^ dp & 3, tensor >> 1 & 1, tensor & 1, dp >> 2 & 3])]
    select_n x1 -> x0, other arithmetic: 2.31 us -> none  [swap_if(): return (jnp.where(flag, second, first), jnp.where(flag, first, second))]
    optimization_barrier x2 -> x0, local copies, waits for them, and re-layouts: 1.87 us -> none  [per_device(): passing[ahead], total = lax.optimization_barrier((passing[ahead], total))]
  transfers between devices with their start and end apart: 22 -> 22, of which waited for: 7 -> 11; matrix products, arithmetic and copies ran while one was open for 23% -> 0% of each run, Pallas kernels for 0% -> 5%
where the time goes in v4:
time: 179 us; the launch traced here: 178 us
  starting transfers between devices  92.5 us (52%)
  waiting for transfers between devices  70.6 us (39%)
  Pallas kernels  11.9 us (7%)
  local copies, waits for them, and re-layouts  1.94 us (1%)
    ppermute x22, starting transfers between devices, permute(): return lax.ppermute(array, AXES, pairs)  92.5 us
    ppermute x22, waiting for transfers between devices, permute(): return lax.ppermute(array, AXES, pairs)  70.6 us
    pallas_call x8, Pallas kernels, call(): pl.pallas_call(kernel, out_shape=outs, in_specs=in_specs, out_specs=[VMEM...  11.9 us
  transfers between devices with their start and end apart: 22, of which 11 were waited for; matrix products, arithmetic and copies ran while one was open for 0% of the time, Pallas kernels for 5%

profile of v4, /device:TPU:7, one launch (start us, length us, event | category | flops | bytes accessed | tf_op | source)
XLA Modules:
  0.0 178.1 jit_solution(10889551875653644374)
XLA Ops:
  0.6 3.5 %collective-permute-start = (bf16[256,1792]{1,0:T(8,128)(2,1)}, bf16[256,1792]{1,0:T(8,128)(2,1)S(1)}, u32[]{:S(2)}, u32[]{:S(2)}) collective-permute-start(bf16[256,1792]{1,0:T(8,128)(2,1)} %refs_0_.5), channel_id=1, source_target_pairs={{0,32},{1,33},{2,34},{3,35},{4,36},{5,37},{6,38},{7,39},{8,40},{9,... | collective-permute-start | bytes 2752520 | tf_op jit(solution)/shard_map/ppermute | solution.py:35
  4.2 4.8 %collective-permute-start.1 = (bf16[256,1792]{1,0:T(8,128)(2,1)}, bf16[256,1792]{1,0:T(8,128)(2,1)S(1)}, u32[]{:S(2)}, u32[]{:S(2)}) collective-permute-start(bf16[256,1792]{1,0:T(8,128)(2,1)} %refs_0_.5), channel_id=1, source_target_pairs={{0,16},{1,17},{2,18},{3,19},{4,20},{5,21},{6,22},{7,23},{8,24},{9,... | collective-permute-start | bytes 2752520 | tf_op jit(solution)/shard_map/ppermute | solution.py:35
  9.0 15.3 %collective-permute-done.refs_2_ = bf16[256,1792]{1,0:T(8,128)(2,1)S(1)} collective-permute-done((bf16[256,1792]{1,0:T(8,128)(2,1)}, bf16[256,1792]{1,0:T(8,128)(2,1)S(1)}, u32[]{:S(2)}, u32[]{:S(2)}) %collective-permute-start) | collective-permute-done | bytes 917536 | tf_op jit(solution)/shard_map/ppermute | solution.py:35
  24.3 4.3 %collective-permute-done.1.refs_1_ = bf16[256,1792]{1,0:T(8,128)(2,1)S(1)} collective-permute-done((bf16[256,1792]{1,0:T(8,128)(2,1)}, bf16[256,1792]{1,0:T(8,128)(2,1)S(1)}, u32[]{:S(2)}, u32[]{:S(2)}) %collective-permute-start.1) | collective-permute-done | bytes 917536 | tf_op jit(solution)/shard_map/ppermute | solution.py:35
  28.7 1.3 collective-permute-start.2
  30.0 4.8 %collective-permute-start.3 = (bf16[256,1792]{1,0:T(8,128)(2,1)S(1)}, bf16[256,1792]{1,0:T(8,128)(2,1)S(1)}, u32[]{:S(2)}, u32[]{:S(2)}) collective-permute-start(bf16[256,1792]{1,0:T(8,128)(2,1)S(1)} %collective-permute-done.refs_2_), channel_id=1, source_target_pairs={{0,16},{1,17},{2,18},{3,19},{4,20},{5,21},{6,22},{7,23},{8,24},{9,... | collective-permute-start | bytes 2752520 | tf_op jit(solution)/shard_map/ppermute | solution.py:35
  34.8 19.8 %collective-permute-done.2.refs_5_ = bf16[256,1792]{1,0:T(8,128)(2,1)} collective-permute-done((bf16[256,1792]{1,0:T(8,128)(2,1)}, bf16[256,1792]{1,0:T(8,128)(2,1)}, u32[]{:S(2)}, u32[]{:S(2)}) %collective-permute-start.2) | collective-permute-done | bytes 917536 | tf_op jit(solution)/shard_map/ppermute | solution.py:35
  54.6 0.0 collective-permute-done.3.refs_3_
  54.6 1.3 collective-permute-start.4
  55.9 0.1 pad_add_fusion.where
  56.0 1.2 copy-done
  57.2 3.3 %block_products.3 = (f32[2,256,256]{2,1,0:T(8,128)S(1)}, f32[2,256,256]{2,1,0:T(8,128)S(1)}, f32[2,256,256]{2,1,0:T(8,128)S(1)}, f32[2,256,256]{2,1,0:T(8,128)S(1)}) custom-call(s32[4]{0:T(128)S(1)} %pad_add_fusion.where, bf16[256,1792]{1,0:T(8,128)(2,1)S(1)} %copy-done, bf16[256,1792]{1,0:T(8,128)(2,1)S(1)} %collective-permute-done.1.refs_1_, ...), custom_call_target="tpu_custom_call" | custom-call | flops 1879048192 | bytes 7602192 | tf_op jit(solution)/shard_map/block_products/pallas_call | solution.py:49
  60.5 2.5 %collective-permute-start.5 = (f32[2,256,256]{2,1,0:T(8,128)S(1)}, f32[2,256,256]{2,1,0:T(8,128)S(1)}, u32[]{:S(2)}, u32[]{:S(2)}) collective-permute-start(f32[2,256,256]{2,1,0:T(8,128)S(1)} %get-tuple-element.46), channel_id=1, source_target_pairs={{0,4},{1,5},{2,6},{3,7},{4,0},{5,1},{6,2},{7,3},{8,12},{9,13},{10,... | collective-permute-start | bytes 1572872 | tf_op jit(solution)/shard_map/ppermute | solution.py:35
  63.0 2.7 %collective-permute-start.6 = (f32[2,256,256]{2,1,0:T(8,128)S(1)}, f32[2,256,256]{2,1,0:T(8,128)S(1)}, u32[]{:S(2)}, u32[]{:S(2)}) collective-permute-start(f32[2,256,256]{2,1,0:T(8,128)S(1)} %get-tuple-element.47), channel_id=1, source_target_pairs={{0,8},{1,9},{2,10},{3,11},{4,12},{5,13},{6,14},{7,15},{8,0},{9,1},... | collective-permute-start | bytes 1572872 | tf_op jit(solution)/shard_map/ppermute | solution.py:35
  65.7 4.4 %collective-permute-start.7 = (f32[2,256,256]{2,1,0:T(8,128)S(1)}, f32[2,256,256]{2,1,0:T(8,128)S(1)}, u32[]{:S(2)}, u32[]{:S(2)}) collective-permute-start(f32[2,256,256]{2,1,0:T(8,128)S(1)} %get-tuple-element.48), channel_id=1, source_target_pairs={{0,12},{1,13},{2,14},{3,15},{4,8},{5,9},{6,10},{7,11},{8,4},{9,5},... | collective-permute-start | bytes 1572872 | tf_op jit(solution)/shard_map/ppermute | solution.py:35
  70.1 3.9 %collective-permute-done.5.second = f32[2,256,256]{2,1,0:T(8,128)S(1)} collective-permute-done((f32[2,256,256]{2,1,0:T(8,128)S(1)}, f32[2,256,256]{2,1,0:T(8,128)S(1)}, u32[]{:S(2)}, u32[]{:S(2)}) %collective-permute-start.5) | collective-permute-done | bytes 524320 | tf_op jit(solution)/shard_map/ppermute | solution.py:35
  74.0 11.5 %collective-permute-done.6.third = f32[2,256,256]{2,1,0:T(8,128)S(1)} collective-permute-done((f32[2,256,256]{2,1,0:T(8,128)S(1)}, f32[2,256,256]{2,1,0:T(8,128)S(1)}, u32[]{:S(2)}, u32[]{:S(2)}) %collective-permute-start.6) | collective-permute-done | bytes 524320 | tf_op jit(solution)/shard_map/ppermute | solution.py:35
  85.6 5.9 %collective-permute-done.7.fourth = f32[2,256,256]{2,1,0:T(8,128)S(1)} collective-permute-done((f32[2,256,256]{2,1,0:T(8,128)S(1)}, f32[2,256,256]{2,1,0:T(8,128)S(1)}, u32[]{:S(2)}, u32[]{:S(2)}) %collective-permute-start.7) | collective-permute-done | bytes 524320 | tf_op jit(solution)/shard_map/ppermute | solution.py:35
  91.5 0.0 collective-permute-done.4.refs_4_
  91.5 1.4 collective-permute-start.9
  92.9 0.7 halves.3
  93.6 2.3 %block_products.4 = (f32[1,256,256]{2,1,0:T(8,128)S(1)}, f32[1,256,256]{2,1,0:T(8,128)S(1)}, f32[1,256,256]{2,1,0:T(8,128)S(1)}, f32[1,256,256]{2,1,0:T(8,128)S(1)}) custom-call(s32[4]{0:T(128)S(1)} %pad_add_fusion.where, bf16[256,1792]{1,0:T(8,128)(2,1)S(1)} %copy-done.1, bf16[256,1792]{1,0:T(8,128)(2,1)S(1)} %collective-permute-done.1.refs_1_, ...), custom_call_target="tpu_custom_call" | custom-call | flops 939524096 | bytes 5636112 | tf_op jit(solution)/shard_map/block_products/pallas_call | solution.py:49
  96.0 1.9 %collective-permute-start.10 = (f32[1,256,256]{2,1,0:T(8,128)S(1)}, f32[1,256,256]{2,1,0:T(8,128)S(1)}, u32[]{:S(2)}, u32[]{:S(2)}) collective-permute-start(f32[1,256,256]{2,1,0:T(8,128)S(1)} %get-tuple-element.60), channel_id=1, source_target_pairs={{1,5},{3,7},{5,1},{7,3},{9,13},{11,15},{13,9},{15,11},{17,21},{19,... | collective-permute-start | bytes 786440 | tf_op jit(solution)/shard_map/ppermute | solution.py:35
  97.9 5.4 %collective-permute-start.11 = (f32[1,256,256]{2,1,0:T(8,128)S(1)}, f32[1,256,256]{2,1,0:T(8,128)S(1)}, u32[]{:S(2)}, u32[]{:S(2)}) collective-permute-start(f32[1,256,256]{2,1,0:T(8,128)S(1)} %get-tuple-element.61), channel_id=1, source_target_pairs={{1,9},{3,11},{5,13},{7,15},{9,1},{11,3},{13,5},{15,7},{17,25},{19,... | collective-permute-start | bytes 786440 | tf_op jit(solution)/shard_map/ppermute | solution.py:35
  103.3 2.2 %collective-permute-start.12 = (f32[1,256,256]{2,1,0:T(8,128)S(1)}, f32[1,256,256]{2,1,0:T(8,128)S(1)}, u32[]{:S(2)}, u32[]{:S(2)}) collective-permute-start(f32[1,256,256]{2,1,0:T(8,128)S(1)} %get-tuple-element.62), channel_id=1, source_target_pairs={{1,13},{3,15},{5,9},{7,11},{9,5},{11,7},{13,1},{15,3},{17,29},{19,... | collective-permute-start | bytes 786440 | tf_op jit(solution)/shard_map/ppermute | solution.py:35
  105.6 3.1 %collective-permute-start.8 = (f32[3,128,256]{2,1,0:T(8,128)S(1)}, f32[3,128,256]{2,1,0:T(8,128)S(1)}, u32[]{:S(2)}, u32[]{:S(2)}) collective-permute-start(f32[3,128,256]{2,1,0:T(8,128)S(1)} %get-tuple-element.57), channel_id=1, source_target_pairs={{0,2},{1,3},{2,0},{3,1},{4,6},{5,7},{6,4},{7,5},{8,10},{9,11},{10,... | collective-permute-start | bytes 1179656 | tf_op jit(solution)/shard_map/ppermute | solution.py:35
  108.7 3.0 %collective-permute-done.12.fourth = f32[1,256,256]{2,1,0:T(8,128)S(1)} collective-permute-done((f32[1,256,256]{2,1,0:T(8,128)S(1)}, f32[1,256,256]{2,1,0:T(8,128)S(1)}, u32[]{:S(2)}, u32[]{:S(2)}) %collective-permute-start.12) | collective-permute-done | bytes 262176 | tf_op jit(solution)/shard_map/ppermute | solution.py:35
  111.7 0.7 halves.4
  112.4 1.7 block_products.5
  114.1 1.9 %collective-permute-start.14 = (f32[1,256,256]{2,1,0:T(8,128)S(1)}, f32[1,256,256]{2,1,0:T(8,128)S(1)}, u32[]{:S(2)}, u32[]{:S(2)}) collective-permute-start(f32[1,256,256]{2,1,0:T(8,128)S(1)} %get-tuple-element.69), channel_id=1, source_target_pairs={{1,5},{3,7},{5,1},{7,3},{9,13},{11,15},{13,9},{15,11},{17,21},{19,... | collective-permute-start | bytes 786440 | tf_op jit(solution)/shard_map/ppermute | solution.py:35
  116.0 3.4 %collective-permute-start.15 = (f32[1,256,256]{2,1,0:T(8,128)S(1)}, f32[1,256,256]{2,1,0:T(8,128)S(1)}, u32[]{:S(2)}, u32[]{:S(2)}) collective-permute-start(f32[1,256,256]{2,1,0:T(8,128)S(1)} %get-tuple-element.70), channel_id=1, source_target_pairs={{1,9},{3,11},{5,13},{7,15},{9,1},{11,3},{13,5},{15,7},{17,25},{19,... | collective-permute-start | bytes 786440 | tf_op jit(solution)/shard_map/ppermute | solution.py:35
  119.4 4.3 %collective-permute-start.16 = (f32[1,256,256]{2,1,0:T(8,128)S(1)}, f32[1,256,256]{2,1,0:T(8,128)S(1)}, u32[]{:S(2)}, u32[]{:S(2)}) collective-permute-start(f32[1,256,256]{2,1,0:T(8,128)S(1)} %get-tuple-element.71), channel_id=1, source_target_pairs={{1,13},{3,15},{5,9},{7,11},{9,5},{11,7},{13,1},{15,3},{17,29},{19,... | collective-permute-start | bytes 786440 | tf_op jit(solution)/shard_map/ppermute | solution.py:35
  123.7 3.2 %collective-permute-start.13 = (f32[2,128,256]{2,1,0:T(8,128)S(1)}, f32[2,128,256]{2,1,0:T(8,128)S(1)}, u32[]{:S(2)}, u32[]{:S(2)}) collective-permute-start(f32[2,128,256]{2,1,0:T(8,128)S(1)} %get-tuple-element.66), channel_id=1, source_target_pairs={{1,3},{3,1},{5,7},{7,5},{9,11},{11,9},{13,15},{15,13},{17,19},{19,... | collective-permute-start | bytes 786440 | tf_op jit(solution)/shard_map/ppermute | solution.py:35
  126.9 1.9 %collective-permute-done.16.fourth = f32[1,256,256]{2,1,0:T(8,128)S(1)} collective-permute-done((f32[1,256,256]{2,1,0:T(8,128)S(1)}, f32[1,256,256]{2,1,0:T(8,128)S(1)}, u32[]{:S(2)}, u32[]{:S(2)}) %collective-permute-start.16) | collective-permute-done | bytes 262176 | tf_op jit(solution)/shard_map/ppermute | solution.py:35
  128.8 0.7 halves.5
  129.5 2.5 %collective-permute-start.17 = (f32[2,128,256]{2,1,0:T(8,128)S(1)}, f32[2,128,256]{2,1,0:T(8,128)S(1)}, u32[]{:S(2)}, u32[]{:S(2)}) collective-permute-start(f32[2,128,256]{2,1,0:T(8,128)S(1)} %get-tuple-element.73), channel_id=1, source_target_pairs={{1,3},{3,1},{5,7},{7,5},{9,11},{11,9},{13,15},{15,13},{17,19},{19,... | collective-permute-start | bytes 786440 | tf_op jit(solution)/shard_map/ppermute | solution.py:35
  132.0 0.1 fusion.2
  132.1 1.3 collective-permute-start.18
  133.4 1.3 collective-permute-start.19
  134.7 1.9 %collective-permute-done.17 = f32[2,128,256]{2,1,0:T(8,128)S(1)} collective-permute-done((f32[2,128,256]{2,1,0:T(8,128)S(1)}, f32[2,128,256]{2,1,0:T(8,128)S(1)}, u32[]{:S(2)}, u32[]{:S(2)}) %collective-permute-start.17) | collective-permute-done | bytes 262176 | tf_op jit(solution)/shard_map/ppermute | solution.py:35
  136.7 1.3 collective-permute-start.20
  138.0 1.9 %collective-permute-done.20.refs_6_ = f32[128,256]{1,0:T(8,128)S(1)} collective-permute-done((f32[128,256]{1,0:T(8,128)S(1)}, f32[128,256]{1,0:T(8,128)S(1)}, u32[]{:S(2)}, u32[]{:S(2)}) %collective-permute-start.20) | collective-permute-done | bytes 131104 | tf_op jit(solution)/shard_map/ppermute | solution.py:35
  139.9 0.6 strips.1
  140.5 33.9 %collective-permute-start.21 = (f32[4,64,256]{2,1,0:T(8,128)S(1)}, f32[4,64,256]{2,1,0:T(8,128)S(1)}, u32[]{:S(2)}, u32[]{:S(2)}) collective-permute-start(f32[4,64,256]{2,1,0:T(8,128)S(1)} %get-tuple-element.75), channel_id=1, source_target_pairs={{0,1},{1,0},{2,3},{3,2},{4,5},{5,4},{6,7},{7,6},{8,9},{9,8},{10,11... | collective-permute-start | bytes 786440 | tf_op jit(solution)/shard_map/ppermute | solution.py:35
  174.4 0.1 copy.5
  174.5 1.0 collective-permute-done.21.other
  175.6 1.9 %refresh.1 = (bf16[64,1024]{1,0:T(8,128)(2,1)}, f32[64,8]{1,0:T(8,128)S(1)}) custom-call(s32[4]{0:T(128)S(1)} %pad_add_fusion.where, f32[4,64,256]{2,1,0:T(8,128)S(1)} %get-tuple-element.74.mine, f32[4,64,256]{2,1,0:T(8,128)S(1)} %collective-permute-done.21.other, bf16[64,1024]{1,0:T(8,128)(2,1)S(1)} %bitcast.23, f32[64,8]{1,0:T(8,128)S(1)} %bitcast.22), custom_call_target="tpu_custom_call" | custom-call | flops 16777216 | bytes 790544 | tf_op jit(solution)/shard_map/refresh/pallas_call | solution.py:49
  177.4 0.7 copy.6
  (18 shorter events, 0.1 us)
Async XLA Ops:
  0.6 23.7 %collective-permute-start = (bf16[256,1792]{1,0:T(8,128)(2,1)}, bf16[256,1792]{1,0:T(8,128)(2,1)S(1)}, u32[]{:S(2)}, u32[]{:S(2)}) collective-permute-start(bf16[256,1792]{1,0:T(8,128)(2,1)} %refs_0_.5), channel_id=1, source_target_pairs={{0,32},{1,33},{2,34},{3,35},{4,36},{5,37},{6,38},{7,39},{8,40},{9,... | collective-permute-start | bytes 2752520 | tf_op jit(solution)/shard_map/ppermute | solution.py:35
  4.2 24.5 %collective-permute-start.1 = (bf16[256,1792]{1,0:T(8,128)(2,1)}, bf16[256,1792]{1,0:T(8,128)(2,1)S(1)}, u32[]{:S(2)}, u32[]{:S(2)}) collective-permute-start(bf16[256,1792]{1,0:T(8,128)(2,1)} %refs_0_.5), channel_id=1, source_target_pairs={{0,16},{1,17},{2,18},{3,19},{4,20},{5,21},{6,22},{7,23},{8,24},{9,... | collective-permute-start | bytes 2752520 | tf_op jit(solution)/shard_map/ppermute | solution.py:35
  28.7 25.9 %collective-permute-start.2 = (bf16[256,1792]{1,0:T(8,128)(2,1)}, bf16[256,1792]{1,0:T(8,128)(2,1)}, u32[]{:S(2)}, u32[]{:S(2)}) collective-permute-start(bf16[256,1792]{1,0:T(8,128)(2,1)} %refs_0_.5), channel_id=1, source_target_pairs={{0,64},{2,66},{4,68},{6,70},{8,72},{10,74},{12,76},{14,78},{16,80}... | collective-permute-start | bytes 2752520 | tf_op jit(solution)/shard_map/ppermute | solution.py:35
  30.0 24.7 %collective-permute-start.3 = (bf16[256,1792]{1,0:T(8,128)(2,1)S(1)}, bf16[256,1792]{1,0:T(8,128)(2,1)S(1)}, u32[]{:S(2)}, u32[]{:S(2)}) collective-permute-start(bf16[256,1792]{1,0:T(8,128)(2,1)S(1)} %collective-permute-done.refs_2_), channel_id=1, source_target_pairs={{0,16},{1,17},{2,18},{3,19},{4,20},{5,21},{6,22},{7,23},{8,24},{9,... | collective-permute-start | bytes 2752520 | tf_op jit(solution)/shard_map/ppermute | solution.py:35
  54.6 36.8 %collective-permute-start.4 = (bf16[256,1792]{1,0:T(8,128)(2,1)}, bf16[256,1792]{1,0:T(8,128)(2,1)}, u32[]{:S(2)}, u32[]{:S(2)}) collective-permute-start(bf16[256,1792]{1,0:T(8,128)(2,1)} %collective-permute-done.2.refs_5_), channel_id=1, source_target_pairs={{64,128},{65,1},{66,130},{67,3},{68,132},{69,5},{70,134},{71,7},{7... | collective-permute-start | bytes 2752520 | tf_op jit(solution)/shard_map/ppermute | solution.py:35
  56.0 1.2 copy-start
  60.5 13.5 %collective-permute-start.5 = (f32[2,256,256]{2,1,0:T(8,128)S(1)}, f32[2,256,256]{2,1,0:T(8,128)S(1)}, u32[]{:S(2)}, u32[]{:S(2)}) collective-permute-start(f32[2,256,256]{2,1,0:T(8,128)S(1)} %get-tuple-element.46), channel_id=1, source_target_pairs={{0,4},{1,5},{2,6},{3,7},{4,0},{5,1},{6,2},{7,3},{8,12},{9,13},{10,... | collective-permute-start | bytes 1572872 | tf_op jit(solution)/shard_map/ppermute | solution.py:35
  63.0 22.6 %collective-permute-start.6 = (f32[2,256,256]{2,1,0:T(8,128)S(1)}, f32[2,256,256]{2,1,0:T(8,128)S(1)}, u32[]{:S(2)}, u32[]{:S(2)}) collective-permute-start(f32[2,256,256]{2,1,0:T(8,128)S(1)} %get-tuple-element.47), channel_id=1, source_target_pairs={{0,8},{1,9},{2,10},{3,11},{4,12},{5,13},{6,14},{7,15},{8,0},{9,1},... | collective-permute-start | bytes 1572872 | tf_op jit(solution)/shard_map/ppermute | solution.py:35
  65.7 25.7 %collective-permute-start.7 = (f32[2,256,256]{2,1,0:T(8,128)S(1)}, f32[2,256,256]{2,1,0:T(8,128)S(1)}, u32[]{:S(2)}, u32[]{:S(2)}) collective-permute-start(f32[2,256,256]{2,1,0:T(8,128)S(1)} %get-tuple-element.48), channel_id=1, source_target_pairs={{0,12},{1,13},{2,14},{3,15},{4,8},{5,9},{6,10},{7,11},{8,4},{9,5},... | collective-permute-start | bytes 1572872 | tf_op jit(solution)/shard_map/ppermute | solution.py:35
  91.5 2.1 %copy-start.1 = (bf16[256,1792]{1,0:T(8,128)(2,1)S(1)}, bf16[256,1792]{1,0:T(8,128)(2,1)}, u32[]{:S(2)}) copy-start(bf16[256,1792]{1,0:T(8,128)(2,1)} %refs_0_.5) | copy-start | bytes 2752516
  91.5 20.9 %collective-permute-start.9 = (bf16[256,1792]{1,0:T(8,128)(2,1)}, bf16[256,1792]{1,0:T(8,128)(2,1)S(1)}, u32[]{:S(2)}, u32[]{:S(2)}) collective-permute-start(bf16[256,1792]{1,0:T(8,128)(2,1)} %collective-permute-done.4.refs_4_), channel_id=1, source_target_pairs={{65,1},{67,3},{69,5},{71,7},{73,9},{75,11},{77,13},{79,15},{81,17}... | collective-permute-start | bytes 2752520 | tf_op jit(solution)/shard_map/ppermute | solution.py:35
  96.0 12.7 %collective-permute-start.10 = (f32[1,256,256]{2,1,0:T(8,128)S(1)}, f32[1,256,256]{2,1,0:T(8,128)S(1)}, u32[]{:S(2)}, u32[]{:S(2)}) collective-permute-start(f32[1,256,256]{2,1,0:T(8,128)S(1)} %get-tuple-element.60), channel_id=1, source_target_pairs={{1,5},{3,7},{5,1},{7,3},{9,13},{11,15},{13,9},{15,11},{17,21},{19,... | collective-permute-start | bytes 786440 | tf_op jit(solution)/shard_map/ppermute | solution.py:35
  97.9 10.8 %collective-permute-start.11 = (f32[1,256,256]{2,1,0:T(8,128)S(1)}, f32[1,256,256]{2,1,0:T(8,128)S(1)}, u32[]{:S(2)}, u32[]{:S(2)}) collective-permute-start(f32[1,256,256]{2,1,0:T(8,128)S(1)} %get-tuple-element.61), channel_id=1, source_target_pairs={{1,9},{3,11},{5,13},{7,15},{9,1},{11,3},{13,5},{15,7},{17,25},{19,... | collective-permute-start | bytes 786440 | tf_op jit(solution)/shard_map/ppermute | solution.py:35
  103.3 8.3 %collective-permute-start.12 = (f32[1,256,256]{2,1,0:T(8,128)S(1)}, f32[1,256,256]{2,1,0:T(8,128)S(1)}, u32[]{:S(2)}, u32[]{:S(2)}) collective-permute-start(f32[1,256,256]{2,1,0:T(8,128)S(1)} %get-tuple-element.62), channel_id=1, source_target_pairs={{1,13},{3,15},{5,9},{7,11},{9,5},{11,7},{13,1},{15,3},{17,29},{19,... | collective-permute-start | bytes 786440 | tf_op jit(solution)/shard_map/ppermute | solution.py:35
  105.6 26.4 %collective-permute-start.8 = (f32[3,128,256]{2,1,0:T(8,128)S(1)}, f32[3,128,256]{2,1,0:T(8,128)S(1)}, u32[]{:S(2)}, u32[]{:S(2)}) collective-permute-start(f32[3,128,256]{2,1,0:T(8,128)S(1)} %get-tuple-element.57), channel_id=1, source_target_pairs={{0,2},{1,3},{2,0},{3,1},{4,6},{5,7},{6,4},{7,5},{8,10},{9,11},{10,... | collective-permute-start | bytes 1179656 | tf_op jit(solution)/shard_map/ppermute | solution.py:35
  114.1 12.8 %collective-permute-start.14 = (f32[1,256,256]{2,1,0:T(8,128)S(1)}, f32[1,256,256]{2,1,0:T(8,128)S(1)}, u32[]{:S(2)}, u32[]{:S(2)}) collective-permute-start(f32[1,256,256]{2,1,0:T(8,128)S(1)} %get-tuple-element.69), channel_id=1, source_target_pairs={{1,5},{3,7},{5,1},{7,3},{9,13},{11,15},{13,9},{15,11},{17,21},{19,... | collective-permute-start | bytes 786440 | tf_op jit(solution)/shard_map/ppermute | solution.py:35
  116.0 10.9 %collective-permute-start.15 = (f32[1,256,256]{2,1,0:T(8,128)S(1)}, f32[1,256,256]{2,1,0:T(8,128)S(1)}, u32[]{:S(2)}, u32[]{:S(2)}) collective-permute-start(f32[1,256,256]{2,1,0:T(8,128)S(1)} %get-tuple-element.70), channel_id=1, source_target_pairs={{1,9},{3,11},{5,13},{7,15},{9,1},{11,3},{13,5},{15,7},{17,25},{19,... | collective-permute-start | bytes 786440 | tf_op jit(solution)/shard_map/ppermute | solution.py:35
  119.4 9.4 %collective-permute-start.16 = (f32[1,256,256]{2,1,0:T(8,128)S(1)}, f32[1,256,256]{2,1,0:T(8,128)S(1)}, u32[]{:S(2)}, u32[]{:S(2)}) collective-permute-start(f32[1,256,256]{2,1,0:T(8,128)S(1)} %get-tuple-element.71), channel_id=1, source_target_pairs={{1,13},{3,15},{5,9},{7,11},{9,5},{11,7},{13,1},{15,3},{17,29},{19,... | collective-permute-start | bytes 786440 | tf_op jit(solution)/shard_map/ppermute | solution.py:35
  123.7 9.7 %collective-permute-start.13 = (f32[2,128,256]{2,1,0:T(8,128)S(1)}, f32[2,128,256]{2,1,0:T(8,128)S(1)}, u32[]{:S(2)}, u32[]{:S(2)}) collective-permute-start(f32[2,128,256]{2,1,0:T(8,128)S(1)} %get-tuple-element.66), channel_id=1, source_target_pairs={{1,3},{3,1},{5,7},{7,5},{9,11},{11,9},{13,15},{15,13},{17,19},{19,... | collective-permute-start | bytes 786440 | tf_op jit(solution)/shard_map/ppermute | solution.py:35
  129.5 7.1 %collective-permute-start.17 = (f32[2,128,256]{2,1,0:T(8,128)S(1)}, f32[2,128,256]{2,1,0:T(8,128)S(1)}, u32[]{:S(2)}, u32[]{:S(2)}) collective-permute-start(f32[2,128,256]{2,1,0:T(8,128)S(1)} %get-tuple-element.73), channel_id=1, source_target_pairs={{1,3},{3,1},{5,7},{7,5},{9,11},{11,9},{13,15},{15,13},{17,19},{19,... | collective-permute-start | bytes 786440 | tf_op jit(solution)/shard_map/ppermute | solution.py:35
  132.1 5.9 %collective-permute-start.18 = (f32[128,256]{1,0:T(8,128)S(1)}, f32[128,256]{1,0:T(8,128)S(1)}, u32[]{:S(2)}, u32[]{:S(2)}) collective-permute-start(f32[128,256]{1,0:T(8,128)S(1)} %get-tuple-element.80), channel_id=1, source_target_pairs={{1,65},{3,67},{5,81},{7,83},{9,97},{11,99},{13,113},{15,115},{17,6... | collective-permute-start | bytes 393224 | tf_op jit(solution)/shard_map/ppermute | solution.py:35
  133.4 4.6 %collective-permute-start.19 = (f32[128,256]{1,0:T(8,128)S(1)}, f32[128,256]{1,0:T(8,128)S(1)}, u32[]{:S(2)}, u32[]{:S(2)}) collective-permute-start(f32[128,256]{1,0:T(8,128)S(1)} %get-tuple-element.85), channel_id=1, source_target_pairs={{1,129},{3,131},{5,145},{7,147},{9,161},{11,163},{13,177},{15,179}... | collective-permute-start | bytes 393224 | tf_op jit(solution)/shard_map/ppermute | solution.py:35
  136.7 3.2 %collective-permute-start.20 = (f32[128,256]{1,0:T(8,128)S(1)}, f32[128,256]{1,0:T(8,128)S(1)}, u32[]{:S(2)}, u32[]{:S(2)}) collective-permute-start(f32[128,256]{1,0:T(8,128)S(1)} %get-tuple-element.83), channel_id=1, source_target_pairs={{1,193},{3,195},{5,209},{7,211},{9,225},{11,227},{13,241},{15,243}... | collective-permute-start | bytes 393224 | tf_op jit(solution)/shard_map/ppermute | solution.py:35
  139.9 34.5 %copy-start.3 = (f32[1,64,8]{1,2,0:T(8,128)S(1)}, f32[1,64,8]{1,2,0:T(8,128)}, u32[]{:S(2)}) copy-start(f32[1,64,8]{1,2,0:T(8,128)} %param.5) | copy-start | bytes 6148
  139.9 35.6 %copy-start.2 = (bf16[1,64,1024]{2,1,0:T(8,128)(2,1)S(1)}, bf16[1,64,1024]{2,1,0:T(8,128)(2,1)}, u32[]{:S(2)}) copy-start(bf16[1,64,1024]{2,1,0:T(8,128)(2,1)} %param.4) | copy-start | bytes 393220
  140.5 35.0 %collective-permute-start.21 = (f32[4,64,256]{2,1,0:T(8,128)S(1)}, f32[4,64,256]{2,1,0:T(8,128)S(1)}, u32[]{:S(2)}, u32[]{:S(2)}) collective-permute-start(f32[4,64,256]{2,1,0:T(8,128)S(1)} %get-tuple-element.75), channel_id=1, source_target_pairs={{0,1},{1,0},{2,3},{3,2},{4,5},{5,4},{6,7},{7,6},{8,9},{9,8},{10,11... | collective-permute-start | bytes 786440 | tf_op jit(solution)/shard_map/ppermute | solution.py:35

commit v5 on v4

v5 whole, which is shorter than its diff:
```python
import functools

import jax
import jax.numpy as jnp
from jax import lax
from jax.experimental import pallas as pl
from jax.experimental.pallas import tpu as pltpu
from jax.sharding import PartitionSpec as P

GROUP = 128
AXES = ("dp", "tensor")
SUPERS = 4
VMEM = pl.BlockSpec(memory_space=pltpu.VMEM)
SMEM = pl.BlockSpec(memory_space=pltpu.SMEM)


def place(index):
    dp, tensor = divmod(index, 16)
    return dict(
        b=dp >> 4, g=(dp >> 2) & 3, h=dp & 3, x=tensor >> 2, yl=(tensor >> 1) & 1, c=tensor & 1
    )


def index_of(b, g, h, x, yl, c):
    return ((b << 4 | g << 2 | h) << 4) | x << 2 | yl << 1 | c


def permute(array, target, keep=lambda at: True):
    total = lax.axis_size("dp") * lax.axis_size("tensor")
    pairs = []
    for i in range(total):
        at = place(i)
        if keep(at):
            pairs.append((i, index_of(**{**at, **target(at)})))
    return lax.ppermute(array, AXES, pairs)


def way(at):
    return 1 if at["c"] == 0 else -1


def reach(at):
    return at["g"] if at["c"] == 0 else SUPERS - 1 - at["g"]


def rank(at):
    z = at["g"] * 2 + (at["h"] >> 1)
    return z if at["c"] == 0 else 2 * SUPERS - 1 - z


def along(at, hops):
    z = at["g"] * 2 + (at["h"] >> 1) + way(at) * hops
    return dict(g=z >> 1, h=(z & 1) << 1 | at["h"] & 1)


def call(kernel, name, outs, flops, *operands, scratch=()):
    in_specs = [SMEM if op.dtype == jnp.int32 else VMEM for op in operands]
    moved = sum(op.size * op.dtype.itemsize for op in (*operands, *outs))
    return pl.pallas_call(
        kernel,
        out_shape=outs,
        in_specs=in_specs,
        out_specs=[VMEM] * len(outs),
        scratch_shapes=list(scratch),
        compiler_params=pltpu.CompilerParams(vmem_limit_bytes=40 * 1024 * 1024),
        cost_estimate=pl.CostEstimate(flops=flops, bytes_accessed=moved, transcendentals=0),
        name=name,
    )(*operands)


def floats(*shape):
    return jax.ShapeDtypeStruct(shape, jnp.float32)


def products_kernel(plan, where, *refs):
    count = len(plan)
    ins, outs, other = refs[:-5], refs[-5:-1], refs[-1]
    for k, (_, _, near, far) in enumerate(plan):
        for flag, number in ((0, near), (1, far)):

            @pl.when(where[1] == flag)
            def _(k=k, number=number):
                other[k] = jnp.zeros_like(other[k]) if number is None else ins[number][...]

    for turn in range(4):

        @pl.when(where[0] == turn)
        def _(turn=turn):
            for d in range(4):
                v = d ^ turn
                for k, (pair, equal, _, _) in enumerate(plan):
                    outs[d][k] = lax.dot_general(
                        ins[pair[v & 1]][...],
                        other[k] if v >> 1 else ins[equal][...],
                        (((1,), (1,)), ((), ())),
                        preferred_element_type=jnp.float32,
                    )


def products(where, plan, blocks):
    size, depth = blocks[0].shape
    count = len(plan)
    return list(
        call(
            functools.partial(products_kernel, plan),
            "block_products",
            [floats(count, size, size)] * 4,
            8 * count * size * size * depth,
            where,
            *blocks,
            scratch=[pltpu.VMEM((count, size, depth), jnp.bfloat16)],
        )
    )


def halves_kernel(where, first, second, third, fourth, keep, give):
    count, size, _ = first.shape
    half = size // 2
    upper = where[2] == 1
    totals = [first[k] + second[k] + third[k] + fourth[k] for k in range(count)]
    for k, total in enumerate(totals + [total.T for total in totals]):
        keep[k] = jnp.where(upper, total[half:], total[:half])
        give[k] = jnp.where(upper, total[:half], total[half:])


def halves(where, parts):
    count, size, _ = parts[0].shape
    shape = floats(2 * count, size // 2, size)
    return call(halves_kernel, "halves", [shape, shape], 0, where, *parts)


def strips_kernel(where, *refs):
    here, there, across, keep, give = refs[:3], refs[3:7], refs[7:11], refs[11], refs[12]
    half = keep.shape[1]
    stays, second = where[5] == 1, where[3] == 1
    own = [jnp.where(stays, here[k][...], there[k][...]) for k in range(3)] + [there[3][...]]
    back = own[3] + across[1][...], own[1] + across[3][...]
    strips = [
        own[0] + across[0][...],
        jnp.where(second, back[1], back[0]),
        own[2] + across[2][...],
        jnp.where(second, back[0], back[1]),
    ]
    for k, strip in enumerate(strips):
        keep[k] = jnp.where(second, strip[half:], strip[:half])
        give[k] = jnp.where(second, strip[:half], strip[half:])


def strips(where, here, there, across):
    rows, cols = here[0].shape
    shape = floats(SUPERS, rows // 2, cols)
    return call(strips_kernel, "strips", [shape, shape], 0, where, *here, *there, *across)


def refresh_kernel(where, mine, other, codes, scales, new_codes, new_scales):
    bits = lax.broadcasted_iota(jnp.int32, (GROUP, GROUP), 0) & lax.broadcasted_iota(
        jnp.int32, (GROUP, GROUP), 1
    )
    for shift in (4, 2, 1):
        bits = bits ^ (bits >> shift)
    signs = 1.0 - 2.0 * (bits & 1).astype(jnp.float32)
    unit = 1.0 / (GROUP**0.5)
    per_block = mine.shape[2] // GROUP
    largest = []
    for j in range(SUPERS):
        offset = (j + SUPERS - where[4]) & (SUPERS - 1)
        block = mine[offset] + other[offset]
        for k in range(per_block):
            group = j * per_block + k
            at = slice(group * GROUP, (group + 1) * GROUP)
            turned = jnp.dot(
                block[:, k * GROUP : (k + 1) * GROUP],
                signs,
                precision=lax.Precision.HIGHEST,
                preferred_element_type=jnp.float32,
            )
            old = codes[:, at].astype(jnp.float32) * scales[:, group : group + 1]
            rotated = 0.95 * old + 0.05 * (turned * unit)
            peak = jnp.max(jnp.abs(rotated), axis=1, keepdims=True)
            new_codes[:, at] = (rotated / (peak + 1e-06)).astype(jnp.bfloat16)
            largest.append(peak)
    new_scales[...] = jnp.concatenate(largest, axis=1)


def refresh(where, mine, other, codes, scales):
    return call(
        refresh_kernel,
        "refresh",
        [
            jax.ShapeDtypeStruct(codes.shape, jnp.bfloat16),
            jax.ShapeDtypeStruct(scales.shape, jnp.float32),
        ],
        2 * codes.size * GROUP,
        where,
        mine,
        other,
        codes,
        scales,
    )


def step_on(block, step):
    def needed(at):
        to = rank(at) + 1
        return to < 2 * SUPERS and step <= to and (step < 5 or to & 1 == 1)

    return permute(block, lambda at: along(at, 1), needed)


def per_device(gradient, left_codes, left_scales):
    dp, tensor = lax.axis_index("dp"), lax.axis_index("tensor")
    turn = (tensor >> 2) ^ (dp & 3)
    core = tensor & 1
    where = jnp.stack(
        [
            turn,
            ((dp >> 1) & 1) ^ core,
            (tensor >> 1) & 1,
            core,
            (dp >> 2) & 3,
            1 - (turn >> 1),
        ]
    ).astype(jnp.int32)

    y_swap = lambda at: dict(h=at["h"] ^ 1)
    y_block = permute(gradient, y_swap)
    passing = [gradient, step_on(gradient, 1)]
    start, passing[1] = lax.optimization_barrier((gradient, passing[1]))
    end_block = permute(start, lambda at: along(at, -2), lambda at: rank(at) >= 6)
    end_y_block = permute(end_block, y_swap, lambda at: rank(at) in (4, 5))
    passing.append(step_on(passing[1], 2))
    passing[2], y_block = lax.optimization_barrier((passing[2], y_block))
    passing.append(step_on(passing[2], 3))
    passing[3], end_block = lax.optimization_barrier((passing[3], end_block))
    passing.append(step_on(passing[3], 4))

    def summed(plan, blocks, valid):
        parts = products(where, plan, blocks)
        parts[1:] = [
            permute(parts[d], lambda at, d=d: dict(x=at["x"] ^ d), valid) for d in (1, 2, 3)
        ]
        return parts

    def settled(parts, valid):
        keep, give = halves(where, parts)
        came = permute(give, lambda at: dict(yl=at["yl"] ^ 1), valid)
        return keep, came

    def home(at):
        z0, y, xh, xl = at["h"] >> 1, at["h"] & 1, at["x"] >> 1, at["x"] & 1
        return dict(h=xh << 1 | y, x=z0 << 1 | xl)

    def flip(at):
        z0, y, xh, xl = at["h"] >> 1, at["h"] & 1, at["x"] >> 1, at["x"] & 1
        return dict(h=z0 << 1 | xl, x=xh << 1 | y)

    moves = lambda at: (at["h"] >> 1) != (at["x"] >> 1)
    own_here, own_there, across = [None] * 3, [None] * SUPERS, [None] * SUPERS

    near = lambda at: True
    blocks = [gradient, y_block, *passing[1:4]]
    first = summed([((0, 1), 0, None, 2), ((0, 1), 3, 2, 4)], blocks, near)
    passing[4], first[1] = lax.optimization_barrier((passing[4], first[1]))
    passing.append(step_on(passing[4], 5))
    keep, came = settled(first, near)
    for k in (0, 1):
        own_here[k] = keep[k] + came[k]
        own_there[k] = permute(own_here[k], home, moves)
        across[k] = permute(
            keep[2 + k] + came[2 + k],
            lambda at, k=k: dict(g=at["g"] - k * way(at), **flip(at)),
            lambda at, k=k: reach(at) >= k and (k > 0 or moves(at) and rank(at) & 1 == 1),
        )

    far = lambda at: reach(at) >= 2
    blocks = [gradient, y_block, end_block, end_y_block, *passing[3:]]
    second = summed([((0, 1), 5, 4, 6), ((2, 3), 5, 4, 6)], blocks, far)
    keep, came = settled(second, far)
    own_here[2] = keep[0] + came[0]
    own_there[2] = permute(own_here[2], home, lambda at: far(at) and moves(at))
    across[2] = permute(
        keep[2] + came[2], lambda at: dict(g=at["g"] - 2 * way(at), **flip(at)), far
    )
    met = lambda at: reach(at) == 2
    own_there[3] = permute(
        keep[1] + came[1], lambda at: dict(g=at["g"] + way(at), **home(at)), met
    )
    across[3] = permute(
        keep[3] + came[3], lambda at: dict(g=at["g"] - 2 * way(at), **flip(at)), met
    )

    mine, given = strips(where, own_here, own_there, across)
    other = permute(given, lambda at: dict(c=at["c"] ^ 1))
    fresh_codes, fresh_scales = refresh(where, mine, other, left_codes[0], left_scales[0])
    return fresh_codes[None], fresh_scales[None]


def solution(mesh):
    return jax.shard_map(
        per_device,
        mesh=mesh,
        in_specs=(P("dp", "tensor"), P("dp", "tensor", None), P("dp", "tensor", None)),
        out_specs=(P("dp", "tensor", None), P("dp", "tensor", None)),
        check_vma=False,
    )
```

time: 179 us -> 175 us (0.978)
  waiting for transfers between devices: 70.6 us -> 63.3 us
  local copies, waits for them, and re-layouts: 1.94 us -> 6.23 us
    ppermute x22 -> x25, waiting for transfers between devices: 70.6 us -> 63.3 us  [permute(): return lax.ppermute(array, AXES, pairs)]
    unnamed x10 -> x16, local copies, waits for them, and re-layouts: 1.94 us -> 6.15 us
    pallas_call x8 -> x6, Pallas kernels: 11.9 us -> 10.4 us  [call(): pl.pallas_call(kernel, out_shape=outs, in_specs=in_specs, out_specs=[VMEM...]
    ppermute x22 -> x25, starting transfers between devices: 92.5 us -> 92.1 us  [permute(): return lax.ppermute(array, AXES, pairs)]
  transfers between devices with their start and end apart: 22 -> 25, of which waited for: 11 -> 12; matrix products, arithmetic and copies ran while one was open for 0% -> 0% of each run, Pallas kernels for 5% -> 5%
where the time goes in v5:
time: 175 us; the launch traced here: 173 us
  starting transfers between devices  92.1 us (53%)
  waiting for transfers between devices  63.3 us (36%)
  Pallas kernels  10.4 us (6%)
  local copies, waits for them, and re-layouts  6.23 us (4%)
    ppermute x25, starting transfers between devices, permute(): return lax.ppermute(array, AXES, pairs)  92.1 us
    ppermute x25, waiting for transfers between devices, permute(): return lax.ppermute(array, AXES, pairs)  63.3 us
    pallas_call x6, Pallas kernels, call(): pl.pallas_call(kernel, out_shape=outs, in_specs=in_specs, out_specs=[VMEM...  10.4 us
    unnamed x16, local copies, waits for them, and re-layouts  6.15 us
  transfers between devices with their start and end apart: 25, of which 12 were waited for; matrix products, arithmetic and copies ran while one was open for 0% of the time, Pallas kernels for 5%

profile of v5, /device:TPU:7, one launch (start us, length us, event | category | flops | bytes accessed | tf_op | source)
XLA Modules:
  0.0 173.1 jit_solution(6296253878660876866)
XLA Ops:
  0.6 1.3 collective-permute-start
  1.9 4.8 %collective-permute-start.2 = (bf16[256,1792]{1,0:T(8,128)(2,1)}, bf16[256,1792]{1,0:T(8,128)(2,1)S(1)}, u32[]{:S(2)}, u32[]{:S(2)}) collective-permute-start(bf16[256,1792]{1,0:T(8,128)(2,1)} %refs_0_.3), channel_id=1, source_target_pairs={{0,16},{1,17},{2,18},{3,19},{4,20},{5,21},{6,22},{7,23},{8,24},{9,... | collective-permute-start | bytes 2752520 | tf_op jit(solution)/shard_map/ppermute | solution.py:35
  6.8 8.7 %collective-permute-done.refs_2_ = bf16[256,1792]{1,0:T(8,128)(2,1)S(1)} collective-permute-done((bf16[256,1792]{1,0:T(8,128)(2,1)}, bf16[256,1792]{1,0:T(8,128)(2,1)S(1)}, u32[]{:S(2)}, u32[]{:S(2)}) %collective-permute-start) | collective-permute-done | bytes 917536 | tf_op jit(solution)/shard_map/ppermute | solution.py:35
  15.5 1.3 collective-permute-start.1
  16.8 0.9 copy-done.2
  17.7 5.6 %collective-permute-start.4 = (bf16[256,1792]{1,0:T(8,128)(2,1)}, bf16[256,1792]{1,0:T(8,128)(2,1)S(1)}, u32[]{:S(2)}, u32[]{:S(2)}) collective-permute-start(bf16[256,1792]{1,0:T(8,128)(2,1)} %refs_0_.3), channel_id=1, source_target_pairs={{1,65},{3,67},{5,69},{7,71},{9,73},{11,75},{13,77},{15,79},{17,81}... | collective-permute-start | bytes 2752520 | tf_op jit(solution)/shard_map/ppermute | solution.py:35
  23.3 0.8 collective-permute-done.2.refs_1_
  24.1 5.6 %collective-permute-done.1.refs_3_ = bf16[256,1792]{1,0:T(8,128)(2,1)S(1)} collective-permute-done((bf16[256,1792]{1,0:T(8,128)(2,1)S(1)}, bf16[256,1792]{1,0:T(8,128)(2,1)S(1)}, u32[]{:S(2)}, u32[]{:S(2)}) %collective-permute-start.1) | collective-permute-done | bytes 917536 | tf_op jit(solution)/shard_map/ppermute | solution.py:35
  29.8 1.3 collective-permute-start.3
  31.1 0.9 copy-done.4
  32.0 1.9 %collective-permute-done.4.refs_2_ = bf16[256,1792]{1,0:T(8,128)(2,1)S(1)} collective-permute-done((bf16[256,1792]{1,0:T(8,128)(2,1)}, bf16[256,1792]{1,0:T(8,128)(2,1)S(1)}, u32[]{:S(2)}, u32[]{:S(2)}) %collective-permute-start.4) | collective-permute-done | bytes 917536 | tf_op jit(solution)/shard_map/ppermute | solution.py:35
  33.9 10.5 %collective-permute-done.3.refs_4_ = bf16[256,1792]{1,0:T(8,128)(2,1)S(1)} collective-permute-done((bf16[256,1792]{1,0:T(8,128)(2,1)S(1)}, bf16[256,1792]{1,0:T(8,128)(2,1)S(1)}, u32[]{:S(2)}, u32[]{:S(2)}) %collective-permute-start.3) | collective-permute-done | bytes 917536 | tf_op jit(solution)/shard_map/ppermute | solution.py:35
  44.4 1.3 collective-permute-start.5
  45.8 1.2 copy-done.1
  46.9 1.2 copy-done.3
  48.1 1.2 copy-done.5
  49.3 2.8 %block_products.2 = (f32[2,256,256]{2,1,0:T(8,128)S(1)}, f32[2,256,256]{2,1,0:T(8,128)S(1)}, f32[2,256,256]{2,1,0:T(8,128)S(1)}, f32[2,256,256]{2,1,0:T(8,128)S(1)}) custom-call(s32[6]{0:T(128)S(1)} %stack.27.where, bf16[256,1792]{1,0:T(8,128)(2,1)S(1)} %copy-done.1, bf16[256,1792]{1,0:T(8,128)(2,1)S(1)} %collective-permute-done.2.refs_1_, ...), custom_call_target="tpu_custom_call" | custom-call | flops 1879048192 | bytes 6684696 | tf_op jit(solution)/shard_map/block_products/pallas_call | solution.py:59
  52.1 2.5 %collective-permute-start.6 = (f32[2,256,256]{2,1,0:T(8,128)S(1)}, f32[2,256,256]{2,1,0:T(8,128)S(1)}, u32[]{:S(2)}, u32[]{:S(2)}) collective-permute-start(f32[2,256,256]{2,1,0:T(8,128)S(1)} %get-tuple-element.32), channel_id=1, source_target_pairs={{0,4},{1,5},{2,6},{3,7},{4,0},{5,1},{6,2},{7,3},{8,12},{9,13},{10,... | collective-permute-start | bytes 1572872 | tf_op jit(solution)/shard_map/ppermute | solution.py:35
  54.6 0.7 collective-permute-start.10
  55.3 10.1 %collective-permute-done.6.second = f32[2,256,256]{2,1,0:T(8,128)S(1)} collective-permute-done((f32[2,256,256]{2,1,0:T(8,128)S(1)}, f32[2,256,256]{2,1,0:T(8,128)S(1)}, u32[]{:S(2)}, u32[]{:S(2)}) %collective-permute-start.6) | collective-permute-done | bytes 524320 | tf_op jit(solution)/shard_map/ppermute | solution.py:35
  65.5 1.3 collective-permute-start.11
  66.8 5.1 %collective-permute-start.7 = (f32[2,256,256]{2,1,0:T(8,128)S(1)}, f32[2,256,256]{2,1,0:T(8,128)S(1)}, u32[]{:S(2)}, u32[]{:S(2)}) collective-permute-start(f32[2,256,256]{2,1,0:T(8,128)S(1)} %get-tuple-element.34), channel_id=1, source_target_pairs={{0,8},{1,9},{2,10},{3,11},{4,12},{5,13},{6,14},{7,15},{8,0},{9,1},... | collective-permute-start | bytes 1572872 | tf_op jit(solution)/shard_map/ppermute | solution.py:35
  71.9 2.8 %collective-permute-start.8 = (f32[2,256,256]{2,1,0:T(8,128)S(1)}, f32[2,256,256]{2,1,0:T(8,128)S(1)}, u32[]{:S(2)}, u32[]{:S(2)}) collective-permute-start(f32[2,256,256]{2,1,0:T(8,128)S(1)} %get-tuple-element.35), channel_id=1, source_target_pairs={{0,12},{1,13},{2,14},{3,15},{4,8},{5,9},{6,10},{7,11},{8,4},{9,5},... | collective-permute-start | bytes 1572872 | tf_op jit(solution)/shard_map/ppermute | solution.py:35
  74.7 13.7 %collective-permute-done.11.refs_6_ = bf16[256,1792]{1,0:T(8,128)(2,1)S(1)} collective-permute-done((bf16[256,1792]{1,0:T(8,128)(2,1)}, bf16[256,1792]{1,0:T(8,128)(2,1)S(1)}, u32[]{:S(2)}, u32[]{:S(2)}) %collective-permute-start.11) | collective-permute-done | bytes 917536 | tf_op jit(solution)/shard_map/ppermute | solution.py:35
  88.4 3.6 %block_products.3 = (f32[2,256,256]{2,1,0:T(8,128)S(1)}, f32[2,256,256]{2,1,0:T(8,128)S(1)}, f32[2,256,256]{2,1,0:T(8,128)S(1)}, f32[2,256,256]{2,1,0:T(8,128)S(1)}) custom-call(s32[6]{0:T(128)S(1)} %stack.27.where, bf16[256,1792]{1,0:T(8,128)(2,1)S(1)} %copy-done.1, bf16[256,1792]{1,0:T(8,128)(2,1)S(1)} %collective-permute-done.2.refs_1_, ...), custom_call_target="tpu_custom_call" | custom-call | flops 1879048192 | bytes 8519704 | tf_op jit(solution)/shard_map/block_products/pallas_call | solution.py:59
  92.1 2.5 %collective-permute-start.12 = (f32[2,256,256]{2,1,0:T(8,128)S(1)}, f32[2,256,256]{2,1,0:T(8,128)S(1)}, u32[]{:S(2)}, u32[]{:S(2)}) collective-permute-start(f32[2,256,256]{2,1,0:T(8,128)S(1)} %get-tuple-element.41), channel_id=1, source_target_pairs={{1,5},{3,7},{5,1},{7,3},{9,13},{11,15},{13,9},{15,11},{17,21},{19,... | collective-permute-start | bytes 1572872 | tf_op jit(solution)/shard_map/ppermute | solution.py:35
  94.6 3.5 %collective-permute-start.13 = (f32[2,256,256]{2,1,0:T(8,128)S(1)}, f32[2,256,256]{2,1,0:T(8,128)S(1)}, u32[]{:S(2)}, u32[]{:S(2)}) collective-permute-start(f32[2,256,256]{2,1,0:T(8,128)S(1)} %get-tuple-element.42), channel_id=1, source_target_pairs={{1,9},{3,11},{5,13},{7,15},{9,1},{11,3},{13,5},{15,7},{17,25},{19,... | collective-permute-start | bytes 1572872 | tf_op jit(solution)/shard_map/ppermute | solution.py:35
  98.1 3.6 %collective-permute-start.14 = (f32[2,256,256]{2,1,0:T(8,128)S(1)}, f32[2,256,256]{2,1,0:T(8,128)S(1)}, u32[]{:S(2)}, u32[]{:S(2)}) collective-permute-start(f32[2,256,256]{2,1,0:T(8,128)S(1)} %get-tuple-element.43), channel_id=1, source_target_pairs={{1,13},{3,15},{5,9},{7,11},{9,5},{11,7},{13,1},{15,3},{17,29},{19,... | collective-permute-start | bytes 1572872 | tf_op jit(solution)/shard_map/ppermute | solution.py:35
  101.7 0.8 halves.2
  102.5 3.2 %collective-permute-start.9 = (f32[4,128,256]{2,1,0:T(8,128)S(1)}, f32[4,128,256]{2,1,0:T(8,128)S(1)}, u32[]{:S(2)}, u32[]{:S(2)}) collective-permute-start(f32[4,128,256]{2,1,0:T(8,128)S(1)} %get-tuple-element.37), channel_id=1, source_target_pairs={{0,2},{1,3},{2,0},{3,1},{4,6},{5,7},{6,4},{7,5},{8,10},{9,11},{10,... | collective-permute-start | bytes 1572872 | tf_op jit(solution)/shard_map/ppermute | solution.py:35
  105.7 2.8 %collective-permute-done.13.third = f32[2,256,256]{2,1,0:T(8,128)S(1)} collective-permute-done((f32[2,256,256]{2,1,0:T(8,128)S(1)}, f32[2,256,256]{2,1,0:T(8,128)S(1)}, u32[]{:S(2)}, u32[]{:S(2)}) %collective-permute-start.13) | collective-permute-done | bytes 524320 | tf_op jit(solution)/shard_map/ppermute | solution.py:35
  108.5 5.5 %collective-permute-done.14.fourth = f32[2,256,256]{2,1,0:T(8,128)S(1)} collective-permute-done((f32[2,256,256]{2,1,0:T(8,128)S(1)}, f32[2,256,256]{2,1,0:T(8,128)S(1)}, u32[]{:S(2)}, u32[]{:S(2)}) %collective-permute-start.14) | collective-permute-done | bytes 524320 | tf_op jit(solution)/shard_map/ppermute | solution.py:35
  114.0 0.8 halves.3
  114.7 2.4 %collective-permute-start.15 = (f32[4,128,256]{2,1,0:T(8,128)S(1)}, f32[4,128,256]{2,1,0:T(8,128)S(1)}, u32[]{:S(2)}, u32[]{:S(2)}) collective-permute-start(f32[4,128,256]{2,1,0:T(8,128)S(1)} %get-tuple-element.45), channel_id=1, source_target_pairs={{1,3},{3,1},{5,7},{7,5},{9,11},{11,9},{13,15},{15,13},{17,19},{19,... | collective-permute-start | bytes 1572872 | tf_op jit(solution)/shard_map/ppermute | solution.py:35
  117.2 13.0 %collective-permute-start.16 = (f32[128,256]{1,0:T(8,128)S(1)}, f32[128,256]{1,0:T(8,128)S(1)}, u32[]{:S(2)}, u32[]{:S(2)}) collective-permute-start(f32[128,256]{1,0:T(8,128)S(1)} %get-tuple-element.59.refs_0_), channel_id=1, source_target_pairs={{8,32},{9,33},{10,34},{11,35},{12,36},{13,37},{14,38},{15,39},{24,... | collective-permute-start | bytes 393224 | tf_op jit(solution)/shard_map/ppermute | solution.py:35
  130.2 1.9 %collective-permute-start.17 = (f32[128,256]{1,0:T(8,128)S(1)}, f32[128,256]{1,0:T(8,128)S(1)}, u32[]{:S(2)}, u32[]{:S(2)}) collective-permute-start(f32[128,256]{1,0:T(8,128)S(1)} %get-tuple-element.58.refs_1_), channel_id=1, source_target_pairs={{8,32},{9,33},{10,34},{11,35},{12,36},{13,37},{14,38},{15,39},{24,... | collective-permute-start | bytes 393224 | tf_op jit(solution)/shard_map/ppermute | solution.py:35
  132.1 4.2 %collective-permute-start.20 = (f32[128,256]{1,0:T(8,128)S(1)}, f32[128,256]{1,0:T(8,128)S(1)}, u32[]{:S(2)}, u32[]{:S(2)}) collective-permute-start(f32[128,256]{1,0:T(8,128)S(1)} %get-tuple-element.57), channel_id=1, source_target_pairs={{9,9},{11,11},{13,25},{15,27},{25,13},{27,15},{29,29},{31,31},{32,... | collective-permute-start | bytes 393224 | tf_op jit(solution)/shard_map/ppermute | solution.py:35
  136.3 6.2 %collective-permute-start.21 = (f32[128,256]{1,0:T(8,128)S(1)}, f32[128,256]{1,0:T(8,128)S(1)}, u32[]{:S(2)}, u32[]{:S(2)}) collective-permute-start(f32[128,256]{1,0:T(8,128)S(1)} %get-tuple-element.56), channel_id=1, source_target_pairs={{1,65},{3,67},{5,81},{7,83},{9,73},{11,75},{13,89},{15,91},{17,69}... | collective-permute-start | bytes 393224 | tf_op jit(solution)/shard_map/ppermute | solution.py:35
  142.5 5.1 %collective-permute-start.18 = (f32[128,256]{1,0:T(8,128)S(1)}, f32[128,256]{1,0:T(8,128)S(1)}, u32[]{:S(2)}, u32[]{:S(2)}) collective-permute-start(f32[128,256]{1,0:T(8,128)S(1)} %get-tuple-element.55.refs_2_), channel_id=1, source_target_pairs={{9,33},{11,35},{13,37},{15,39},{25,49},{27,51},{29,53},{31,55},{33... | collective-permute-start | bytes 393224 | tf_op jit(solution)/shard_map/ppermute | solution.py:35
  147.7 1.3 collective-permute-start.19
  149.0 6.7 %collective-permute-start.22 = (f32[128,256]{1,0:T(8,128)S(1)}, f32[128,256]{1,0:T(8,128)S(1)}, u32[]{:S(2)}, u32[]{:S(2)}) collective-permute-start(f32[128,256]{1,0:T(8,128)S(1)} %get-tuple-element.53), channel_id=1, source_target_pairs={{1,129},{3,131},{5,145},{7,147},{9,137},{11,139},{13,153},{15,155}... | collective-permute-start | bytes 393224 | tf_op jit(solution)/shard_map/ppermute | solution.py:35
  155.7 0.7 collective-permute-start.23
  156.4 2.4 %collective-permute-done.19.refs_6_ = f32[128,256]{1,0:T(8,128)S(1)} collective-permute-done((f32[128,256]{1,0:T(8,128)S(1)}, f32[128,256]{1,0:T(8,128)S(1)}, u32[]{:S(2)}, u32[]{:S(2)}) %collective-permute-start.19) | collective-permute-done | bytes 131104 | tf_op jit(solution)/shard_map/ppermute | solution.py:35
  158.8 0.6 strips.1
  159.4 10.0 %collective-permute-start.24 = (f32[4,64,256]{2,1,0:T(8,128)S(1)}, f32[4,64,256]{2,1,0:T(8,128)S(1)}, u32[]{:S(2)}, u32[]{:S(2)}) collective-permute-start(f32[4,64,256]{2,1,0:T(8,128)S(1)} %get-tuple-element.47), channel_id=1, source_target_pairs={{0,1},{1,0},{2,3},{3,2},{4,5},{5,4},{6,7},{7,6},{8,9},{9,8},{10,11... | collective-permute-start | bytes 786440 | tf_op jit(solution)/shard_map/ppermute | solution.py:35
  169.6 1.0 collective-permute-done.24.other
  170.6 1.9 %refresh.1 = (bf16[64,1024]{1,0:T(8,128)(2,1)}, f32[64,8]{1,0:T(8,128)S(1)}) custom-call(s32[6]{0:T(128)S(1)} %stack.27.where, f32[4,64,256]{2,1,0:T(8,128)S(1)} %get-tuple-element.46.mine, f32[4,64,256]{2,1,0:T(8,128)S(1)} %collective-permute-done.24.other, bf16[64,1024]{1,0:T(8,128)(2,1)S(1)} %bitcast.27, f32[64,8]{1,0:T(8,128)S(1)} %bitcast.26), custom_call_target="tpu_custom_call" | custom-call | flops 16777216 | bytes 790552 | tf_op jit(solution)/shard_map/refresh/pallas_call | solution.py:59
  172.5 0.7 copy.6
  (27 shorter events, 0.5 us)
Async XLA Ops:
  0.6 14.8 %collective-permute-start = (bf16[256,1792]{1,0:T(8,128)(2,1)}, bf16[256,1792]{1,0:T(8,128)(2,1)S(1)}, u32[]{:S(2)}, u32[]{:S(2)}) collective-permute-start(bf16[256,1792]{1,0:T(8,128)(2,1)} %refs_0_.3), channel_id=1, source_target_pairs={{0,32},{2,34},{4,36},{6,38},{8,40},{10,42},{12,44},{14,46},{16,48}... | collective-permute-start | bytes 2752520 | tf_op jit(solution)/shard_map/ppermute | solution.py:35
  1.9 22.2 %collective-permute-start.2 = (bf16[256,1792]{1,0:T(8,128)(2,1)}, bf16[256,1792]{1,0:T(8,128)(2,1)S(1)}, u32[]{:S(2)}, u32[]{:S(2)}) collective-permute-start(bf16[256,1792]{1,0:T(8,128)(2,1)} %refs_0_.3), channel_id=1, source_target_pairs={{0,16},{1,17},{2,18},{3,19},{4,20},{5,21},{6,22},{7,23},{8,24},{9,... | collective-permute-start | bytes 2752520 | tf_op jit(solution)/shard_map/ppermute | solution.py:35
  15.5 14.3 %collective-permute-start.1 = (bf16[256,1792]{1,0:T(8,128)(2,1)S(1)}, bf16[256,1792]{1,0:T(8,128)(2,1)S(1)}, u32[]{:S(2)}, u32[]{:S(2)}) collective-permute-start(bf16[256,1792]{1,0:T(8,128)(2,1)S(1)} %collective-permute-done.refs_2_), channel_id=1, source_target_pairs={{32,64},{33,1},{34,66},{35,3},{36,68},{37,5},{38,70},{39,7},{40,72... | collective-permute-start | bytes 2752520 | tf_op jit(solution)/shard_map/ppermute | solution.py:35
  16.7 0.9 copy-start.2
  17.7 16.2 %collective-permute-start.4 = (bf16[256,1792]{1,0:T(8,128)(2,1)}, bf16[256,1792]{1,0:T(8,128)(2,1)S(1)}, u32[]{:S(2)}, u32[]{:S(2)}) collective-permute-start(bf16[256,1792]{1,0:T(8,128)(2,1)} %refs_0_.3), channel_id=1, source_target_pairs={{1,65},{3,67},{5,69},{7,71},{9,73},{11,75},{13,77},{15,79},{17,81}... | collective-permute-start | bytes 2752520 | tf_op jit(solution)/shard_map/ppermute | solution.py:35
  29.8 14.6 %collective-permute-start.3 = (bf16[256,1792]{1,0:T(8,128)(2,1)S(1)}, bf16[256,1792]{1,0:T(8,128)(2,1)S(1)}, u32[]{:S(2)}, u32[]{:S(2)}) collective-permute-start(bf16[256,1792]{1,0:T(8,128)(2,1)S(1)} %collective-permute-done.1.refs_3_), channel_id=1, source_target_pairs={{33,1},{35,3},{37,5},{39,7},{41,9},{43,11},{45,13},{47,15},{49,17}... | collective-permute-start | bytes 2752520 | tf_op jit(solution)/shard_map/ppermute | solution.py:35
  31.1 0.9 copy-start.4
  44.4 21.1 %collective-permute-start.5 = (bf16[256,1792]{1,0:T(8,128)(2,1)S(1)}, bf16[256,1792]{1,0:T(8,128)(2,1)}, u32[]{:S(2)}, u32[]{:S(2)}) collective-permute-start(bf16[256,1792]{1,0:T(8,128)(2,1)S(1)} %collective-permute-done.3.refs_4_), channel_id=1, source_target_pairs={{33,1},{35,3},{37,5},{39,7},{41,9},{43,11},{45,13},{47,15},{49,17}... | collective-permute-start | bytes 2752520 | tf_op jit(solution)/shard_map/ppermute | solution.py:35
  45.8 1.2 copy-start.1
  46.9 1.2 copy-start.3
  48.1 1.2 copy-start.5
  52.1 13.2 %collective-permute-start.6 = (f32[2,256,256]{2,1,0:T(8,128)S(1)}, f32[2,256,256]{2,1,0:T(8,128)S(1)}, u32[]{:S(2)}, u32[]{:S(2)}) collective-permute-start(f32[2,256,256]{2,1,0:T(8,128)S(1)} %get-tuple-element.32), channel_id=1, source_target_pairs={{0,4},{1,5},{2,6},{3,7},{4,0},{5,1},{6,2},{7,3},{8,12},{9,13},{10,... | collective-permute-start | bytes 1572872 | tf_op jit(solution)/shard_map/ppermute | solution.py:35
  54.6 20.2 %collective-permute-start.10 = (bf16[256,1792]{1,0:T(8,128)(2,1)S(1)}, bf16[256,1792]{1,0:T(8,128)(2,1)S(1)}, u32[]{:S(2)}, u32[]{:S(2)}) collective-permute-start(bf16[256,1792]{1,0:T(8,128)(2,1)S(1)} %collective-permute-done.4.refs_2_), channel_id=1, source_target_pairs={{65,81},{67,83},{69,85},{71,87},{73,89},{75,91},{77,93},{79,95},{8... | collective-permute-start | bytes 2752520 | tf_op jit(solution)/shard_map/ppermute | solution.py:35
  65.5 22.9 %collective-permute-start.11 = (bf16[256,1792]{1,0:T(8,128)(2,1)}, bf16[256,1792]{1,0:T(8,128)(2,1)S(1)}, u32[]{:S(2)}, u32[]{:S(2)}) collective-permute-start(bf16[256,1792]{1,0:T(8,128)(2,1)} %collective-permute-done.5.refs_5_), channel_id=1, source_target_pairs={{33,1},{35,3},{37,5},{39,7},{41,9},{43,11},{45,13},{47,15},{49,17}... | collective-permute-start | bytes 2752520 | tf_op jit(solution)/shard_map/ppermute | solution.py:35
  66.8 34.9 %collective-permute-start.7 = (f32[2,256,256]{2,1,0:T(8,128)S(1)}, f32[2,256,256]{2,1,0:T(8,128)S(1)}, u32[]{:S(2)}, u32[]{:S(2)}) collective-permute-start(f32[2,256,256]{2,1,0:T(8,128)S(1)} %get-tuple-element.34), channel_id=1, source_target_pairs={{0,8},{1,9},{2,10},{3,11},{4,12},{5,13},{6,14},{7,15},{8,0},{9,1},... | collective-permute-start | bytes 1572872 | tf_op jit(solution)/shard_map/ppermute | solution.py:35
  71.9 29.8 %collective-permute-start.8 = (f32[2,256,256]{2,1,0:T(8,128)S(1)}, f32[2,256,256]{2,1,0:T(8,128)S(1)}, u32[]{:S(2)}, u32[]{:S(2)}) collective-permute-start(f32[2,256,256]{2,1,0:T(8,128)S(1)} %get-tuple-element.35), channel_id=1, source_target_pairs={{0,12},{1,13},{2,14},{3,15},{4,8},{5,9},{6,10},{7,11},{8,4},{9,5},... | collective-permute-start | bytes 1572872 | tf_op jit(solution)/shard_map/ppermute | solution.py:35
  92.1 13.6 %collective-permute-start.12 = (f32[2,256,256]{2,1,0:T(8,128)S(1)}, f32[2,256,256]{2,1,0:T(8,128)S(1)}, u32[]{:S(2)}, u32[]{:S(2)}) collective-permute-start(f32[2,256,256]{2,1,0:T(8,128)S(1)} %get-tuple-element.41), channel_id=1, source_target_pairs={{1,5},{3,7},{5,1},{7,3},{9,13},{11,15},{13,9},{15,11},{17,21},{19,... | collective-permute-start | bytes 1572872 | tf_op jit(solution)/shard_map/ppermute | solution.py:35
  94.6 13.9 %collective-permute-start.13 = (f32[2,256,256]{2,1,0:T(8,128)S(1)}, f32[2,256,256]{2,1,0:T(8,128)S(1)}, u32[]{:S(2)}, u32[]{:S(2)}) collective-permute-start(f32[2,256,256]{2,1,0:T(8,128)S(1)} %get-tuple-element.42), channel_id=1, source_target_pairs={{1,9},{3,11},{5,13},{7,15},{9,1},{11,3},{13,5},{15,7},{17,25},{19,... | collective-permute-start | bytes 1572872 | tf_op jit(solution)/shard_map/ppermute | solution.py:35
  98.1 15.9 %collective-permute-start.14 = (f32[2,256,256]{2,1,0:T(8,128)S(1)}, f32[2,256,256]{2,1,0:T(8,128)S(1)}, u32[]{:S(2)}, u32[]{:S(2)}) collective-permute-start(f32[2,256,256]{2,1,0:T(8,128)S(1)} %get-tuple-element.43), channel_id=1, source_target_pairs={{1,13},{3,15},{5,9},{7,11},{9,5},{11,7},{13,1},{15,3},{17,29},{19,... | collective-permute-start | bytes 1572872 | tf_op jit(solution)/shard_map/ppermute | solution.py:35
  102.5 14.6 %collective-permute-start.9 = (f32[4,128,256]{2,1,0:T(8,128)S(1)}, f32[4,128,256]{2,1,0:T(8,128)S(1)}, u32[]{:S(2)}, u32[]{:S(2)}) collective-permute-start(f32[4,128,256]{2,1,0:T(8,128)S(1)} %get-tuple-element.37), channel_id=1, source_target_pairs={{0,2},{1,3},{2,0},{3,1},{4,6},{5,7},{6,4},{7,5},{8,10},{9,11},{10,... | collective-permute-start | bytes 1572872 | tf_op jit(solution)/shard_map/ppermute | solution.py:35
  114.7 27.7 %collective-permute-start.15 = (f32[4,128,256]{2,1,0:T(8,128)S(1)}, f32[4,128,256]{2,1,0:T(8,128)S(1)}, u32[]{:S(2)}, u32[]{:S(2)}) collective-permute-start(f32[4,128,256]{2,1,0:T(8,128)S(1)} %get-tuple-element.45), channel_id=1, source_target_pairs={{1,3},{3,1},{5,7},{7,5},{9,11},{11,9},{13,15},{15,13},{17,19},{19,... | collective-permute-start | bytes 1572872 | tf_op jit(solution)/shard_map/ppermute | solution.py:35
  117.2 30.5 %collective-permute-start.16 = (f32[128,256]{1,0:T(8,128)S(1)}, f32[128,256]{1,0:T(8,128)S(1)}, u32[]{:S(2)}, u32[]{:S(2)}) collective-permute-start(f32[128,256]{1,0:T(8,128)S(1)} %get-tuple-element.59.refs_0_), channel_id=1, source_target_pairs={{8,32},{9,33},{10,34},{11,35},{12,36},{13,37},{14,38},{15,39},{24,... | collective-permute-start | bytes 393224 | tf_op jit(solution)/shard_map/ppermute | solution.py:35
  130.2 18.8 %collective-permute-start.17 = (f32[128,256]{1,0:T(8,128)S(1)}, f32[128,256]{1,0:T(8,128)S(1)}, u32[]{:S(2)}, u32[]{:S(2)}) collective-permute-start(f32[128,256]{1,0:T(8,128)S(1)} %get-tuple-element.58.refs_1_), channel_id=1, source_target_pairs={{8,32},{9,33},{10,34},{11,35},{12,36},{13,37},{14,38},{15,39},{24,... | collective-permute-start | bytes 393224 | tf_op jit(solution)/shard_map/ppermute | solution.py:35
  132.1 23.6 %collective-permute-start.20 = (f32[128,256]{1,0:T(8,128)S(1)}, f32[128,256]{1,0:T(8,128)S(1)}, u32[]{:S(2)}, u32[]{:S(2)}) collective-permute-start(f32[128,256]{1,0:T(8,128)S(1)} %get-tuple-element.57), channel_id=1, source_target_pairs={{9,9},{11,11},{13,25},{15,27},{25,13},{27,15},{29,29},{31,31},{32,... | collective-permute-start | bytes 393224 | tf_op jit(solution)/shard_map/ppermute | solution.py:35
  136.3 20.1 %collective-permute-start.21 = (f32[128,256]{1,0:T(8,128)S(1)}, f32[128,256]{1,0:T(8,128)S(1)}, u32[]{:S(2)}, u32[]{:S(2)}) collective-permute-start(f32[128,256]{1,0:T(8,128)S(1)} %get-tuple-element.56), channel_id=1, source_target_pairs={{1,65},{3,67},{5,81},{7,83},{9,73},{11,75},{13,89},{15,91},{17,69}... | collective-permute-start | bytes 393224 | tf_op jit(solution)/shard_map/ppermute | solution.py:35
  142.5 13.8 %collective-permute-start.18 = (f32[128,256]{1,0:T(8,128)S(1)}, f32[128,256]{1,0:T(8,128)S(1)}, u32[]{:S(2)}, u32[]{:S(2)}) collective-permute-start(f32[128,256]{1,0:T(8,128)S(1)} %get-tuple-element.55.refs_2_), channel_id=1, source_target_pairs={{9,33},{11,35},{13,37},{15,39},{25,49},{27,51},{29,53},{31,55},{33... | collective-permute-start | bytes 393224 | tf_op jit(solution)/shard_map/ppermute | solution.py:35
  147.7 11.1 %collective-permute-start.19 = (f32[128,256]{1,0:T(8,128)S(1)}, f32[128,256]{1,0:T(8,128)S(1)}, u32[]{:S(2)}, u32[]{:S(2)}) collective-permute-start(f32[128,256]{1,0:T(8,128)S(1)} %get-tuple-element.54), channel_id=1, source_target_pairs={{65,1},{67,3},{69,5},{71,7},{73,33},{75,35},{77,37},{79,39},{81,17... | collective-permute-start | bytes 393224 | tf_op jit(solution)/shard_map/ppermute | solution.py:35
  149.0 9.8 %collective-permute-start.22 = (f32[128,256]{1,0:T(8,128)S(1)}, f32[128,256]{1,0:T(8,128)S(1)}, u32[]{:S(2)}, u32[]{:S(2)}) collective-permute-start(f32[128,256]{1,0:T(8,128)S(1)} %get-tuple-element.53), channel_id=1, source_target_pairs={{1,129},{3,131},{5,145},{7,147},{9,137},{11,139},{13,153},{15,155}... | collective-permute-start | bytes 393224 | tf_op jit(solution)/shard_map/ppermute | solution.py:35
  155.7 3.1 %collective-permute-start.23 = (f32[128,256]{1,0:T(8,128)S(1)}, f32[128,256]{1,0:T(8,128)S(1)}, u32[]{:S(2)}, u32[]{:S(2)}) collective-permute-start(f32[128,256]{1,0:T(8,128)S(1)} %get-tuple-element.52), channel_id=1, source_target_pairs={{65,193},{67,195},{69,209},{71,211},{73,201},{75,203},{77,217},{79... | collective-permute-start | bytes 393224 | tf_op jit(solution)/shard_map/ppermute | solution.py:35
  158.8 10.7 %copy-start.6 = (f32[1,64,8]{1,2,0:T(8,128)S(1)}, f32[1,64,8]{1,2,0:T(8,128)}, u32[]{:S(2)}) copy-start(f32[1,64,8]{1,2,0:T(8,128)} %param.5) | copy-start | bytes 6148
  158.8 11.8 %copy-start = (bf16[1,64,1024]{2,1,0:T(8,128)(2,1)S(1)}, bf16[1,64,1024]{2,1,0:T(8,128)(2,1)}, u32[]{:S(2)}) copy-start(bf16[1,64,1024]{2,1,0:T(8,128)(2,1)} %param.4) | copy-start | bytes 393220
  159.4 11.2 %collective-permute-start.24 = (f32[4,64,256]{2,1,0:T(8,128)S(1)}, f32[4,64,256]{2,1,0:T(8,128)S(1)}, u32[]{:S(2)}, u32[]{:S(2)}) collective-permute-start(f32[4,64,256]{2,1,0:T(8,128)S(1)} %get-tuple-element.47), channel_id=1, source_target_pairs={{0,1},{1,0},{2,3},{3,2},{4,5},{5,4},{6,7},{7,6},{8,9},{9,8},{10,11... | collective-permute-start | bytes 786440 | tf_op jit(solution)/shard_map/ppermute | solution.py:35

commit v6 on v4

--- a/solution.py
+++ b/solution.py
@@ -61,49 +61,29 @@
     return jax.ShapeDtypeStruct(shape, jnp.float32)
 
 
-def products_kernel(where, *refs):
-    rows, cols, outs = refs[:4], refs[4:-4], refs[-4:]
-    for turn in range(4):
-
-        @pl.when(where[0] == turn)
-        def _():
-            for d in range(4):
-                for k, col in enumerate(cols):
-                    outs[d][k] = lax.dot_general(
-                        rows[d ^ turn][...],
-                        col[...],
-                        (((1,), (1,)), ((), ())),
-                        preferred_element_type=jnp.float32,
-                    )
-
-
-def products(where, rows, cols):
-    size, depth = rows[0].shape
-    count = len(cols)
-    return call(
-        products_kernel,
-        "block_products",
-        [floats(count, size, size)] * 4,
-        8 * count * size * size * depth,
-        where,
-        *rows,
-        *cols,
-    )
+def products(rows, cols):
+    cols = jnp.concatenate(cols, axis=0)
+    return [
+        lax.dot_general(
+            row, cols, (((1,), (1,)), ((), ())), preferred_element_type=jnp.float32
+        )
+        for row in rows
+    ]
 
 
 def halves_kernel(far, where, first, second, third, fourth, keep, give):
-    count, size, _ = first.shape
-    half = size // 2
+    half, size = keep.shape[1:]
     upper = where[1] == 1
-    totals = [first[k] + second[k] + third[k] + fourth[k] for k in range(count)]
+    total = first[...] + second[...] + third[...] + fourth[...]
+    totals = [total[:, k : k + size] for k in range(0, total.shape[1], size)]
     for k, total in enumerate(totals + [totals[k].T for k in far]):
         keep[k] = jnp.where(upper, total[half:], total[:half])
         give[k] = jnp.where(upper, total[:half], total[half:])
 
 
 def halves(where, far, parts):
-    count, size, _ = parts[0].shape
-    shape = floats(count + len(far), size // 2, size)
+    size, width = parts[0].shape
+    shape = floats(width // size + len(far), size // 2, size)
     return call(
         functools.partial(halves_kernel, far), "halves", [shape, shape], 0, where, *parts
     )
@@ -178,6 +158,10 @@
     )
 
 
+def swap_if(flag, first, second):
+    return jnp.where(flag, second, first), jnp.where(flag, first, second)
+
+
 def per_device(gradient, left_codes, left_scales):
     dp, tensor = lax.axis_index("dp"), lax.axis_index("tensor")
     where = jnp.stack(
@@ -186,32 +170,33 @@
 
     z_block = permute(gradient, lambda at: dict(h=at["h"] ^ 2))
     y_block = permute(gradient, lambda at: dict(h=at["h"] ^ 1))
-    z_block, y_block, sent = lax.optimization_barrier((z_block, y_block, gradient))
     zy_block = permute(z_block, lambda at: dict(h=at["h"] ^ 1))
-    rows = [gradient, y_block, z_block, zy_block]
-
-    def onwards(block, step):
-        return permute(block, onward, lambda at: step - 1 <= reach(at) < SUPERS - 1)
-
-    passing = [sent, onwards(sent, 1)]
-    passing[1], rows[3] = lax.optimization_barrier((passing[1], rows[3]))
-    passing.append(onwards(passing[1], 2))
+    turn = (tensor >> 2) ^ (dp & 3)
+    low = swap_if(turn & 1 == 1, gradient, y_block)
+    high = swap_if(turn & 1 == 1, z_block, zy_block)
+    s0, s2 = swap_if(turn >> 1 == 1, low[0], high[0])
+    s1, s3 = swap_if(turn >> 1 == 1, low[1], high[1])
+    rows = [s0, s1, s2, s3]
+
+    passing = [gradient, permute(gradient, onward, lambda at: reach(at) < 3)]
+    passing.append(permute(passing[1], onward, lambda at: 1 <= reach(at) < 3))
+    passing.append(
+        permute(
+            passing[1],
+            lambda at: dict(g=at["g"] + (2 if at["c"] == 0 else -2)),
+            lambda at: reach(at) == 1,
+        )
+    )
 
     own, across = [None] * SUPERS, [None] * SUPERS
-    for steps in ((0, 1), (2,), (3,)):
-        parts = list(products(where, rows, [passing[step] for step in steps]))
+    for steps in ((0, 1), (2, 3)):
+        parts = products(rows, [passing[step] for step in steps])
         valid = lambda at, steps=steps: reach(at) >= steps[0]
         parts[1:] = [
             permute(parts[d], lambda at, d=d: dict(x=at["x"] ^ d), valid) for d in (1, 2, 3)
         ]
-        if steps[0] == 0:
-            passing[2], *parts = lax.optimization_barrier((passing[2], *parts))
-            passing.append(onwards(passing[2], 3))
         far = [k for k, step in enumerate(steps) if step]
         keep, give = halves(where, far, parts)
-        if steps[-1] < SUPERS - 1:
-            ahead = steps[-1] + 1
-            passing[ahead], keep, give = lax.optimization_barrier((passing[ahead], keep, give))
         came = permute(give, lambda at: dict(yl=at["yl"] ^ 1), valid)
         for k, step in enumerate(steps):
             own[step] = keep[k] + came[k]

time: 179 us -> 147 us (0.82)
  starting transfers between devices: 92.5 us -> 62.1 us
  Pallas kernels: 11.9 us -> 3.96 us
  matrix products: 0 us -> 5.33 us
    ppermute x22 -> x18, starting transfers between devices: 92.5 us -> 62.1 us  [permute(): return lax.ppermute(array, AXES, pairs)]
    pallas_call x8 -> x4, Pallas kernels: 11.9 us -> 3.96 us  [call(): pl.pallas_call(kernel, out_shape=outs, in_specs=in_specs, out_specs=[VMEM...]
    dot_general x0 -> x8, matrix products: none -> 5.33 us  [products(): lax.dot_general(row, cols, (((1,), (1,)), ((), ())), preferred_element_ty...]
    ppermute x22 -> x18, waiting for transfers between devices: 70.6 us -> 71.4 us  [permute(): return lax.ppermute(array, AXES, pairs)]
  transfers between devices with their start and end apart: 22 -> 18, of which waited for: 11 -> 8; matrix products, arithmetic and copies ran while one was open for 0% -> 5% of each run, Pallas kernels for 5% -> 1%
where the time goes in v6:
time: 147 us
  waiting for transfers between devices  71.4 us (49%)
  starting transfers between devices  62.1 us (42%)
  matrix products  5.33 us (4%)
  Pallas kernels  3.96 us (3%)
  other arithmetic  1.87 us (1%)
    ppermute x18, waiting for transfers between devices, permute(): return lax.ppermute(array, AXES, pairs)  71.4 us
    ppermute x18, starting transfers between devices, permute(): return lax.ppermute(array, AXES, pairs)  62.1 us
    dot_general x8, matrix products, products(): lax.dot_general(row, cols, (((1,), (1,)), ((), ())), preferred_element_ty...  5.33 us
    pallas_call x4, Pallas kernels, call(): pl.pallas_call(kernel, out_shape=outs, in_specs=in_specs, out_specs=[VMEM...  3.96 us
  transfers between devices with their start and end apart: 18, of which 8 were waited for; matrix products, arithmetic and copies ran while one was open for 5% of the time, Pallas kernels for 1%

profile of v6, /device:TPU:7, one launch (start us, length us, event | category | flops | bytes accessed | tf_op | source)
XLA Modules:
  0.0 146.6 jit_solution(13316689034845834944)
XLA Ops:
  0.6 3.5 %collective-permute-start = (bf16[256,1792]{1,0:T(8,128)(2,1)}, bf16[256,1792]{1,0:T(8,128)(2,1)S(1)}, u32[]{:S(2)}, u32[]{:S(2)}) collective-permute-start(bf16[256,1792]{1,0:T(8,128)(2,1)} %param.3), channel_id=1, source_target_pairs={{0,32},{1,33},{2,34},{3,35},{4,36},{5,37},{6,38},{7,39},{8,40},{9,... | collective-permute-start | bytes 2752520 | tf_op jit(solution)/shard_map/ppermute | solution.py:35
  4.2 1.3 collective-permute-start.3
  5.5 4.8 %collective-permute-start.2 = (bf16[256,1792]{1,0:T(8,128)(2,1)}, bf16[256,1792]{1,0:T(8,128)(2,1)S(1)}, u32[]{:S(2)}, u32[]{:S(2)}) collective-permute-start(bf16[256,1792]{1,0:T(8,128)(2,1)} %param.3), channel_id=1, source_target_pairs={{0,16},{1,17},{2,18},{3,19},{4,20},{5,21},{6,22},{7,23},{8,24},{9,... | collective-permute-start | bytes 2752520 | tf_op jit(solution)/shard_map/ppermute | solution.py:35
  10.3 23.8 %collective-permute-done = bf16[256,1792]{1,0:T(8,128)(2,1)S(1)} collective-permute-done((bf16[256,1792]{1,0:T(8,128)(2,1)}, bf16[256,1792]{1,0:T(8,128)(2,1)S(1)}, u32[]{:S(2)}, u32[]{:S(2)}) %collective-permute-start) | collective-permute-done | bytes 917536 | tf_op jit(solution)/shard_map/ppermute | solution.py:35
  34.2 4.8 %collective-permute-start.1 = (bf16[256,1792]{1,0:T(8,128)(2,1)S(1)}, bf16[256,1792]{1,0:T(8,128)(2,1)S(1)}, u32[]{:S(2)}, u32[]{:S(2)}) collective-permute-start(bf16[256,1792]{1,0:T(8,128)(2,1)S(1)} %collective-permute-done), channel_id=1, source_target_pairs={{0,16},{1,17},{2,18},{3,19},{4,20},{5,21},{6,22},{7,23},{8,24},{9,... | collective-permute-start | bytes 2752520 | tf_op jit(solution)/shard_map/ppermute | solution.py:35
  39.0 0.1 pad_add_fusion.where
  39.1 1.3 collective-permute-start.8
  40.4 1.3 collective-permute-start.9
  41.7 1.5 %broadcast_select_fusion = (bf16[256,1792]{1,0:T(8,128)(2,1)S(1)}, bf16[256,1792]{1,0:T(8,128)(2,1)S(1)}, bf16[512,1792]{1,0:T(8,128)(2,1)S(1)}) fusion(bf16[256,1792]{1,0:T(8,128)(2,1)} %param.3, bf16[256,1792]{1,0:T(8,128)(2,1)S(1)} %collective-permute-done.2, pred[]{:T(512)S(6)} %eq.9), kind=kLoop, calls=%fused_computation | loop fusion | flops 917503 | bytes 4587521 | tf_op jit(solution)/shard_map/jit(_where)/select_n | solution.py:162
  43.2 0.1 constant_dynamic-update-slice_fusion
  43.3 14.8 %collective-permute-done.1 = bf16[256,1792]{1,0:T(8,128)(2,1)S(1)} collective-permute-done((bf16[256,1792]{1,0:T(8,128)(2,1)S(1)}, bf16[256,1792]{1,0:T(8,128)(2,1)S(1)}, u32[]{:S(2)}, u32[]{:S(2)}) %collective-permute-start.1) | collective-permute-done | bytes 917536 | tf_op jit(solution)/shard_map/ppermute | solution.py:35
  58.1 0.1 broadcast_select_fusion.1
  58.2 0.7 fusion.3
  58.9 2.5 %collective-permute-start.4 = (f32[256,512]{1,0:T(8,128)S(1)}, f32[256,512]{1,0:T(8,128)S(1)}, u32[]{:S(2)}, u32[]{:S(2)}) collective-permute-start(f32[256,512]{1,0:T(8,128)S(1)} %fusion.3), channel_id=1, source_target_pairs={{0,4},{1,5},{2,6},{3,7},{4,0},{5,1},{6,2},{7,3},{8,12},{9,13},{10,... | collective-permute-start | bytes 1572872 | tf_op jit(solution)/shard_map/ppermute | solution.py:35
  61.3 0.7 fusion.5
  62.0 2.7 %collective-permute-start.5 = (f32[256,512]{1,0:T(8,128)S(1)}, f32[256,512]{1,0:T(8,128)S(1)}, u32[]{:S(2)}, u32[]{:S(2)}) collective-permute-start(f32[256,512]{1,0:T(8,128)S(1)} %fusion.5), channel_id=1, source_target_pairs={{0,8},{1,9},{2,10},{3,11},{4,12},{5,13},{6,14},{7,15},{8,0},{9,1},... | collective-permute-start | bytes 1572872 | tf_op jit(solution)/shard_map/ppermute | solution.py:35
  64.7 0.7 fusion.7
  65.3 4.5 %collective-permute-start.6 = (f32[256,512]{1,0:T(8,128)S(1)}, f32[256,512]{1,0:T(8,128)S(1)}, u32[]{:S(2)}, u32[]{:S(2)}) collective-permute-start(f32[256,512]{1,0:T(8,128)S(1)} %fusion.7), channel_id=1, source_target_pairs={{0,12},{1,13},{2,14},{3,15},{4,8},{5,9},{6,10},{7,11},{8,4},{9,5},... | collective-permute-start | bytes 1572872 | tf_op jit(solution)/shard_map/ppermute | solution.py:35
  69.8 0.1 constant_dynamic-update-slice_fusion.3
  69.9 20.7 %collective-permute-done.9 = bf16[256,1792]{1,0:T(8,128)(2,1)S(1)} collective-permute-done((bf16[256,1792]{1,0:T(8,128)(2,1)S(1)}, bf16[256,1792]{1,0:T(8,128)(2,1)S(1)}, u32[]{:S(2)}, u32[]{:S(2)}) %collective-permute-start.9) | collective-permute-done | bytes 917536 | tf_op jit(solution)/shard_map/ppermute | solution.py:35
  90.6 0.1 constant_dynamic-update-slice_fusion.2
  90.7 0.7 fusion.2
  91.4 2.5 %collective-permute-start.10 = (f32[256,512]{1,0:T(8,128)S(1)}, f32[256,512]{1,0:T(8,128)S(1)}, u32[]{:S(2)}, u32[]{:S(2)}) collective-permute-start(f32[256,512]{1,0:T(8,128)S(1)} %fusion.2), channel_id=1, source_target_pairs={{1,5},{3,7},{5,1},{7,3},{9,13},{11,15},{13,9},{15,11},{17,21},{19,... | collective-permute-start | bytes 1572872 | tf_op jit(solution)/shard_map/ppermute | solution.py:35
  93.9 0.7 fusion.4
  94.5 2.7 %collective-permute-start.11 = (f32[256,512]{1,0:T(8,128)S(1)}, f32[256,512]{1,0:T(8,128)S(1)}, u32[]{:S(2)}, u32[]{:S(2)}) collective-permute-start(f32[256,512]{1,0:T(8,128)S(1)} %fusion.4), channel_id=1, source_target_pairs={{1,9},{3,11},{5,13},{7,15},{9,1},{11,3},{13,5},{15,7},{17,25},{19,... | collective-permute-start | bytes 1572872 | tf_op jit(solution)/shard_map/ppermute | solution.py:35
  97.3 0.7 fusion.6
  98.0 4.4 %collective-permute-start.12 = (f32[256,512]{1,0:T(8,128)S(1)}, f32[256,512]{1,0:T(8,128)S(1)}, u32[]{:S(2)}, u32[]{:S(2)}) collective-permute-start(f32[256,512]{1,0:T(8,128)S(1)} %fusion.6), channel_id=1, source_target_pairs={{1,13},{3,15},{5,9},{7,11},{9,5},{11,7},{13,1},{15,3},{17,29},{19,... | collective-permute-start | bytes 1572872 | tf_op jit(solution)/shard_map/ppermute | solution.py:35
  102.4 0.7 fusion.1.first
  103.0 0.7 halves.2
  103.8 3.2 %collective-permute-start.7 = (f32[3,128,256]{2,1,0:T(8,128)S(1)}, f32[3,128,256]{2,1,0:T(8,128)S(1)}, u32[]{:S(2)}, u32[]{:S(2)}) collective-permute-start(f32[3,128,256]{2,1,0:T(8,128)S(1)} %get-tuple-element.11), channel_id=1, source_target_pairs={{0,2},{1,3},{2,0},{3,1},{4,6},{5,7},{6,4},{7,5},{8,10},{9,11},{10,... | collective-permute-start | bytes 1179656 | tf_op jit(solution)/shard_map/ppermute | solution.py:35
  107.0 0.7 fusion.first
  107.7 4.8 %collective-permute-done.12.fourth = f32[256,512]{1,0:T(8,128)S(1)} collective-permute-done((f32[256,512]{1,0:T(8,128)S(1)}, f32[256,512]{1,0:T(8,128)S(1)}, u32[]{:S(2)}, u32[]{:S(2)}) %collective-permute-start.12) | collective-permute-done | bytes 524320 | tf_op jit(solution)/shard_map/ppermute | solution.py:35
  112.5 0.8 halves.3
  113.3 3.2 %collective-permute-start.13 = (f32[4,128,256]{2,1,0:T(8,128)S(1)}, f32[4,128,256]{2,1,0:T(8,128)S(1)}, u32[]{:S(2)}, u32[]{:S(2)}) collective-permute-start(f32[4,128,256]{2,1,0:T(8,128)S(1)} %get-tuple-element.13), channel_id=1, source_target_pairs={{1,3},{3,1},{5,7},{7,5},{9,11},{11,9},{13,15},{15,13},{17,19},{19,... | collective-permute-start | bytes 1572872 | tf_op jit(solution)/shard_map/ppermute | solution.py:35
  116.5 0.1 fusion.10
  116.6 2.4 %collective-permute-start.14 = (f32[128,256]{1,0:T(8,128)S(1)}, f32[128,256]{1,0:T(8,128)S(1)}, u32[]{:S(2)}, u32[]{:S(2)}) collective-permute-start(f32[128,256]{1,0:T(8,128)S(1)} %get-tuple-element.29), channel_id=1, source_target_pairs={{1,65},{3,67},{5,81},{7,83},{9,97},{11,99},{13,113},{15,115},{17,6... | collective-permute-start | bytes 393224 | tf_op jit(solution)/shard_map/ppermute | solution.py:35
  119.0 4.2 %collective-permute-done.13 = f32[4,128,256]{2,1,0:T(8,128)S(1)} collective-permute-done((f32[4,128,256]{2,1,0:T(8,128)S(1)}, f32[4,128,256]{2,1,0:T(8,128)S(1)}, u32[]{:S(2)}, u32[]{:S(2)}) %collective-permute-start.13) | collective-permute-done | bytes 524320 | tf_op jit(solution)/shard_map/ppermute | solution.py:35
  123.2 0.1 fusion.8
  123.2 2.4 %collective-permute-start.15 = (f32[128,256]{1,0:T(8,128)S(1)}, f32[128,256]{1,0:T(8,128)S(1)}, u32[]{:S(2)}, u32[]{:S(2)}) collective-permute-start(f32[128,256]{1,0:T(8,128)S(1)} %get-tuple-element.25), channel_id=1, source_target_pairs={{1,129},{3,131},{5,145},{7,147},{9,161},{11,163},{13,177},{15,179}... | collective-permute-start | bytes 393224 | tf_op jit(solution)/shard_map/ppermute | solution.py:35
  125.6 1.3 collective-permute-start.16
  126.9 0.6 collective-permute-done.15.refs_5_
  127.5 1.4 collective-permute-done.16.refs_6_
  128.9 0.6 strips.1
  129.5 13.4 %collective-permute-start.17 = (f32[4,64,256]{2,1,0:T(8,128)S(1)}, f32[4,64,256]{2,1,0:T(8,128)S(1)}, u32[]{:S(2)}, u32[]{:S(2)}) collective-permute-start(f32[4,64,256]{2,1,0:T(8,128)S(1)} %get-tuple-element.15), channel_id=1, source_target_pairs={{0,1},{1,0},{2,3},{3,2},{4,5},{5,4},{6,7},{7,6},{8,9},{9,8},{10,11... | collective-permute-start | bytes 786440 | tf_op jit(solution)/shard_map/ppermute | solution.py:35
  143.0 0.1 copy.5
  143.1 1.0 collective-permute-done.17.other
  144.1 1.9 %refresh.1 = (bf16[64,1024]{1,0:T(8,128)(2,1)}, f32[64,8]{1,0:T(8,128)S(1)}) custom-call(s32[4]{0:T(128)S(1)} %pad_add_fusion.where, f32[4,64,256]{2,1,0:T(8,128)S(1)} %get-tuple-element.14.mine, f32[4,64,256]{2,1,0:T(8,128)S(1)} %collective-permute-done.17.other, bf16[64,1024]{1,0:T(8,128)(2,1)S(1)} %bitcast.31, f32[64,8]{1,0:T(8,128)S(1)} %bitcast.30), custom_call_target="tpu_custom_call" | custom-call | flops 16777216 | bytes 790544 | tf_op jit(solution)/shard_map/refresh/pallas_call | solution.py:49
  146.0 0.7 copy.6
  (14 shorter events, 0.0 us)
Async XLA Ops:
  0.6 33.5 %collective-permute-start = (bf16[256,1792]{1,0:T(8,128)(2,1)}, bf16[256,1792]{1,0:T(8,128)(2,1)S(1)}, u32[]{:S(2)}, u32[]{:S(2)}) collective-permute-start(bf16[256,1792]{1,0:T(8,128)(2,1)} %param.3), channel_id=1, source_target_pairs={{0,32},{1,33},{2,34},{3,35},{4,36},{5,37},{6,38},{7,39},{8,40},{9,... | collective-permute-start | bytes 2752520 | tf_op jit(solution)/shard_map/ppermute | solution.py:35
  4.2 34.9 %collective-permute-start.3 = (bf16[256,1792]{1,0:T(8,128)(2,1)}, bf16[256,1792]{1,0:T(8,128)(2,1)S(1)}, u32[]{:S(2)}, u32[]{:S(2)}) collective-permute-start(bf16[256,1792]{1,0:T(8,128)(2,1)} %param.3), channel_id=1, source_target_pairs={{0,64},{2,66},{4,68},{6,70},{8,72},{10,74},{12,76},{14,78},{16,80}... | collective-permute-start | bytes 2752520 | tf_op jit(solution)/shard_map/ppermute | solution.py:35
  5.5 36.2 %collective-permute-start.2 = (bf16[256,1792]{1,0:T(8,128)(2,1)}, bf16[256,1792]{1,0:T(8,128)(2,1)S(1)}, u32[]{:S(2)}, u32[]{:S(2)}) collective-permute-start(bf16[256,1792]{1,0:T(8,128)(2,1)} %param.3), channel_id=1, source_target_pairs={{0,16},{1,17},{2,18},{3,19},{4,20},{5,21},{6,22},{7,23},{8,24},{9,... | collective-permute-start | bytes 2752520 | tf_op jit(solution)/shard_map/ppermute | solution.py:35
  34.2 23.9 %collective-permute-start.1 = (bf16[256,1792]{1,0:T(8,128)(2,1)S(1)}, bf16[256,1792]{1,0:T(8,128)(2,1)S(1)}, u32[]{:S(2)}, u32[]{:S(2)}) collective-permute-start(bf16[256,1792]{1,0:T(8,128)(2,1)S(1)} %collective-permute-done), channel_id=1, source_target_pairs={{0,16},{1,17},{2,18},{3,19},{4,20},{5,21},{6,22},{7,23},{8,24},{9,... | collective-permute-start | bytes 2752520 | tf_op jit(solution)/shard_map/ppermute | solution.py:35
  39.1 30.8 %collective-permute-start.8 = (bf16[256,1792]{1,0:T(8,128)(2,1)S(1)}, bf16[256,1792]{1,0:T(8,128)(2,1)S(1)}, u32[]{:S(2)}, u32[]{:S(2)}) collective-permute-start(bf16[256,1792]{1,0:T(8,128)(2,1)S(1)} %collective-permute-done.3), channel_id=1, source_target_pairs={{64,128},{65,1},{66,130},{67,3},{68,132},{69,5},{70,134},{71,7},{7... | collective-permute-start | bytes 2752520 | tf_op jit(solution)/shard_map/ppermute | solution.py:35
  40.4 50.3 %collective-permute-start.9 = (bf16[256,1792]{1,0:T(8,128)(2,1)S(1)}, bf16[256,1792]{1,0:T(8,128)(2,1)S(1)}, u32[]{:S(2)}, u32[]{:S(2)}) collective-permute-start(bf16[256,1792]{1,0:T(8,128)(2,1)S(1)} %collective-permute-done.3), channel_id=1, source_target_pairs={{64,192},{66,194},{68,196},{70,198},{72,200},{74,202},{76,204},{78... | collective-permute-start | bytes 2752520 | tf_op jit(solution)/shard_map/ppermute | solution.py:35
  58.9 39.1 %collective-permute-start.4 = (f32[256,512]{1,0:T(8,128)S(1)}, f32[256,512]{1,0:T(8,128)S(1)}, u32[]{:S(2)}, u32[]{:S(2)}) collective-permute-start(f32[256,512]{1,0:T(8,128)S(1)} %fusion.3), channel_id=1, source_target_pairs={{0,4},{1,5},{2,6},{3,7},{4,0},{5,1},{6,2},{7,3},{8,12},{9,13},{10,... | collective-permute-start | bytes 1572872 | tf_op jit(solution)/shard_map/ppermute | solution.py:35
  62.0 41.0 %collective-permute-start.5 = (f32[256,512]{1,0:T(8,128)S(1)}, f32[256,512]{1,0:T(8,128)S(1)}, u32[]{:S(2)}, u32[]{:S(2)}) collective-permute-start(f32[256,512]{1,0:T(8,128)S(1)} %fusion.5), channel_id=1, source_target_pairs={{0,8},{1,9},{2,10},{3,11},{4,12},{5,13},{6,14},{7,15},{8,0},{9,1},... | collective-permute-start | bytes 1572872 | tf_op jit(solution)/shard_map/ppermute | solution.py:35
  65.3 37.7 %collective-permute-start.6 = (f32[256,512]{1,0:T(8,128)S(1)}, f32[256,512]{1,0:T(8,128)S(1)}, u32[]{:S(2)}, u32[]{:S(2)}) collective-permute-start(f32[256,512]{1,0:T(8,128)S(1)} %fusion.7), channel_id=1, source_target_pairs={{0,12},{1,13},{2,14},{3,15},{4,8},{5,9},{6,10},{7,11},{8,4},{9,5},... | collective-permute-start | bytes 1572872 | tf_op jit(solution)/shard_map/ppermute | solution.py:35
  91.4 16.3 %collective-permute-start.10 = (f32[256,512]{1,0:T(8,128)S(1)}, f32[256,512]{1,0:T(8,128)S(1)}, u32[]{:S(2)}, u32[]{:S(2)}) collective-permute-start(f32[256,512]{1,0:T(8,128)S(1)} %fusion.2), channel_id=1, source_target_pairs={{1,5},{3,7},{5,1},{7,3},{9,13},{11,15},{13,9},{15,11},{17,21},{19,... | collective-permute-start | bytes 1572872 | tf_op jit(solution)/shard_map/ppermute | solution.py:35
  94.5 13.2 %collective-permute-start.11 = (f32[256,512]{1,0:T(8,128)S(1)}, f32[256,512]{1,0:T(8,128)S(1)}, u32[]{:S(2)}, u32[]{:S(2)}) collective-permute-start(f32[256,512]{1,0:T(8,128)S(1)} %fusion.4), channel_id=1, source_target_pairs={{1,9},{3,11},{5,13},{7,15},{9,1},{11,3},{13,5},{15,7},{17,25},{19,... | collective-permute-start | bytes 1572872 | tf_op jit(solution)/shard_map/ppermute | solution.py:35
  98.0 14.5 %collective-permute-start.12 = (f32[256,512]{1,0:T(8,128)S(1)}, f32[256,512]{1,0:T(8,128)S(1)}, u32[]{:S(2)}, u32[]{:S(2)}) collective-permute-start(f32[256,512]{1,0:T(8,128)S(1)} %fusion.6), channel_id=1, source_target_pairs={{1,13},{3,15},{5,9},{7,11},{9,5},{11,7},{13,1},{15,3},{17,29},{19,... | collective-permute-start | bytes 1572872 | tf_op jit(solution)/shard_map/ppermute | solution.py:35
  103.8 12.7 %collective-permute-start.7 = (f32[3,128,256]{2,1,0:T(8,128)S(1)}, f32[3,128,256]{2,1,0:T(8,128)S(1)}, u32[]{:S(2)}, u32[]{:S(2)}) collective-permute-start(f32[3,128,256]{2,1,0:T(8,128)S(1)} %get-tuple-element.11), channel_id=1, source_target_pairs={{0,2},{1,3},{2,0},{3,1},{4,6},{5,7},{6,4},{7,5},{8,10},{9,11},{10,... | collective-permute-start | bytes 1179656 | tf_op jit(solution)/shard_map/ppermute | solution.py:35
  113.3 9.9 %collective-permute-start.13 = (f32[4,128,256]{2,1,0:T(8,128)S(1)}, f32[4,128,256]{2,1,0:T(8,128)S(1)}, u32[]{:S(2)}, u32[]{:S(2)}) collective-permute-start(f32[4,128,256]{2,1,0:T(8,128)S(1)} %get-tuple-element.13), channel_id=1, source_target_pairs={{1,3},{3,1},{5,7},{7,5},{9,11},{11,9},{13,15},{15,13},{17,19},{19,... | collective-permute-start | bytes 1572872 | tf_op jit(solution)/shard_map/ppermute | solution.py:35
  116.5 26.5 %copy-start.1 = (f32[1,64,8]{1,2,0:T(8,128)S(1)}, f32[1,64,8]{1,2,0:T(8,128)}, u32[]{:S(2)}) copy-start(f32[1,64,8]{1,2,0:T(8,128)} %param.5) | copy-start | bytes 6148
  116.5 27.6 %copy-start = (bf16[1,64,1024]{2,1,0:T(8,128)(2,1)S(1)}, bf16[1,64,1024]{2,1,0:T(8,128)(2,1)}, u32[]{:S(2)}) copy-start(bf16[1,64,1024]{2,1,0:T(8,128)(2,1)} %param.4) | copy-start | bytes 393220
  116.6 10.4 %collective-permute-start.14 = (f32[128,256]{1,0:T(8,128)S(1)}, f32[128,256]{1,0:T(8,128)S(1)}, u32[]{:S(2)}, u32[]{:S(2)}) collective-permute-start(f32[128,256]{1,0:T(8,128)S(1)} %get-tuple-element.29), channel_id=1, source_target_pairs={{1,65},{3,67},{5,81},{7,83},{9,97},{11,99},{13,113},{15,115},{17,6... | collective-permute-start | bytes 393224 | tf_op jit(solution)/shard_map/ppermute | solution.py:35
  123.2 4.3 %collective-permute-start.15 = (f32[128,256]{1,0:T(8,128)S(1)}, f32[128,256]{1,0:T(8,128)S(1)}, u32[]{:S(2)}, u32[]{:S(2)}) collective-permute-start(f32[128,256]{1,0:T(8,128)S(1)} %get-tuple-element.25), channel_id=1, source_target_pairs={{1,129},{3,131},{5,145},{7,147},{9,161},{11,163},{13,177},{15,179}... | collective-permute-start | bytes 393224 | tf_op jit(solution)/shard_map/ppermute | solution.py:35
  125.6 3.3 %collective-permute-start.16 = (f32[128,256]{1,0:T(8,128)S(1)}, f32[128,256]{1,0:T(8,128)S(1)}, u32[]{:S(2)}, u32[]{:S(2)}) collective-permute-start(f32[128,256]{1,0:T(8,128)S(1)} %get-tuple-element.24), channel_id=1, source_target_pairs={{1,193},{3,195},{5,209},{7,211},{9,225},{11,227},{13,241},{15,243}... | collective-permute-start | bytes 393224 | tf_op jit(solution)/shard_map/ppermute | solution.py:35
  129.5 14.6 %collective-permute-start.17 = (f32[4,64,256]{2,1,0:T(8,128)S(1)}, f32[4,64,256]{2,1,0:T(8,128)S(1)}, u32[]{:S(2)}, u32[]{:S(2)}) collective-permute-start(f32[4,64,256]{2,1,0:T(8,128)S(1)} %get-tuple-element.15), channel_id=1, source_target_pairs={{0,1},{1,0},{2,3},{3,2},{4,5},{5,4},{6,7},{7,6},{8,9},{9,8},{10,11... | collective-permute-start | bytes 786440 | tf_op jit(solution)/shard_map/ppermute | solution.py:35

commit v7 on v6

--- a/solution.py
+++ b/solution.py
@@ -193,7 +193,7 @@
         parts = products(rows, [passing[step] for step in steps])
         valid = lambda at, steps=steps: reach(at) >= steps[0]
         parts[1:] = [
-            permute(parts[d], lambda at, d=d: dict(x=at["x"] ^ d), valid) for d in (1, 2, 3)
+            permute(parts[d], lambda at, d=d: dict(x=at["x"] ^ d), valid) for d in (2, 1, 3)
         ]
         far = [k for k, step in enumerate(steps) if step]
         keep, give = halves(where, far, parts)

time: 147 us -> 147 us (level)
  the two profiles are of different devices: /device:TPU:7 before, /device:TPU:5 now
where the time goes in v7:
time: 147 us; the launch traced here: 146 us
  waiting for transfers between devices  70.9 us (48%)
  starting transfers between devices  62.1 us (42%)
  matrix products  5.33 us (4%)
  Pallas kernels  3.96 us (3%)
  other arithmetic  1.87 us (1%)
    ppermute x18, waiting for transfers between devices, permute(): return lax.ppermute(array, AXES, pairs)  70.9 us
    ppermute x18, starting transfers between devices, permute(): return lax.ppermute(array, AXES, pairs)  62.1 us
    dot_general x8, matrix products, products(): lax.dot_general(row, cols, (((1,), (1,)), ((), ())), preferred_element_ty...  5.33 us
    pallas_call x4, Pallas kernels, call(): pl.pallas_call(kernel, out_shape=outs, in_specs=in_specs, out_specs=[VMEM...  3.96 us
  transfers between devices with their start and end apart: 18, of which 9 were waited for; matrix products, arithmetic and copies ran while one was open for 5% of the time, Pallas kernels for 1%

profile of v7, /device:TPU:5, one launch (start us, length us, event | category | flops | bytes accessed | tf_op | source)
XLA Modules:
  0.0 146.1 jit_solution(13507620287723411609)
XLA Ops:
  0.6 3.5 %collective-permute-start = (bf16[256,1792]{1,0:T(8,128)(2,1)}, bf16[256,1792]{1,0:T(8,128)(2,1)S(1)}, u32[]{:S(2)}, u32[]{:S(2)}) collective-permute-start(bf16[256,1792]{1,0:T(8,128)(2,1)} %param.3), channel_id=1, source_target_pairs={{0,32},{1,33},{2,34},{3,35},{4,36},{5,37},{6,38},{7,39},{8,40},{9,... | collective-permute-start | bytes 2752520 | tf_op jit(solution)/shard_map/ppermute | solution.py:35
  4.2 1.3 collective-permute-start.3
  5.5 4.8 %collective-permute-start.2 = (bf16[256,1792]{1,0:T(8,128)(2,1)}, bf16[256,1792]{1,0:T(8,128)(2,1)S(1)}, u32[]{:S(2)}, u32[]{:S(2)}) collective-permute-start(bf16[256,1792]{1,0:T(8,128)(2,1)} %param.3), channel_id=1, source_target_pairs={{0,16},{1,17},{2,18},{3,19},{4,20},{5,21},{6,22},{7,23},{8,24},{9,... | collective-permute-start | bytes 2752520 | tf_op jit(solution)/shard_map/ppermute | solution.py:35
  10.3 23.8 %collective-permute-done = bf16[256,1792]{1,0:T(8,128)(2,1)S(1)} collective-permute-done((bf16[256,1792]{1,0:T(8,128)(2,1)}, bf16[256,1792]{1,0:T(8,128)(2,1)S(1)}, u32[]{:S(2)}, u32[]{:S(2)}) %collective-permute-start) | collective-permute-done | bytes 917536 | tf_op jit(solution)/shard_map/ppermute | solution.py:35
  34.2 4.8 %collective-permute-start.1 = (bf16[256,1792]{1,0:T(8,128)(2,1)S(1)}, bf16[256,1792]{1,0:T(8,128)(2,1)S(1)}, u32[]{:S(2)}, u32[]{:S(2)}) collective-permute-start(bf16[256,1792]{1,0:T(8,128)(2,1)S(1)} %collective-permute-done), channel_id=1, source_target_pairs={{0,16},{1,17},{2,18},{3,19},{4,20},{5,21},{6,22},{7,23},{8,24},{9,... | collective-permute-start | bytes 2752520 | tf_op jit(solution)/shard_map/ppermute | solution.py:35
  39.0 0.1 pad_add_fusion.where
  39.1 1.3 collective-permute-start.8
  40.4 1.3 collective-permute-start.9
  41.7 1.5 %broadcast_select_fusion = (bf16[256,1792]{1,0:T(8,128)(2,1)S(1)}, bf16[256,1792]{1,0:T(8,128)(2,1)S(1)}, bf16[512,1792]{1,0:T(8,128)(2,1)S(1)}) fusion(bf16[256,1792]{1,0:T(8,128)(2,1)} %param.3, bf16[256,1792]{1,0:T(8,128)(2,1)S(1)} %collective-permute-done.2, pred[]{:T(512)S(6)} %eq.9), kind=kLoop, calls=%fused_computation | loop fusion | flops 917503 | bytes 4587521 | tf_op jit(solution)/shard_map/jit(_where)/select_n | solution.py:162
  43.2 0.1 constant_dynamic-update-slice_fusion
  43.3 14.8 %collective-permute-done.1 = bf16[256,1792]{1,0:T(8,128)(2,1)S(1)} collective-permute-done((bf16[256,1792]{1,0:T(8,128)(2,1)S(1)}, bf16[256,1792]{1,0:T(8,128)(2,1)S(1)}, u32[]{:S(2)}, u32[]{:S(2)}) %collective-permute-start.1) | collective-permute-done | bytes 917536 | tf_op jit(solution)/shard_map/ppermute | solution.py:35
  58.1 0.1 broadcast_select_fusion.1
  58.2 0.7 fusion.3
  58.9 2.1 %collective-permute-start.4 = (f32[256,512]{1,0:T(8,128)S(1)}, f32[256,512]{1,0:T(8,128)S(1)}, u32[]{:S(2)}, u32[]{:S(2)}) collective-permute-start(f32[256,512]{1,0:T(8,128)S(1)} %fusion.3), channel_id=1, source_target_pairs={{0,8},{1,9},{2,10},{3,11},{4,12},{5,13},{6,14},{7,15},{8,0},{9,1},... | collective-permute-start | bytes 1572872 | tf_op jit(solution)/shard_map/ppermute | solution.py:35
  60.9 0.7 fusion.5
  61.6 3.8 %collective-permute-start.5 = (f32[256,512]{1,0:T(8,128)S(1)}, f32[256,512]{1,0:T(8,128)S(1)}, u32[]{:S(2)}, u32[]{:S(2)}) collective-permute-start(f32[256,512]{1,0:T(8,128)S(1)} %fusion.5), channel_id=1, source_target_pairs={{0,4},{1,5},{2,6},{3,7},{4,0},{5,1},{6,2},{7,3},{8,12},{9,13},{10,... | collective-permute-start | bytes 1572872 | tf_op jit(solution)/shard_map/ppermute | solution.py:35
  65.4 0.7 fusion.7
  66.1 3.1 %collective-permute-start.6 = (f32[256,512]{1,0:T(8,128)S(1)}, f32[256,512]{1,0:T(8,128)S(1)}, u32[]{:S(2)}, u32[]{:S(2)}) collective-permute-start(f32[256,512]{1,0:T(8,128)S(1)} %fusion.7), channel_id=1, source_target_pairs={{0,12},{1,13},{2,14},{3,15},{4,8},{5,9},{6,10},{7,11},{8,4},{9,5},... | collective-permute-start | bytes 1572872 | tf_op jit(solution)/shard_map/ppermute | solution.py:35
  69.2 0.1 constant_dynamic-update-slice_fusion.3
  69.3 21.4 %collective-permute-done.9 = bf16[256,1792]{1,0:T(8,128)(2,1)S(1)} collective-permute-done((bf16[256,1792]{1,0:T(8,128)(2,1)S(1)}, bf16[256,1792]{1,0:T(8,128)(2,1)S(1)}, u32[]{:S(2)}, u32[]{:S(2)}) %collective-permute-start.9) | collective-permute-done | bytes 917536 | tf_op jit(solution)/shard_map/ppermute | solution.py:35
  90.6 0.1 constant_dynamic-update-slice_fusion.2
  90.7 0.7 fusion.2
  91.4 2.1 %collective-permute-start.10 = (f32[256,512]{1,0:T(8,128)S(1)}, f32[256,512]{1,0:T(8,128)S(1)}, u32[]{:S(2)}, u32[]{:S(2)}) collective-permute-start(f32[256,512]{1,0:T(8,128)S(1)} %fusion.2), channel_id=1, source_target_pairs={{1,9},{3,11},{5,13},{7,15},{9,1},{11,3},{13,5},{15,7},{17,25},{19,... | collective-permute-start | bytes 1572872 | tf_op jit(solution)/shard_map/ppermute | solution.py:35
  93.5 0.7 fusion.4
  94.2 3.7 %collective-permute-start.11 = (f32[256,512]{1,0:T(8,128)S(1)}, f32[256,512]{1,0:T(8,128)S(1)}, u32[]{:S(2)}, u32[]{:S(2)}) collective-permute-start(f32[256,512]{1,0:T(8,128)S(1)} %fusion.4), channel_id=1, source_target_pairs={{1,5},{3,7},{5,1},{7,3},{9,13},{11,15},{13,9},{15,11},{17,21},{19,... | collective-permute-start | bytes 1572872 | tf_op jit(solution)/shard_map/ppermute | solution.py:35
  97.9 0.7 fusion.6
  98.6 3.1 %collective-permute-start.12 = (f32[256,512]{1,0:T(8,128)S(1)}, f32[256,512]{1,0:T(8,128)S(1)}, u32[]{:S(2)}, u32[]{:S(2)}) collective-permute-start(f32[256,512]{1,0:T(8,128)S(1)} %fusion.6), channel_id=1, source_target_pairs={{1,13},{3,15},{5,9},{7,11},{9,5},{11,7},{13,1},{15,3},{17,29},{19,... | collective-permute-start | bytes 1572872 | tf_op jit(solution)/shard_map/ppermute | solution.py:35
  101.8 0.7 fusion.1.first
  102.5 0.7 halves.2
  103.2 3.2 %collective-permute-start.7 = (f32[3,128,256]{2,1,0:T(8,128)S(1)}, f32[3,128,256]{2,1,0:T(8,128)S(1)}, u32[]{:S(2)}, u32[]{:S(2)}) collective-permute-start(f32[3,128,256]{2,1,0:T(8,128)S(1)} %get-tuple-element.11), channel_id=1, source_target_pairs={{0,2},{1,3},{2,0},{3,1},{4,6},{5,7},{6,4},{7,5},{8,10},{9,11},{10,... | collective-permute-start | bytes 1179656 | tf_op jit(solution)/shard_map/ppermute | solution.py:35
  106.4 0.7 fusion.first
  107.1 0.4 collective-permute-done.11.third
  107.5 1.0 collective-permute-done.12.fourth
  108.5 0.8 halves.3
  109.3 3.2 %collective-permute-start.13 = (f32[4,128,256]{2,1,0:T(8,128)S(1)}, f32[4,128,256]{2,1,0:T(8,128)S(1)}, u32[]{:S(2)}, u32[]{:S(2)}) collective-permute-start(f32[4,128,256]{2,1,0:T(8,128)S(1)} %get-tuple-element.13), channel_id=1, source_target_pairs={{1,3},{3,1},{5,7},{7,5},{9,11},{11,9},{13,15},{15,13},{17,19},{19,... | collective-permute-start | bytes 1572872 | tf_op jit(solution)/shard_map/ppermute | solution.py:35
  112.6 1.3 collective-permute-start.14
  113.9 6.4 %collective-permute-done.13 = f32[4,128,256]{2,1,0:T(8,128)S(1)} collective-permute-done((f32[4,128,256]{2,1,0:T(8,128)S(1)}, f32[4,128,256]{2,1,0:T(8,128)S(1)}, u32[]{:S(2)}, u32[]{:S(2)}) %collective-permute-start.13) | collective-permute-done | bytes 524320 | tf_op jit(solution)/shard_map/ppermute | solution.py:35
  120.4 0.1 fusion.8
  120.5 1.3 collective-permute-start.15
  121.8 1.3 collective-permute-start.16
  123.1 0.6 collective-permute-done.15.refs_5_
  123.7 1.4 collective-permute-done.16.refs_6_
  125.1 0.6 strips.1
  125.7 16.8 %collective-permute-start.17 = (f32[4,64,256]{2,1,0:T(8,128)S(1)}, f32[4,64,256]{2,1,0:T(8,128)S(1)}, u32[]{:S(2)}, u32[]{:S(2)}) collective-permute-start(f32[4,64,256]{2,1,0:T(8,128)S(1)} %get-tuple-element.15), channel_id=1, source_target_pairs={{0,1},{1,0},{2,3},{3,2},{4,5},{5,4},{6,7},{7,6},{8,9},{9,8},{10,11... | collective-permute-start | bytes 786440 | tf_op jit(solution)/shard_map/ppermute | solution.py:35
  142.5 0.1 copy.5
  142.5 1.0 collective-permute-done.17.other
  143.6 1.9 %refresh.1 = (bf16[64,1024]{1,0:T(8,128)(2,1)}, f32[64,8]{1,0:T(8,128)S(1)}) custom-call(s32[4]{0:T(128)S(1)} %pad_add_fusion.where, f32[4,64,256]{2,1,0:T(8,128)S(1)} %get-tuple-element.14.mine, f32[4,64,256]{2,1,0:T(8,128)S(1)} %collective-permute-done.17.other, bf16[64,1024]{1,0:T(8,128)(2,1)S(1)} %bitcast.31, f32[64,8]{1,0:T(8,128)S(1)} %bitcast.30), custom_call_target="tpu_custom_call" | custom-call | flops 16777216 | bytes 790544 | tf_op jit(solution)/shard_map/refresh/pallas_call | solution.py:49
  145.4 0.7 copy.6
  (14 shorter events, 0.1 us)
Async XLA Ops:
  0.6 33.5 %collective-permute-start = (bf16[256,1792]{1,0:T(8,128)(2,1)}, bf16[256,1792]{1,0:T(8,128)(2,1)S(1)}, u32[]{:S(2)}, u32[]{:S(2)}) collective-permute-start(bf16[256,1792]{1,0:T(8,128)(2,1)} %param.3), channel_id=1, source_target_pairs={{0,32},{1,33},{2,34},{3,35},{4,36},{5,37},{6,38},{7,39},{8,40},{9,... | collective-permute-start | bytes 2752520 | tf_op jit(solution)/shard_map/ppermute | solution.py:35
  4.2 34.9 %collective-permute-start.3 = (bf16[256,1792]{1,0:T(8,128)(2,1)}, bf16[256,1792]{1,0:T(8,128)(2,1)S(1)}, u32[]{:S(2)}, u32[]{:S(2)}) collective-permute-start(bf16[256,1792]{1,0:T(8,128)(2,1)} %param.3), channel_id=1, source_target_pairs={{0,64},{2,66},{4,68},{6,70},{8,72},{10,74},{12,76},{14,78},{16,80}... | collective-permute-start | bytes 2752520 | tf_op jit(solution)/shard_map/ppermute | solution.py:35
  5.5 36.2 %collective-permute-start.2 = (bf16[256,1792]{1,0:T(8,128)(2,1)}, bf16[256,1792]{1,0:T(8,128)(2,1)S(1)}, u32[]{:S(2)}, u32[]{:S(2)}) collective-permute-start(bf16[256,1792]{1,0:T(8,128)(2,1)} %param.3), channel_id=1, source_target_pairs={{0,16},{1,17},{2,18},{3,19},{4,20},{5,21},{6,22},{7,23},{8,24},{9,... | collective-permute-start | bytes 2752520 | tf_op jit(solution)/shard_map/ppermute | solution.py:35
  34.2 23.9 %collective-permute-start.1 = (bf16[256,1792]{1,0:T(8,128)(2,1)S(1)}, bf16[256,1792]{1,0:T(8,128)(2,1)S(1)}, u32[]{:S(2)}, u32[]{:S(2)}) collective-permute-start(bf16[256,1792]{1,0:T(8,128)(2,1)S(1)} %collective-permute-done), channel_id=1, source_target_pairs={{0,16},{1,17},{2,18},{3,19},{4,20},{5,21},{6,22},{7,23},{8,24},{9,... | collective-permute-start | bytes 2752520 | tf_op jit(solution)/shard_map/ppermute | solution.py:35
  39.1 30.1 %collective-permute-start.8 = (bf16[256,1792]{1,0:T(8,128)(2,1)S(1)}, bf16[256,1792]{1,0:T(8,128)(2,1)S(1)}, u32[]{:S(2)}, u32[]{:S(2)}) collective-permute-start(bf16[256,1792]{1,0:T(8,128)(2,1)S(1)} %collective-permute-done.3), channel_id=1, source_target_pairs={{64,128},{65,1},{66,130},{67,3},{68,132},{69,5},{70,134},{71,7},{7... | collective-permute-start | bytes 2752520 | tf_op jit(solution)/shard_map/ppermute | solution.py:35
  40.4 50.3 %collective-permute-start.9 = (bf16[256,1792]{1,0:T(8,128)(2,1)S(1)}, bf16[256,1792]{1,0:T(8,128)(2,1)S(1)}, u32[]{:S(2)}, u32[]{:S(2)}) collective-permute-start(bf16[256,1792]{1,0:T(8,128)(2,1)S(1)} %collective-permute-done.3), channel_id=1, source_target_pairs={{64,192},{66,194},{68,196},{70,198},{72,200},{74,202},{76,204},{78... | collective-permute-start | bytes 2752520 | tf_op jit(solution)/shard_map/ppermute | solution.py:35
  58.9 39.7 %collective-permute-start.4 = (f32[256,512]{1,0:T(8,128)S(1)}, f32[256,512]{1,0:T(8,128)S(1)}, u32[]{:S(2)}, u32[]{:S(2)}) collective-permute-start(f32[256,512]{1,0:T(8,128)S(1)} %fusion.3), channel_id=1, source_target_pairs={{0,8},{1,9},{2,10},{3,11},{4,12},{5,13},{6,14},{7,15},{8,0},{9,1},... | collective-permute-start | bytes 1572872 | tf_op jit(solution)/shard_map/ppermute | solution.py:35
  61.6 40.8 %collective-permute-start.5 = (f32[256,512]{1,0:T(8,128)S(1)}, f32[256,512]{1,0:T(8,128)S(1)}, u32[]{:S(2)}, u32[]{:S(2)}) collective-permute-start(f32[256,512]{1,0:T(8,128)S(1)} %fusion.5), channel_id=1, source_target_pairs={{0,4},{1,5},{2,6},{3,7},{4,0},{5,1},{6,2},{7,3},{8,12},{9,13},{10,... | collective-permute-start | bytes 1572872 | tf_op jit(solution)/shard_map/ppermute | solution.py:35
  66.1 36.3 %collective-permute-start.6 = (f32[256,512]{1,0:T(8,128)S(1)}, f32[256,512]{1,0:T(8,128)S(1)}, u32[]{:S(2)}, u32[]{:S(2)}) collective-permute-start(f32[256,512]{1,0:T(8,128)S(1)} %fusion.7), channel_id=1, source_target_pairs={{0,12},{1,13},{2,14},{3,15},{4,8},{5,9},{6,10},{7,11},{8,4},{9,5},... | collective-permute-start | bytes 1572872 | tf_op jit(solution)/shard_map/ppermute | solution.py:35
  91.4 15.7 %collective-permute-start.10 = (f32[256,512]{1,0:T(8,128)S(1)}, f32[256,512]{1,0:T(8,128)S(1)}, u32[]{:S(2)}, u32[]{:S(2)}) collective-permute-start(f32[256,512]{1,0:T(8,128)S(1)} %fusion.2), channel_id=1, source_target_pairs={{1,9},{3,11},{5,13},{7,15},{9,1},{11,3},{13,5},{15,7},{17,25},{19,... | collective-permute-start | bytes 1572872 | tf_op jit(solution)/shard_map/ppermute | solution.py:35
  94.2 13.3 %collective-permute-start.11 = (f32[256,512]{1,0:T(8,128)S(1)}, f32[256,512]{1,0:T(8,128)S(1)}, u32[]{:S(2)}, u32[]{:S(2)}) collective-permute-start(f32[256,512]{1,0:T(8,128)S(1)} %fusion.4), channel_id=1, source_target_pairs={{1,5},{3,7},{5,1},{7,3},{9,13},{11,15},{13,9},{15,11},{17,21},{19,... | collective-permute-start | bytes 1572872 | tf_op jit(solution)/shard_map/ppermute | solution.py:35
  98.6 9.9 %collective-permute-start.12 = (f32[256,512]{1,0:T(8,128)S(1)}, f32[256,512]{1,0:T(8,128)S(1)}, u32[]{:S(2)}, u32[]{:S(2)}) collective-permute-start(f32[256,512]{1,0:T(8,128)S(1)} %fusion.6), channel_id=1, source_target_pairs={{1,13},{3,15},{5,9},{7,11},{9,5},{11,7},{13,1},{15,3},{17,29},{19,... | collective-permute-start | bytes 1572872 | tf_op jit(solution)/shard_map/ppermute | solution.py:35
  103.2 9.4 %collective-permute-start.7 = (f32[3,128,256]{2,1,0:T(8,128)S(1)}, f32[3,128,256]{2,1,0:T(8,128)S(1)}, u32[]{:S(2)}, u32[]{:S(2)}) collective-permute-start(f32[3,128,256]{2,1,0:T(8,128)S(1)} %get-tuple-element.11), channel_id=1, source_target_pairs={{0,2},{1,3},{2,0},{3,1},{4,6},{5,7},{6,4},{7,5},{8,10},{9,11},{10,... | collective-permute-start | bytes 1179656 | tf_op jit(solution)/shard_map/ppermute | solution.py:35
  109.3 11.0 %collective-permute-start.13 = (f32[4,128,256]{2,1,0:T(8,128)S(1)}, f32[4,128,256]{2,1,0:T(8,128)S(1)}, u32[]{:S(2)}, u32[]{:S(2)}) collective-permute-start(f32[4,128,256]{2,1,0:T(8,128)S(1)} %get-tuple-element.13), channel_id=1, source_target_pairs={{1,3},{3,1},{5,7},{7,5},{9,11},{11,9},{13,15},{15,13},{17,19},{19,... | collective-permute-start | bytes 1572872 | tf_op jit(solution)/shard_map/ppermute | solution.py:35
  112.6 29.9 %copy-start.1 = (f32[1,64,8]{1,2,0:T(8,128)S(1)}, f32[1,64,8]{1,2,0:T(8,128)}, u32[]{:S(2)}) copy-start(f32[1,64,8]{1,2,0:T(8,128)} %param.5) | copy-start | bytes 6148
  112.6 31.0 %copy-start = (bf16[1,64,1024]{2,1,0:T(8,128)(2,1)S(1)}, bf16[1,64,1024]{2,1,0:T(8,128)(2,1)}, u32[]{:S(2)}) copy-start(bf16[1,64,1024]{2,1,0:T(8,128)(2,1)} %param.4) | copy-start | bytes 393220
  112.6 10.4 %collective-permute-start.14 = (f32[128,256]{1,0:T(8,128)S(1)}, f32[128,256]{1,0:T(8,128)S(1)}, u32[]{:S(2)}, u32[]{:S(2)}) collective-permute-start(f32[128,256]{1,0:T(8,128)S(1)} %get-tuple-element.29), channel_id=1, source_target_pairs={{1,65},{3,67},{5,81},{7,83},{9,97},{11,99},{13,113},{15,115},{17,6... | collective-permute-start | bytes 393224 | tf_op jit(solution)/shard_map/ppermute | solution.py:35
  120.5 3.2 %collective-permute-start.15 = (f32[128,256]{1,0:T(8,128)S(1)}, f32[128,256]{1,0:T(8,128)S(1)}, u32[]{:S(2)}, u32[]{:S(2)}) collective-permute-start(f32[128,256]{1,0:T(8,128)S(1)} %get-tuple-element.25), channel_id=1, source_target_pairs={{1,129},{3,131},{5,145},{7,147},{9,161},{11,163},{13,177},{15,179}... | collective-permute-start | bytes 393224 | tf_op jit(solution)/shard_map/ppermute | solution.py:35
  121.8 3.3 %collective-permute-start.16 = (f32[128,256]{1,0:T(8,128)S(1)}, f32[128,256]{1,0:T(8,128)S(1)}, u32[]{:S(2)}, u32[]{:S(2)}) collective-permute-start(f32[128,256]{1,0:T(8,128)S(1)} %get-tuple-element.24), channel_id=1, source_target_pairs={{1,193},{3,195},{5,209},{7,211},{9,225},{11,227},{13,241},{15,243}... | collective-permute-start | bytes 393224 | tf_op jit(solution)/shard_map/ppermute | solution.py:35
  125.7 17.9 %collective-permute-start.17 = (f32[4,64,256]{2,1,0:T(8,128)S(1)}, f32[4,64,256]{2,1,0:T(8,128)S(1)}, u32[]{:S(2)}, u32[]{:S(2)}) collective-permute-start(f32[4,64,256]{2,1,0:T(8,128)S(1)} %get-tuple-element.15), channel_id=1, source_target_pairs={{0,1},{1,0},{2,3},{3,2},{4,5},{5,4},{6,7},{7,6},{8,9},{9,8},{10,11... | collective-permute-start | bytes 786440 | tf_op jit(solution)/shard_map/ppermute | solution.py:35

commit v8 on v7

--- a/solution.py
+++ b/solution.py
@@ -39,8 +39,12 @@
     return at["g"] if at["c"] == 0 else SUPERS - 1 - at["g"]
 
 
+def way(at):
+    return 1 if at["c"] == 0 else -1
+
+
 def onward(at):
-    return dict(g=at["g"] + (1 if at["c"] == 0 else -1))
+    return dict(g=at["g"] + way(at))
 
 
 def call(kernel, name, outs, flops, *operands):
@@ -73,7 +77,7 @@
 
 def halves_kernel(far, where, first, second, third, fourth, keep, give):
     half, size = keep.shape[1:]
-    upper = where[1] == 1
+    upper = where[0] == 1
     total = first[...] + second[...] + third[...] + fourth[...]
     totals = [total[:, k : k + size] for k in range(0, total.shape[1], size)]
     for k, total in enumerate(totals + [totals[k].T for k in far]):
@@ -89,26 +93,30 @@
     )
 
 
-def strips_kernel(where, *refs):
-    own, across, keep, give = refs[:4], (None, *refs[4:7]), refs[7], refs[8]
+def strips_kernel(where, own_0, own_1, across_1, own_late, across_late, keep, give):
     half = keep.shape[1]
-    second = where[2] == 1
-    back = own[3][...] + across[1][...], own[1][...] + across[3][...]
+    second = where[1] == 1
+    reached = jnp.where(second, SUPERS - 1 - where[2], where[2])
+    own_two, across_two = reached >= 2, reached <= 1
+    none = jnp.zeros_like(own_late)
+    mine, others = own_late[...], across_late[...]
+    forth = own_1[...] + jnp.where(own_two, none, mine)
+    back = across_1[...] + jnp.where(across_two, none, others)
     strips = [
-        own[0][...],
-        jnp.where(second, back[1], back[0]),
-        own[2][...] + across[2][...],
-        jnp.where(second, back[0], back[1]),
+        own_0[...],
+        jnp.where(second, forth, back),
+        jnp.where(own_two, mine, none) + jnp.where(across_two, others, none),
+        jnp.where(second, back, forth),
     ]
     for k, strip in enumerate(strips):
         keep[k] = jnp.where(second, strip[half:], strip[:half])
         give[k] = jnp.where(second, strip[:half], strip[half:])
 
 
-def strips(where, own, across):
-    rows, cols = own[0].shape
+def strips(where, *parts):
+    rows, cols = parts[0].shape
     shape = floats(SUPERS, rows // 2, cols)
-    return call(strips_kernel, "strips", [shape, shape], 0, where, *own, *across)
+    return call(strips_kernel, "strips", [shape, shape], 0, where, *parts)
 
 
 def refresh_kernel(where, mine, other, codes, scales, new_codes, new_scales):
@@ -122,7 +130,7 @@
     per_block = mine.shape[2] // GROUP
     largest = []
     for j in range(SUPERS):
-        offset = (j + SUPERS - where[3]) & (SUPERS - 1)
+        offset = (j + SUPERS - where[2]) & (SUPERS - 1)
         block = mine[offset] + other[offset]
         for k in range(per_block):
             group = j * per_block + k
@@ -164,9 +172,8 @@
 
 def per_device(gradient, left_codes, left_scales):
     dp, tensor = lax.axis_index("dp"), lax.axis_index("tensor")
-    where = jnp.stack(
-        [(tensor >> 2) ^ (dp & 3), (tensor >> 1) & 1, tensor & 1, (dp >> 2) & 3]
-    ).astype(jnp.int32)
+    core, place_no = tensor & 1, (dp >> 2) & 3
+    where = jnp.stack([(tensor >> 1) & 1, core, place_no]).astype(jnp.int32)
 
     z_block = permute(gradient, lambda at: dict(h=at["h"] ^ 2))
     y_block = permute(gradient, lambda at: dict(h=at["h"] ^ 1))
@@ -178,39 +185,42 @@
     s1, s3 = swap_if(turn >> 1 == 1, low[1], high[1])
     rows = [s0, s1, s2, s3]
 
-    passing = [gradient, permute(gradient, onward, lambda at: reach(at) < 3)]
-    passing.append(permute(passing[1], onward, lambda at: 1 <= reach(at) < 3))
-    passing.append(
-        permute(
-            passing[1],
-            lambda at: dict(g=at["g"] + (2 if at["c"] == 0 else -2)),
-            lambda at: reach(at) == 1,
-        )
-    )
-
-    own, across = [None] * SUPERS, [None] * SUPERS
-    for steps in ((0, 1), (2, 3)):
-        parts = products(rows, [passing[step] for step in steps])
-        valid = lambda at, steps=steps: reach(at) >= steps[0]
+    passing = permute(gradient, onward, lambda at: reach(at) < 3)
+    passing, sent = lax.optimization_barrier((passing, gradient))
+    second = permute(passing, onward, lambda at: 1 <= reach(at) < 3)
+    opposite = permute(sent, lambda at: dict(g=SUPERS - 1 - at["g"]), lambda at: reach(at) == 3)
+    reached = jnp.where(core == 0, place_no, SUPERS - 1 - place_no)
+    late = jnp.where(reached >= 2, second, opposite)
+
+    def summed(cols, valid):
+        parts = products(rows, cols)
         parts[1:] = [
             permute(parts[d], lambda at, d=d: dict(x=at["x"] ^ d), valid) for d in (2, 1, 3)
         ]
-        far = [k for k, step in enumerate(steps) if step]
+        return parts
+
+    def settle(parts, far, valid):
         keep, give = halves(where, far, parts)
         came = permute(give, lambda at: dict(yl=at["yl"] ^ 1), valid)
-        for k, step in enumerate(steps):
-            own[step] = keep[k] + came[k]
-        for k, place_no in enumerate(far, len(steps)):
-            step = steps[place_no]
-            across[step] = permute(
-                keep[k] + came[k],
-                lambda at, step=step: dict(
-                    g=at["g"] + (-step if at["c"] == 0 else step), h=at["x"], x=at["h"]
-                ),
-                lambda at, step=step: reach(at) >= step,
-            )
-
-    mine, given = strips(where, own, across[1:])
+        return [keep[k] + came[k] for k in range(keep.shape[0])]
+
+    def back(at):
+        g = at["g"]
+        return dict(g=SUPERS - 1 - g if reach(at) == 0 else g - 2 * way(at), h=at["x"], x=at["h"])
+
+    early = summed([gradient, passing], lambda at: True)
+    late, early[1] = lax.optimization_barrier((late, early[1]))
+    valid = lambda at: reach(at) != 1
+    last = summed([late], valid)
+    last[1], *early = lax.optimization_barrier((last[1], *early))
+    own_0, own_1, across_1 = settle(early, (1,), lambda at: True)
+    across_1 = permute(
+        across_1, lambda at: dict(g=at["g"] - way(at), h=at["x"], x=at["h"]), lambda at: reach(at) > 0
+    )
+    own_late, across_late = settle(last, (0,), valid)
+    across_late = permute(across_late, back, valid)
+
+    mine, given = strips(where, own_0, own_1, across_1, own_late, across_late)
     other = permute(given, lambda at: dict(c=at["c"] ^ 1))
     fresh_codes, fresh_scales = refresh(where, mine, other, left_codes[0], left_scales[0])
     return fresh_codes[None], fresh_scales[None]

time: 147 us -> 147 us (level)
  the two profiles are of different devices: /device:TPU:5 before, /device:TPU:7 now
where the time goes in v8:
time: 147 us; the launch traced here: 146 us
  starting transfers between devices  69 us (47%)
  waiting for transfers between devices  65.1 us (44%)
  matrix products  4.43 us (3%)
  Pallas kernels  3.88 us (3%)
  other arithmetic  1.93 us (1%)
    ppermute x17, starting transfers between devices, permute(): return lax.ppermute(array, AXES, pairs)  69 us
    ppermute x17, waiting for transfers between devices, permute(): return lax.ppermute(array, AXES, pairs)  65.1 us
    dot_general x8, matrix products, products(): lax.dot_general(row, cols, (((1,), (1,)), ((), ())), preferred_element_ty...  4.43 us
    pallas_call x4, Pallas kernels, call(): pl.pallas_call(kernel, out_shape=outs, in_specs=in_specs, out_specs=[VMEM...  3.88 us
  transfers between devices with their start and end apart: 17, of which 8 were waited for; matrix products, arithmetic and copies ran while one was open for 4% of the time, Pallas kernels for 1%

profile of v8, /device:TPU:7, one launch (start us, length us, event | category | flops | bytes accessed | tf_op | source)
XLA Modules:
  0.0 146.1 jit_solution(14857856496845492373)
XLA Ops:
  0.6 3.5 %collective-permute-start.1 = (bf16[256,1792]{1,0:T(8,128)(2,1)}, bf16[256,1792]{1,0:T(8,128)(2,1)S(1)}, u32[]{:S(2)}, u32[]{:S(2)}) collective-permute-start(bf16[256,1792]{1,0:T(8,128)(2,1)} %param.3), channel_id=1, source_target_pairs={{0,32},{1,33},{2,34},{3,35},{4,36},{5,37},{6,38},{7,39},{8,40},{9,... | collective-permute-start | bytes 2752520 | tf_op jit(solution)/shard_map/ppermute | solution.py:35
  4.2 1.3 collective-permute-start.3
  5.5 4.8 %collective-permute-start = (bf16[256,1792]{1,0:T(8,128)(2,1)}, bf16[256,1792]{1,0:T(8,128)(2,1)S(1)}, u32[]{:S(2)}, u32[]{:S(2)}) collective-permute-start(bf16[256,1792]{1,0:T(8,128)(2,1)} %param.3), channel_id=1, source_target_pairs={{0,16},{1,17},{2,18},{3,19},{4,20},{5,21},{6,22},{7,23},{8,24},{9,... | collective-permute-start | bytes 2752520 | tf_op jit(solution)/shard_map/ppermute | solution.py:35
  10.3 23.8 %collective-permute-done.1 = bf16[256,1792]{1,0:T(8,128)(2,1)S(1)} collective-permute-done((bf16[256,1792]{1,0:T(8,128)(2,1)}, bf16[256,1792]{1,0:T(8,128)(2,1)S(1)}, u32[]{:S(2)}, u32[]{:S(2)}) %collective-permute-start.1) | collective-permute-done | bytes 917536 | tf_op jit(solution)/shard_map/ppermute | solution.py:35
  34.2 4.8 %collective-permute-start.2 = (bf16[256,1792]{1,0:T(8,128)(2,1)S(1)}, bf16[256,1792]{1,0:T(8,128)(2,1)S(1)}, u32[]{:S(2)}, u32[]{:S(2)}) collective-permute-start(bf16[256,1792]{1,0:T(8,128)(2,1)S(1)} %collective-permute-done.1), channel_id=1, source_target_pairs={{0,16},{1,17},{2,18},{3,19},{4,20},{5,21},{6,22},{7,23},{8,24},{9,... | collective-permute-start | bytes 2752520 | tf_op jit(solution)/shard_map/ppermute | solution.py:35
  39.0 0.1 pad_add_fusion.where
  39.1 1.3 collective-permute-start.4
  40.4 10.2 %collective-permute-start.5 = (bf16[256,1792]{1,0:T(8,128)(2,1)}, bf16[256,1792]{1,0:T(8,128)(2,1)S(1)}, u32[]{:S(2)}, u32[]{:S(2)}) collective-permute-start(bf16[256,1792]{1,0:T(8,128)(2,1)} %param.3), channel_id=1, source_target_pairs={{1,193},{3,195},{5,197},{7,199},{9,201},{11,203},{13,205},{15,207}... | collective-permute-start | bytes 2752520 | tf_op jit(solution)/shard_map/ppermute | solution.py:35
  50.5 1.5 %broadcast_select_fusion.1 = (bf16[256,1792]{1,0:T(8,128)(2,1)S(1)}, bf16[256,1792]{1,0:T(8,128)(2,1)S(1)}, bf16[512,1792]{1,0:T(8,128)(2,1)S(1)}) fusion(bf16[256,1792]{1,0:T(8,128)(2,1)} %param.3, bf16[256,1792]{1,0:T(8,128)(2,1)S(1)} %collective-permute-done, pred[]{:T(512)S(6)} %eq.12), kind=kLoop, calls=%fused_computation.1 | loop fusion | flops 917503 | bytes 4587521 | tf_op jit(solution)/shard_map/jit(_where)/select_n | solution.py:170
  52.1 0.1 constant_dynamic-update-slice_fusion
  52.2 5.9 %collective-permute-done.2 = bf16[256,1792]{1,0:T(8,128)(2,1)S(1)} collective-permute-done((bf16[256,1792]{1,0:T(8,128)(2,1)S(1)}, bf16[256,1792]{1,0:T(8,128)(2,1)S(1)}, u32[]{:S(2)}, u32[]{:S(2)}) %collective-permute-start.2) | collective-permute-done | bytes 917536 | tf_op jit(solution)/shard_map/ppermute | solution.py:35
  58.1 0.1 broadcast_select_fusion.2
  58.2 0.7 fusion.1
  58.9 3.0 %collective-permute-start.6 = (f32[256,512]{1,0:T(8,128)S(1)}, f32[256,512]{1,0:T(8,128)S(1)}, u32[]{:S(2)}, u32[]{:S(2)}) collective-permute-start(f32[256,512]{1,0:T(8,128)S(1)} %fusion.1), channel_id=1, source_target_pairs={{0,8},{1,9},{2,10},{3,11},{4,12},{5,13},{6,14},{7,15},{8,0},{9,1},... | collective-permute-start | bytes 1572872 | tf_op jit(solution)/shard_map/ppermute | solution.py:35
  61.9 0.7 fusion.5
  62.6 1.9 %collective-permute-start.8 = (f32[256,512]{1,0:T(8,128)S(1)}, f32[256,512]{1,0:T(8,128)S(1)}, u32[]{:S(2)}, u32[]{:S(2)}) collective-permute-start(f32[256,512]{1,0:T(8,128)S(1)} %fusion.5), channel_id=1, source_target_pairs={{0,4},{1,5},{2,6},{3,7},{4,0},{5,1},{6,2},{7,3},{8,12},{9,13},{10,... | collective-permute-start | bytes 1572872 | tf_op jit(solution)/shard_map/ppermute | solution.py:35
  64.5 0.7 fusion.7
  65.2 4.0 %collective-permute-start.9 = (f32[256,512]{1,0:T(8,128)S(1)}, f32[256,512]{1,0:T(8,128)S(1)}, u32[]{:S(2)}, u32[]{:S(2)}) collective-permute-start(f32[256,512]{1,0:T(8,128)S(1)} %fusion.7), channel_id=1, source_target_pairs={{0,12},{1,13},{2,14},{3,15},{4,8},{5,9},{6,10},{7,11},{8,4},{9,5},... | collective-permute-start | bytes 1572872 | tf_op jit(solution)/shard_map/ppermute | solution.py:35
  69.2 0.7 fusion.3.first
  69.9 17.1 %collective-permute-done.4 = bf16[256,1792]{1,0:T(8,128)(2,1)S(1)} collective-permute-done((bf16[256,1792]{1,0:T(8,128)(2,1)S(1)}, bf16[256,1792]{1,0:T(8,128)(2,1)S(1)}, u32[]{:S(2)}, u32[]{:S(2)}) %collective-permute-start.4) | collective-permute-done | bytes 917536 | tf_op jit(solution)/shard_map/ppermute | solution.py:35
  87.0 0.0 collective-permute-done.5
  87.0 0.1 broadcast_select_fusion
  87.1 0.4 fusion
  87.5 0.4 fusion.4
  88.0 2.7 %collective-permute-start.7 = (f32[256,256]{1,0:T(8,128)S(1)}, f32[256,256]{1,0:T(8,128)S(1)}, u32[]{:S(2)}, u32[]{:S(2)}) collective-permute-start(f32[256,256]{1,0:T(8,128)S(1)} %fusion), channel_id=1, source_target_pairs={{0,8},{1,9},{2,10},{3,11},{4,12},{5,13},{6,14},{7,15},{8,0},{9,1},... | collective-permute-start | bytes 786440 | tf_op jit(solution)/shard_map/ppermute | solution.py:35
  90.7 1.9 %collective-permute-start.12 = (f32[256,256]{1,0:T(8,128)S(1)}, f32[256,256]{1,0:T(8,128)S(1)}, u32[]{:S(2)}, u32[]{:S(2)}) collective-permute-start(f32[256,256]{1,0:T(8,128)S(1)} %fusion.4), channel_id=1, source_target_pairs={{0,4},{1,5},{2,6},{3,7},{4,0},{5,1},{6,2},{7,3},{8,12},{9,13},{10,... | collective-permute-start | bytes 786440 | tf_op jit(solution)/shard_map/ppermute | solution.py:35
  92.7 0.4 fusion.6
  93.1 4.3 %collective-permute-start.13 = (f32[256,256]{1,0:T(8,128)S(1)}, f32[256,256]{1,0:T(8,128)S(1)}, u32[]{:S(2)}, u32[]{:S(2)}) collective-permute-start(f32[256,256]{1,0:T(8,128)S(1)} %fusion.6), channel_id=1, source_target_pairs={{0,12},{1,13},{2,14},{3,15},{4,8},{5,9},{6,10},{7,11},{8,4},{9,5},... | collective-permute-start | bytes 786440 | tf_op jit(solution)/shard_map/ppermute | solution.py:35
  97.4 0.4 fusion.2.first
  97.9 3.5 %collective-permute-done.13.fourth = f32[256,256]{1,0:T(8,128)S(1)} collective-permute-done((f32[256,256]{1,0:T(8,128)S(1)}, f32[256,256]{1,0:T(8,128)S(1)}, u32[]{:S(2)}, u32[]{:S(2)}) %collective-permute-start.13) | collective-permute-done | bytes 262176 | tf_op jit(solution)/shard_map/ppermute | solution.py:35
  101.5 0.7 halves.3
  102.1 3.2 %collective-permute-start.14 = (f32[2,128,256]{2,1,0:T(8,128)S(1)}, f32[2,128,256]{2,1,0:T(8,128)S(1)}, u32[]{:S(2)}, u32[]{:S(2)}) collective-permute-start(f32[2,128,256]{2,1,0:T(8,128)S(1)} %get-tuple-element.31), channel_id=1, source_target_pairs={{0,2},{1,3},{2,0},{3,1},{4,6},{5,7},{6,4},{7,5},{8,10},{9,11},{10,... | collective-permute-start | bytes 786440 | tf_op jit(solution)/shard_map/ppermute | solution.py:35
  105.3 0.7 halves.2
  106.1 0.0 copy-start.1
  106.1 0.0 copy-start
  106.1 2.2 %collective-permute-start.10 = (f32[3,128,256]{2,1,0:T(8,128)S(1)}, f32[3,128,256]{2,1,0:T(8,128)S(1)}, u32[]{:S(2)}, u32[]{:S(2)}) collective-permute-start(f32[3,128,256]{2,1,0:T(8,128)S(1)} %get-tuple-element.28), channel_id=1, source_target_pairs={{0,2},{1,3},{2,0},{3,1},{4,6},{5,7},{6,4},{7,5},{8,10},{9,11},{10,... | collective-permute-start | bytes 1179656 | tf_op jit(solution)/shard_map/ppermute | solution.py:35
  108.3 2.8 %collective-permute-done.14 = f32[2,128,256]{2,1,0:T(8,128)S(1)} collective-permute-done((f32[2,128,256]{2,1,0:T(8,128)S(1)}, f32[2,128,256]{2,1,0:T(8,128)S(1)}, u32[]{:S(2)}, u32[]{:S(2)}) %collective-permute-start.14) | collective-permute-done | bytes 262176 | tf_op jit(solution)/shard_map/ppermute | solution.py:35
  111.2 1.9 %collective-permute-start.15 = (f32[128,256]{1,0:T(8,128)S(1)}, f32[128,256]{1,0:T(8,128)S(1)}, u32[]{:S(2)}, u32[]{:S(2)}) collective-permute-start(f32[128,256]{1,0:T(8,128)S(1)} %get-tuple-element.46), channel_id=1, source_target_pairs={{0,192},{1,129},{2,194},{3,131},{4,208},{5,145},{6,210},{7,147},{8... | collective-permute-start | bytes 393224 | tf_op jit(solution)/shard_map/ppermute | solution.py:35
  113.1 4.7 %collective-permute-done.10 = f32[3,128,256]{2,1,0:T(8,128)S(1)} collective-permute-done((f32[3,128,256]{2,1,0:T(8,128)S(1)}, f32[3,128,256]{2,1,0:T(8,128)S(1)}, u32[]{:S(2)}, u32[]{:S(2)}) %collective-permute-start.10) | collective-permute-done | bytes 393248 | tf_op jit(solution)/shard_map/ppermute | solution.py:35
  117.8 0.1 fusion.10
  117.9 5.1 %collective-permute-start.11 = (f32[128,256]{1,0:T(8,128)S(1)}, f32[128,256]{1,0:T(8,128)S(1)}, u32[]{:S(2)}, u32[]{:S(2)}) collective-permute-start(f32[128,256]{1,0:T(8,128)S(1)} %get-tuple-element.43), channel_id=1, source_target_pairs={{1,65},{3,67},{5,81},{7,83},{9,97},{11,99},{13,113},{15,115},{17,6... | collective-permute-start | bytes 393224 | tf_op jit(solution)/shard_map/ppermute | solution.py:35
  122.9 6.2 %collective-permute-done.15.across_late = f32[128,256]{1,0:T(8,128)S(1)} collective-permute-done((f32[128,256]{1,0:T(8,128)S(1)}, f32[128,256]{1,0:T(8,128)S(1)}, u32[]{:S(2)}, u32[]{:S(2)}) %collective-permute-start.15) | collective-permute-done | bytes 131104 | tf_op jit(solution)/shard_map/ppermute | solution.py:35
  129.1 0.6 strips.1
  129.7 12.7 %collective-permute-start.16 = (f32[4,64,256]{2,1,0:T(8,128)S(1)}, f32[4,64,256]{2,1,0:T(8,128)S(1)}, u32[]{:S(2)}, u32[]{:S(2)}) collective-permute-start(f32[4,64,256]{2,1,0:T(8,128)S(1)} %get-tuple-element.33), channel_id=1, source_target_pairs={{0,1},{1,0},{2,3},{3,2},{4,5},{5,4},{6,7},{7,6},{8,9},{9,8},{10,11... | collective-permute-start | bytes 786440 | tf_op jit(solution)/shard_map/ppermute | solution.py:35
  142.5 0.1 copy.5
  142.6 1.0 collective-permute-done.16.other
  143.6 1.9 %refresh.1 = (bf16[64,1024]{1,0:T(8,128)(2,1)}, f32[64,8]{1,0:T(8,128)S(1)}) custom-call(s32[3]{0:T(128)S(1)} %pad_add_fusion.where, f32[4,64,256]{2,1,0:T(8,128)S(1)} %get-tuple-element.32.mine, f32[4,64,256]{2,1,0:T(8,128)S(1)} %collective-permute-done.16.other, bf16[64,1024]{1,0:T(8,128)(2,1)S(1)} %bitcast.26, f32[64,8]{1,0:T(8,128)S(1)} %bitcast.25), custom_call_target="tpu_custom_call" | custom-call | flops 16777216 | bytes 790540 | tf_op jit(solution)/shard_map/refresh/pallas_call | solution.py:53
  145.5 0.7 copy.6
  (11 shorter events, 0.1 us)
Async XLA Ops:
  0.6 33.5 %collective-permute-start.1 = (bf16[256,1792]{1,0:T(8,128)(2,1)}, bf16[256,1792]{1,0:T(8,128)(2,1)S(1)}, u32[]{:S(2)}, u32[]{:S(2)}) collective-permute-start(bf16[256,1792]{1,0:T(8,128)(2,1)} %param.3), channel_id=1, source_target_pairs={{0,32},{1,33},{2,34},{3,35},{4,36},{5,37},{6,38},{7,39},{8,40},{9,... | collective-permute-start | bytes 2752520 | tf_op jit(solution)/shard_map/ppermute | solution.py:35
  4.2 34.9 %collective-permute-start.3 = (bf16[256,1792]{1,0:T(8,128)(2,1)}, bf16[256,1792]{1,0:T(8,128)(2,1)S(1)}, u32[]{:S(2)}, u32[]{:S(2)}) collective-permute-start(bf16[256,1792]{1,0:T(8,128)(2,1)} %param.3), channel_id=1, source_target_pairs={{0,64},{2,66},{4,68},{6,70},{8,72},{10,74},{12,76},{14,78},{16,80}... | collective-permute-start | bytes 2752520 | tf_op jit(solution)/shard_map/ppermute | solution.py:35
  5.5 45.1 %collective-permute-start = (bf16[256,1792]{1,0:T(8,128)(2,1)}, bf16[256,1792]{1,0:T(8,128)(2,1)S(1)}, u32[]{:S(2)}, u32[]{:S(2)}) collective-permute-start(bf16[256,1792]{1,0:T(8,128)(2,1)} %param.3), channel_id=1, source_target_pairs={{0,16},{1,17},{2,18},{3,19},{4,20},{5,21},{6,22},{7,23},{8,24},{9,... | collective-permute-start | bytes 2752520 | tf_op jit(solution)/shard_map/ppermute | solution.py:35
  34.2 23.9 %collective-permute-start.2 = (bf16[256,1792]{1,0:T(8,128)(2,1)S(1)}, bf16[256,1792]{1,0:T(8,128)(2,1)S(1)}, u32[]{:S(2)}, u32[]{:S(2)}) collective-permute-start(bf16[256,1792]{1,0:T(8,128)(2,1)S(1)} %collective-permute-done.1), channel_id=1, source_target_pairs={{0,16},{1,17},{2,18},{3,19},{4,20},{5,21},{6,22},{7,23},{8,24},{9,... | collective-permute-start | bytes 2752520 | tf_op jit(solution)/shard_map/ppermute | solution.py:35
  39.1 47.9 %collective-permute-start.4 = (bf16[256,1792]{1,0:T(8,128)(2,1)S(1)}, bf16[256,1792]{1,0:T(8,128)(2,1)S(1)}, u32[]{:S(2)}, u32[]{:S(2)}) collective-permute-start(bf16[256,1792]{1,0:T(8,128)(2,1)S(1)} %collective-permute-done.3), channel_id=1, source_target_pairs={{64,128},{65,1},{66,130},{67,3},{68,132},{69,5},{70,134},{71,7},{7... | collective-permute-start | bytes 2752520 | tf_op jit(solution)/shard_map/ppermute | solution.py:35
  40.4 46.6 %collective-permute-start.5 = (bf16[256,1792]{1,0:T(8,128)(2,1)}, bf16[256,1792]{1,0:T(8,128)(2,1)S(1)}, u32[]{:S(2)}, u32[]{:S(2)}) collective-permute-start(bf16[256,1792]{1,0:T(8,128)(2,1)} %param.3), channel_id=1, source_target_pairs={{1,193},{3,195},{5,197},{7,199},{9,201},{11,203},{13,205},{15,207}... | collective-permute-start | bytes 2752520 | tf_op jit(solution)/shard_map/ppermute | solution.py:35
  58.9 28.2 %collective-permute-start.6 = (f32[256,512]{1,0:T(8,128)S(1)}, f32[256,512]{1,0:T(8,128)S(1)}, u32[]{:S(2)}, u32[]{:S(2)}) collective-permute-start(f32[256,512]{1,0:T(8,128)S(1)} %fusion.1), channel_id=1, source_target_pairs={{0,8},{1,9},{2,10},{3,11},{4,12},{5,13},{6,14},{7,15},{8,0},{9,1},... | collective-permute-start | bytes 1572872 | tf_op jit(solution)/shard_map/ppermute | solution.py:35
  62.6 35.3 %collective-permute-start.8 = (f32[256,512]{1,0:T(8,128)S(1)}, f32[256,512]{1,0:T(8,128)S(1)}, u32[]{:S(2)}, u32[]{:S(2)}) collective-permute-start(f32[256,512]{1,0:T(8,128)S(1)} %fusion.5), channel_id=1, source_target_pairs={{0,4},{1,5},{2,6},{3,7},{4,0},{5,1},{6,2},{7,3},{8,12},{9,13},{10,... | collective-permute-start | bytes 1572872 | tf_op jit(solution)/shard_map/ppermute | solution.py:35
  65.2 32.7 %collective-permute-start.9 = (f32[256,512]{1,0:T(8,128)S(1)}, f32[256,512]{1,0:T(8,128)S(1)}, u32[]{:S(2)}, u32[]{:S(2)}) collective-permute-start(f32[256,512]{1,0:T(8,128)S(1)} %fusion.7), channel_id=1, source_target_pairs={{0,12},{1,13},{2,14},{3,15},{4,8},{5,9},{6,10},{7,11},{8,4},{9,5},... | collective-permute-start | bytes 1572872 | tf_op jit(solution)/shard_map/ppermute | solution.py:35
  88.0 9.9 %collective-permute-start.7 = (f32[256,256]{1,0:T(8,128)S(1)}, f32[256,256]{1,0:T(8,128)S(1)}, u32[]{:S(2)}, u32[]{:S(2)}) collective-permute-start(f32[256,256]{1,0:T(8,128)S(1)} %fusion), channel_id=1, source_target_pairs={{0,8},{1,9},{2,10},{3,11},{4,12},{5,13},{6,14},{7,15},{8,0},{9,1},... | collective-permute-start | bytes 786440 | tf_op jit(solution)/shard_map/ppermute | solution.py:35
  90.7 7.2 %collective-permute-start.12 = (f32[256,256]{1,0:T(8,128)S(1)}, f32[256,256]{1,0:T(8,128)S(1)}, u32[]{:S(2)}, u32[]{:S(2)}) collective-permute-start(f32[256,256]{1,0:T(8,128)S(1)} %fusion.4), channel_id=1, source_target_pairs={{0,4},{1,5},{2,6},{3,7},{4,0},{5,1},{6,2},{7,3},{8,12},{9,13},{10,... | collective-permute-start | bytes 786440 | tf_op jit(solution)/shard_map/ppermute | solution.py:35
  93.1 8.3 %collective-permute-start.13 = (f32[256,256]{1,0:T(8,128)S(1)}, f32[256,256]{1,0:T(8,128)S(1)}, u32[]{:S(2)}, u32[]{:S(2)}) collective-permute-start(f32[256,256]{1,0:T(8,128)S(1)} %fusion.6), channel_id=1, source_target_pairs={{0,12},{1,13},{2,14},{3,15},{4,8},{5,9},{6,10},{7,11},{8,4},{9,5},... | collective-permute-start | bytes 786440 | tf_op jit(solution)/shard_map/ppermute | solution.py:35
  102.1 9.0 %collective-permute-start.14 = (f32[2,128,256]{2,1,0:T(8,128)S(1)}, f32[2,128,256]{2,1,0:T(8,128)S(1)}, u32[]{:S(2)}, u32[]{:S(2)}) collective-permute-start(f32[2,128,256]{2,1,0:T(8,128)S(1)} %get-tuple-element.31), channel_id=1, source_target_pairs={{0,2},{1,3},{2,0},{3,1},{4,6},{5,7},{6,4},{7,5},{8,10},{9,11},{10,... | collective-permute-start | bytes 786440 | tf_op jit(solution)/shard_map/ppermute | solution.py:35
  106.1 36.4 %copy-start.1 = (f32[1,64,8]{1,2,0:T(8,128)S(1)}, f32[1,64,8]{1,2,0:T(8,128)}, u32[]{:S(2)}) copy-start(f32[1,64,8]{1,2,0:T(8,128)} %param.5) | copy-start | bytes 6148
  106.1 37.5 %copy-start = (bf16[1,64,1024]{2,1,0:T(8,128)(2,1)S(1)}, bf16[1,64,1024]{2,1,0:T(8,128)(2,1)}, u32[]{:S(2)}) copy-start(bf16[1,64,1024]{2,1,0:T(8,128)(2,1)} %param.4) | copy-start | bytes 393220
  106.1 11.7 %collective-permute-start.10 = (f32[3,128,256]{2,1,0:T(8,128)S(1)}, f32[3,128,256]{2,1,0:T(8,128)S(1)}, u32[]{:S(2)}, u32[]{:S(2)}) collective-permute-start(f32[3,128,256]{2,1,0:T(8,128)S(1)} %get-tuple-element.28), channel_id=1, source_target_pairs={{0,2},{1,3},{2,0},{3,1},{4,6},{5,7},{6,4},{7,5},{8,10},{9,11},{10,... | collective-permute-start | bytes 1179656 | tf_op jit(solution)/shard_map/ppermute | solution.py:35
  111.2 17.9 %collective-permute-start.15 = (f32[128,256]{1,0:T(8,128)S(1)}, f32[128,256]{1,0:T(8,128)S(1)}, u32[]{:S(2)}, u32[]{:S(2)}) collective-permute-start(f32[128,256]{1,0:T(8,128)S(1)} %get-tuple-element.46), channel_id=1, source_target_pairs={{0,192},{1,129},{2,194},{3,131},{4,208},{5,145},{6,210},{7,147},{8... | collective-permute-start | bytes 393224 | tf_op jit(solution)/shard_map/ppermute | solution.py:35
  117.9 11.2 %collective-permute-start.11 = (f32[128,256]{1,0:T(8,128)S(1)}, f32[128,256]{1,0:T(8,128)S(1)}, u32[]{:S(2)}, u32[]{:S(2)}) collective-permute-start(f32[128,256]{1,0:T(8,128)S(1)} %get-tuple-element.43), channel_id=1, source_target_pairs={{1,65},{3,67},{5,81},{7,83},{9,97},{11,99},{13,113},{15,115},{17,6... | collective-permute-start | bytes 393224 | tf_op jit(solution)/shard_map/ppermute | solution.py:35
  129.7 13.9 %collective-permute-start.16 = (f32[4,64,256]{2,1,0:T(8,128)S(1)}, f32[4,64,256]{2,1,0:T(8,128)S(1)}, u32[]{:S(2)}, u32[]{:S(2)}) collective-permute-start(f32[4,64,256]{2,1,0:T(8,128)S(1)} %get-tuple-element.33), channel_id=1, source_target_pairs={{0,1},{1,0},{2,3},{3,2},{4,5},{5,4},{6,7},{7,6},{8,9},{9,8},{10,11... | collective-permute-start | bytes 786440 | tf_op jit(solution)/shard_map/ppermute | solution.py:35

commit v9 on v7

--- a/solution.py
+++ b/solution.py
@@ -176,6 +176,7 @@
     high = swap_if(turn & 1 == 1, z_block, zy_block)
     s0, s2 = swap_if(turn >> 1 == 1, low[0], high[0])
     s1, s3 = swap_if(turn >> 1 == 1, low[1], high[1])
+    s1, s3 = swap_if(tensor & 1 == 1, s1, s3)
     rows = [s0, s1, s2, s3]
 
     passing = [gradient, permute(gradient, onward, lambda at: reach(at) < 3)]
@@ -193,7 +194,7 @@
         parts = products(rows, [passing[step] for step in steps])
         valid = lambda at, steps=steps: reach(at) >= steps[0]
         parts[1:] = [
-            permute(parts[d], lambda at, d=d: dict(x=at["x"] ^ d), valid) for d in (2, 1, 3)
+            permute(parts[d], lambda at, d=d: dict(x=at["x"] ^ (d if at["c"] == 0 else -d & 3)), valid) for d in (2, 1, 3)
         ]
         far = [k for k, step in enumerate(steps) if step]
         keep, give = halves(where, far, parts)

time: 147 us -> 147 us (level)
  waiting for transfers between devices: 70.9 us -> 68.7 us
    ppermute x18, waiting for transfers between devices: 70.9 us -> 68.7 us  [permute(): return lax.ppermute(array, AXES, pairs)]
  transfers between devices with their start and end apart: 18 -> 18, of which waited for: 9 -> 9; matrix products, arithmetic and copies ran while one was open for 5% -> 6% of each run, Pallas kernels for 1% -> 1%
where the time goes in v9:
time: 147 us; the launch traced here: 146 us
  waiting for transfers between devices  68.7 us (47%)
  starting transfers between devices  62.9 us (43%)
  matrix products  5.34 us (4%)
  Pallas kernels  3.96 us (3%)
  other arithmetic  2.32 us (2%)
  local copies, waits for them, and re-layouts  2.12 us (1%)
    ppermute x18, waiting for transfers between devices, permute(): return lax.ppermute(array, AXES, pairs)  68.7 us
    ppermute x18, starting transfers between devices, permute(): return lax.ppermute(array, AXES, pairs)  62.9 us
    dot_general x8, matrix products, products(): lax.dot_general(row, cols, (((1,), (1,)), ((), ())), preferred_element_ty...  5.34 us
    pallas_call x4, Pallas kernels, call(): pl.pallas_call(kernel, out_shape=outs, in_specs=in_specs, out_specs=[VMEM...  3.96 us
  transfers between devices with their start and end apart: 18, of which 9 were waited for; matrix products, arithmetic and copies ran while one was open for 6% of the time, Pallas kernels for 1%

profile of v9, /device:TPU:5, one launch (start us, length us, event | category | flops | bytes accessed | tf_op | source)
XLA Modules:
  0.0 146.4 jit_solution(17853401645307711638)
XLA Ops:
  0.6 3.5 %collective-permute-start = (bf16[256,1792]{1,0:T(8,128)(2,1)}, bf16[256,1792]{1,0:T(8,128)(2,1)S(1)}, u32[]{:S(2)}, u32[]{:S(2)}) collective-permute-start(bf16[256,1792]{1,0:T(8,128)(2,1)} %param.3), channel_id=1, source_target_pairs={{0,32},{1,33},{2,34},{3,35},{4,36},{5,37},{6,38},{7,39},{8,40},{9,... | collective-permute-start | bytes 2752520 | tf_op jit(solution)/shard_map/ppermute | solution.py:35
  4.2 1.3 collective-permute-start.3
  5.5 4.8 %collective-permute-start.2 = (bf16[256,1792]{1,0:T(8,128)(2,1)}, bf16[256,1792]{1,0:T(8,128)(2,1)S(1)}, u32[]{:S(2)}, u32[]{:S(2)}) collective-permute-start(bf16[256,1792]{1,0:T(8,128)(2,1)} %param.3), channel_id=1, source_target_pairs={{0,16},{1,17},{2,18},{3,19},{4,20},{5,21},{6,22},{7,23},{8,24},{9,... | collective-permute-start | bytes 2752520 | tf_op jit(solution)/shard_map/ppermute | solution.py:35
  10.3 23.9 %collective-permute-done = bf16[256,1792]{1,0:T(8,128)(2,1)S(1)} collective-permute-done((bf16[256,1792]{1,0:T(8,128)(2,1)}, bf16[256,1792]{1,0:T(8,128)(2,1)S(1)}, u32[]{:S(2)}, u32[]{:S(2)}) %collective-permute-start) | collective-permute-done | bytes 917536 | tf_op jit(solution)/shard_map/ppermute | solution.py:35
  34.2 4.8 %collective-permute-start.1 = (bf16[256,1792]{1,0:T(8,128)(2,1)S(1)}, bf16[256,1792]{1,0:T(8,128)(2,1)S(1)}, u32[]{:S(2)}, u32[]{:S(2)}) collective-permute-start(bf16[256,1792]{1,0:T(8,128)(2,1)S(1)} %collective-permute-done), channel_id=1, source_target_pairs={{0,16},{1,17},{2,18},{3,19},{4,20},{5,21},{6,22},{7,23},{8,24},{9,... | collective-permute-start | bytes 2752520 | tf_op jit(solution)/shard_map/ppermute | solution.py:35
  39.0 0.1 pad_add_fusion.where
  39.1 1.3 collective-permute-start.8
  40.4 1.3 collective-permute-start.9
  41.7 16.4 %collective-permute-done.1 = bf16[256,1792]{1,0:T(8,128)(2,1)S(1)} collective-permute-done((bf16[256,1792]{1,0:T(8,128)(2,1)S(1)}, bf16[256,1792]{1,0:T(8,128)(2,1)S(1)}, u32[]{:S(2)}, u32[]{:S(2)}) %collective-permute-start.1) | collective-permute-done | bytes 917536 | tf_op jit(solution)/shard_map/ppermute | solution.py:35
  58.1 2.1 %broadcast_select_fusion = (bf16[256,1792]{1,0:T(8,128)(2,1)S(1)}, bf16[256,1792]{1,0:T(8,128)(2,1)S(1)}, bf16[256,1792]{1,0:T(8,128)(2,1)S(1)}, bf16[256,1792]{1,0:T(8,128)(2,1)S(1)}, bf16[512,1792]{1,0:T(8,128)(2,1)S(1)}) fusion(pred[]{:T(512)S(6)} %eq.13, pred[]{:T(512)S(6)} %eq.11, bf16[256,1792]{1,0:T(8,128)(2,1)} %param.3, ...), kind=kLoop, calls=%fused_computation | loop fusion | flops 3670015 | bytes 8257539 | tf_op jit(solution)/shard_map/jit(_where)/select_n | solution.py:162
  60.2 1.2 constant_dynamic-update-slice_fusion
  61.4 0.7 fusion.3
  62.1 2.0 %collective-permute-start.4 = (f32[256,512]{1,0:T(8,128)S(1)}, f32[256,512]{1,0:T(8,128)S(1)}, u32[]{:S(2)}, u32[]{:S(2)}) collective-permute-start(f32[256,512]{1,0:T(8,128)S(1)} %fusion.3), channel_id=1, source_target_pairs={{0,8},{1,9},{2,10},{3,11},{4,12},{5,13},{6,14},{7,15},{8,0},{9,1},... | collective-permute-start | bytes 1572872 | tf_op jit(solution)/shard_map/ppermute | solution.py:35
  64.2 0.7 fusion.11
  64.8 3.9 %collective-permute-start.5 = (f32[256,512]{1,0:T(8,128)S(1)}, f32[256,512]{1,0:T(8,128)S(1)}, u32[]{:S(2)}, u32[]{:S(2)}) collective-permute-start(f32[256,512]{1,0:T(8,128)S(1)} %fusion.11), channel_id=1, source_target_pairs={{0,4},{1,13},{2,6},{3,15},{4,0},{5,9},{6,2},{7,11},{8,12},{9,5},{1... | collective-permute-start | bytes 1572872 | tf_op jit(solution)/shard_map/ppermute | solution.py:35
  68.7 0.7 fusion.12
  69.4 3.7 %collective-permute-start.6 = (f32[256,512]{1,0:T(8,128)S(1)}, f32[256,512]{1,0:T(8,128)S(1)}, u32[]{:S(2)}, u32[]{:S(2)}) collective-permute-start(f32[256,512]{1,0:T(8,128)S(1)} %fusion.12), channel_id=1, source_target_pairs={{0,12},{1,5},{2,14},{3,7},{4,8},{5,1},{6,10},{7,3},{8,4},{9,13},{1... | collective-permute-start | bytes 1572872 | tf_op jit(solution)/shard_map/ppermute | solution.py:35
  73.1 0.1 constant_dynamic-update-slice_fusion.3
  73.2 17.5 %collective-permute-done.9 = bf16[256,1792]{1,0:T(8,128)(2,1)S(1)} collective-permute-done((bf16[256,1792]{1,0:T(8,128)(2,1)}, bf16[256,1792]{1,0:T(8,128)(2,1)S(1)}, u32[]{:S(2)}, u32[]{:S(2)}) %collective-permute-start.9) | collective-permute-done | bytes 917536 | tf_op jit(solution)/shard_map/ppermute | solution.py:35
  90.6 0.1 constant_dynamic-update-slice_fusion.2
  90.7 0.7 fusion.2
  91.4 2.1 %collective-permute-start.10 = (f32[256,512]{1,0:T(8,128)S(1)}, f32[256,512]{1,0:T(8,128)S(1)}, u32[]{:S(2)}, u32[]{:S(2)}) collective-permute-start(f32[256,512]{1,0:T(8,128)S(1)} %fusion.2), channel_id=1, source_target_pairs={{1,9},{3,11},{5,13},{7,15},{9,1},{11,3},{13,5},{15,7},{17,25},{19,... | collective-permute-start | bytes 1572872 | tf_op jit(solution)/shard_map/ppermute | solution.py:35
  93.5 0.7 fusion.13
  94.2 3.8 %collective-permute-start.11 = (f32[256,512]{1,0:T(8,128)S(1)}, f32[256,512]{1,0:T(8,128)S(1)}, u32[]{:S(2)}, u32[]{:S(2)}) collective-permute-start(f32[256,512]{1,0:T(8,128)S(1)} %fusion.13), channel_id=1, source_target_pairs={{1,13},{3,15},{5,9},{7,11},{9,5},{11,7},{13,1},{15,3},{17,29},{19,... | collective-permute-start | bytes 1572872 | tf_op jit(solution)/shard_map/ppermute | solution.py:35
  98.0 0.7 fusion.14
  98.7 3.7 %collective-permute-start.12 = (f32[256,512]{1,0:T(8,128)S(1)}, f32[256,512]{1,0:T(8,128)S(1)}, u32[]{:S(2)}, u32[]{:S(2)}) collective-permute-start(f32[256,512]{1,0:T(8,128)S(1)} %fusion.14), channel_id=1, source_target_pairs={{1,5},{3,7},{5,1},{7,3},{9,13},{11,15},{13,9},{15,11},{17,21},{19,... | collective-permute-start | bytes 1572872 | tf_op jit(solution)/shard_map/ppermute | solution.py:35
  102.4 0.7 fusion.1.first
  103.1 0.7 halves.2
  103.8 3.2 %collective-permute-start.7 = (f32[3,128,256]{2,1,0:T(8,128)S(1)}, f32[3,128,256]{2,1,0:T(8,128)S(1)}, u32[]{:S(2)}, u32[]{:S(2)}) collective-permute-start(f32[3,128,256]{2,1,0:T(8,128)S(1)} %get-tuple-element.11), channel_id=1, source_target_pairs={{0,2},{1,3},{2,0},{3,1},{4,6},{5,7},{6,4},{7,5},{8,10},{9,11},{10,... | collective-permute-start | bytes 1179656 | tf_op jit(solution)/shard_map/ppermute | solution.py:35
  107.0 0.7 fusion.first
  107.7 0.8 collective-permute-done.11.third
  108.4 0.5 collective-permute-done.12.fourth
  108.9 0.8 halves.3
  109.7 3.2 %collective-permute-start.13 = (f32[4,128,256]{2,1,0:T(8,128)S(1)}, f32[4,128,256]{2,1,0:T(8,128)S(1)}, u32[]{:S(2)}, u32[]{:S(2)}) collective-permute-start(f32[4,128,256]{2,1,0:T(8,128)S(1)} %get-tuple-element.13), channel_id=1, source_target_pairs={{1,3},{3,1},{5,7},{7,5},{9,11},{11,9},{13,15},{15,13},{17,19},{19,... | collective-permute-start | bytes 1572872 | tf_op jit(solution)/shard_map/ppermute | solution.py:35
  112.9 0.1 fusion.6
  113.0 1.3 collective-permute-start.14
  114.3 6.7 %collective-permute-done.13 = f32[4,128,256]{2,1,0:T(8,128)S(1)} collective-permute-done((f32[4,128,256]{2,1,0:T(8,128)S(1)}, f32[4,128,256]{2,1,0:T(8,128)S(1)}, u32[]{:S(2)}, u32[]{:S(2)}) %collective-permute-start.13) | collective-permute-done | bytes 524320 | tf_op jit(solution)/shard_map/ppermute | solution.py:35
  121.0 0.1 fusion.4
  121.1 1.3 collective-permute-start.15
  122.4 1.3 collective-permute-start.16
  123.7 0.6 collective-permute-done.15.refs_5_
  124.3 1.4 collective-permute-done.16.refs_6_
  125.7 0.6 strips.1
  126.3 16.4 %collective-permute-start.17 = (f32[4,64,256]{2,1,0:T(8,128)S(1)}, f32[4,64,256]{2,1,0:T(8,128)S(1)}, u32[]{:S(2)}, u32[]{:S(2)}) collective-permute-start(f32[4,64,256]{2,1,0:T(8,128)S(1)} %get-tuple-element.15), channel_id=1, source_target_pairs={{0,1},{1,0},{2,3},{3,2},{4,5},{5,4},{6,7},{7,6},{8,9},{9,8},{10,11... | collective-permute-start | bytes 786440 | tf_op jit(solution)/shard_map/ppermute | solution.py:35
  142.7 0.1 copy.5
  142.8 1.0 collective-permute-done.17.other
  143.9 1.9 %refresh.1 = (bf16[64,1024]{1,0:T(8,128)(2,1)}, f32[64,8]{1,0:T(8,128)S(1)}) custom-call(s32[4]{0:T(128)S(1)} %pad_add_fusion.where, f32[4,64,256]{2,1,0:T(8,128)S(1)} %get-tuple-element.14.mine, f32[4,64,256]{2,1,0:T(8,128)S(1)} %collective-permute-done.17.other, bf16[64,1024]{1,0:T(8,128)(2,1)S(1)} %bitcast.35, f32[64,8]{1,0:T(8,128)S(1)} %bitcast.34), custom_call_target="tpu_custom_call" | custom-call | flops 16777216 | bytes 790544 | tf_op jit(solution)/shard_map/refresh/pallas_call | solution.py:49
  145.7 0.7 copy.6
  (13 shorter events, 0.0 us)
Async XLA Ops:
  0.6 33.5 %collective-permute-start = (bf16[256,1792]{1,0:T(8,128)(2,1)}, bf16[256,1792]{1,0:T(8,128)(2,1)S(1)}, u32[]{:S(2)}, u32[]{:S(2)}) collective-permute-start(bf16[256,1792]{1,0:T(8,128)(2,1)} %param.3), channel_id=1, source_target_pairs={{0,32},{1,33},{2,34},{3,35},{4,36},{5,37},{6,38},{7,39},{8,40},{9,... | collective-permute-start | bytes 2752520 | tf_op jit(solution)/shard_map/ppermute | solution.py:35
  4.2 34.9 %collective-permute-start.3 = (bf16[256,1792]{1,0:T(8,128)(2,1)}, bf16[256,1792]{1,0:T(8,128)(2,1)}, u32[]{:S(2)}, u32[]{:S(2)}) collective-permute-start(bf16[256,1792]{1,0:T(8,128)(2,1)} %param.3), channel_id=1, source_target_pairs={{0,64},{2,66},{4,68},{6,70},{8,72},{10,74},{12,76},{14,78},{16,80}... | collective-permute-start | bytes 2752520 | tf_op jit(solution)/shard_map/ppermute | solution.py:35
  5.5 36.2 %collective-permute-start.2 = (bf16[256,1792]{1,0:T(8,128)(2,1)}, bf16[256,1792]{1,0:T(8,128)(2,1)S(1)}, u32[]{:S(2)}, u32[]{:S(2)}) collective-permute-start(bf16[256,1792]{1,0:T(8,128)(2,1)} %param.3), channel_id=1, source_target_pairs={{0,16},{1,17},{2,18},{3,19},{4,20},{5,21},{6,22},{7,23},{8,24},{9,... | collective-permute-start | bytes 2752520 | tf_op jit(solution)/shard_map/ppermute | solution.py:35
  34.2 23.9 %collective-permute-start.1 = (bf16[256,1792]{1,0:T(8,128)(2,1)S(1)}, bf16[256,1792]{1,0:T(8,128)(2,1)S(1)}, u32[]{:S(2)}, u32[]{:S(2)}) collective-permute-start(bf16[256,1792]{1,0:T(8,128)(2,1)S(1)} %collective-permute-done), channel_id=1, source_target_pairs={{0,16},{1,17},{2,18},{3,19},{4,20},{5,21},{6,22},{7,23},{8,24},{9,... | collective-permute-start | bytes 2752520 | tf_op jit(solution)/shard_map/ppermute | solution.py:35
  39.1 34.0 %collective-permute-start.8 = (bf16[256,1792]{1,0:T(8,128)(2,1)}, bf16[256,1792]{1,0:T(8,128)(2,1)S(1)}, u32[]{:S(2)}, u32[]{:S(2)}) collective-permute-start(bf16[256,1792]{1,0:T(8,128)(2,1)} %collective-permute-done.3), channel_id=1, source_target_pairs={{64,128},{65,1},{66,130},{67,3},{68,132},{69,5},{70,134},{71,7},{7... | collective-permute-start | bytes 2752520 | tf_op jit(solution)/shard_map/ppermute | solution.py:35
  40.4 50.3 %collective-permute-start.9 = (bf16[256,1792]{1,0:T(8,128)(2,1)}, bf16[256,1792]{1,0:T(8,128)(2,1)S(1)}, u32[]{:S(2)}, u32[]{:S(2)}) collective-permute-start(bf16[256,1792]{1,0:T(8,128)(2,1)} %collective-permute-done.3), channel_id=1, source_target_pairs={{64,192},{66,194},{68,196},{70,198},{72,200},{74,202},{76,204},{78... | collective-permute-start | bytes 2752520 | tf_op jit(solution)/shard_map/ppermute | solution.py:35
  62.1 36.6 %collective-permute-start.4 = (f32[256,512]{1,0:T(8,128)S(1)}, f32[256,512]{1,0:T(8,128)S(1)}, u32[]{:S(2)}, u32[]{:S(2)}) collective-permute-start(f32[256,512]{1,0:T(8,128)S(1)} %fusion.3), channel_id=1, source_target_pairs={{0,8},{1,9},{2,10},{3,11},{4,12},{5,13},{6,14},{7,15},{8,0},{9,1},... | collective-permute-start | bytes 1572872 | tf_op jit(solution)/shard_map/ppermute | solution.py:35
  64.8 38.2 %collective-permute-start.5 = (f32[256,512]{1,0:T(8,128)S(1)}, f32[256,512]{1,0:T(8,128)S(1)}, u32[]{:S(2)}, u32[]{:S(2)}) collective-permute-start(f32[256,512]{1,0:T(8,128)S(1)} %fusion.11), channel_id=1, source_target_pairs={{0,4},{1,13},{2,6},{3,15},{4,0},{5,9},{6,2},{7,11},{8,12},{9,5},{1... | collective-permute-start | bytes 1572872 | tf_op jit(solution)/shard_map/ppermute | solution.py:35
  69.4 33.7 %collective-permute-start.6 = (f32[256,512]{1,0:T(8,128)S(1)}, f32[256,512]{1,0:T(8,128)S(1)}, u32[]{:S(2)}, u32[]{:S(2)}) collective-permute-start(f32[256,512]{1,0:T(8,128)S(1)} %fusion.12), channel_id=1, source_target_pairs={{0,12},{1,5},{2,14},{3,7},{4,8},{5,1},{6,10},{7,3},{8,4},{9,13},{1... | collective-permute-start | bytes 1572872 | tf_op jit(solution)/shard_map/ppermute | solution.py:35
  91.4 16.3 %collective-permute-start.10 = (f32[256,512]{1,0:T(8,128)S(1)}, f32[256,512]{1,0:T(8,128)S(1)}, u32[]{:S(2)}, u32[]{:S(2)}) collective-permute-start(f32[256,512]{1,0:T(8,128)S(1)} %fusion.2), channel_id=1, source_target_pairs={{1,9},{3,11},{5,13},{7,15},{9,1},{11,3},{13,5},{15,7},{17,25},{19,... | collective-permute-start | bytes 1572872 | tf_op jit(solution)/shard_map/ppermute | solution.py:35
  94.2 14.2 %collective-permute-start.11 = (f32[256,512]{1,0:T(8,128)S(1)}, f32[256,512]{1,0:T(8,128)S(1)}, u32[]{:S(2)}, u32[]{:S(2)}) collective-permute-start(f32[256,512]{1,0:T(8,128)S(1)} %fusion.13), channel_id=1, source_target_pairs={{1,13},{3,15},{5,9},{7,11},{9,5},{11,7},{13,1},{15,3},{17,29},{19,... | collective-permute-start | bytes 1572872 | tf_op jit(solution)/shard_map/ppermute | solution.py:35
  98.7 10.2 %collective-permute-start.12 = (f32[256,512]{1,0:T(8,128)S(1)}, f32[256,512]{1,0:T(8,128)S(1)}, u32[]{:S(2)}, u32[]{:S(2)}) collective-permute-start(f32[256,512]{1,0:T(8,128)S(1)} %fusion.14), channel_id=1, source_target_pairs={{1,5},{3,7},{5,1},{7,3},{9,13},{11,15},{13,9},{15,11},{17,21},{19,... | collective-permute-start | bytes 1572872 | tf_op jit(solution)/shard_map/ppermute | solution.py:35
  103.8 9.1 %collective-permute-start.7 = (f32[3,128,256]{2,1,0:T(8,128)S(1)}, f32[3,128,256]{2,1,0:T(8,128)S(1)}, u32[]{:S(2)}, u32[]{:S(2)}) collective-permute-start(f32[3,128,256]{2,1,0:T(8,128)S(1)} %get-tuple-element.11), channel_id=1, source_target_pairs={{0,2},{1,3},{2,0},{3,1},{4,6},{5,7},{6,4},{7,5},{8,10},{9,11},{10,... | collective-permute-start | bytes 1179656 | tf_op jit(solution)/shard_map/ppermute | solution.py:35
  109.7 11.3 %collective-permute-start.13 = (f32[4,128,256]{2,1,0:T(8,128)S(1)}, f32[4,128,256]{2,1,0:T(8,128)S(1)}, u32[]{:S(2)}, u32[]{:S(2)}) collective-permute-start(f32[4,128,256]{2,1,0:T(8,128)S(1)} %get-tuple-element.13), channel_id=1, source_target_pairs={{1,3},{3,1},{5,7},{7,5},{9,11},{11,9},{13,15},{15,13},{17,19},{19,... | collective-permute-start | bytes 1572872 | tf_op jit(solution)/shard_map/ppermute | solution.py:35
  112.9 29.8 %copy-start.1 = (f32[1,64,8]{1,2,0:T(8,128)S(1)}, f32[1,64,8]{1,2,0:T(8,128)}, u32[]{:S(2)}) copy-start(f32[1,64,8]{1,2,0:T(8,128)} %param.5) | copy-start | bytes 6148
  112.9 30.9 %copy-start = (bf16[1,64,1024]{2,1,0:T(8,128)(2,1)S(1)}, bf16[1,64,1024]{2,1,0:T(8,128)(2,1)}, u32[]{:S(2)}) copy-start(bf16[1,64,1024]{2,1,0:T(8,128)(2,1)} %param.4) | copy-start | bytes 393220
  113.0 10.7 %collective-permute-start.14 = (f32[128,256]{1,0:T(8,128)S(1)}, f32[128,256]{1,0:T(8,128)S(1)}, u32[]{:S(2)}, u32[]{:S(2)}) collective-permute-start(f32[128,256]{1,0:T(8,128)S(1)} %get-tuple-element.29), channel_id=1, source_target_pairs={{1,65},{3,67},{5,81},{7,83},{9,97},{11,99},{13,113},{15,115},{17,6... | collective-permute-start | bytes 393224 | tf_op jit(solution)/shard_map/ppermute | solution.py:35
  121.1 3.2 %collective-permute-start.15 = (f32[128,256]{1,0:T(8,128)S(1)}, f32[128,256]{1,0:T(8,128)S(1)}, u32[]{:S(2)}, u32[]{:S(2)}) collective-permute-start(f32[128,256]{1,0:T(8,128)S(1)} %get-tuple-element.25), channel_id=1, source_target_pairs={{1,129},{3,131},{5,145},{7,147},{9,161},{11,163},{13,177},{15,179}... | collective-permute-start | bytes 393224 | tf_op jit(solution)/shard_map/ppermute | solution.py:35
  122.4 3.3 %collective-permute-start.16 = (f32[128,256]{1,0:T(8,128)S(1)}, f32[128,256]{1,0:T(8,128)S(1)}, u32[]{:S(2)}, u32[]{:S(2)}) collective-permute-start(f32[128,256]{1,0:T(8,128)S(1)} %get-tuple-element.24), channel_id=1, source_target_pairs={{1,193},{3,195},{5,209},{7,211},{9,225},{11,227},{13,241},{15,243}... | collective-permute-start | bytes 393224 | tf_op jit(solution)/shard_map/ppermute | solution.py:35
  126.3 17.5 %collective-permute-start.17 = (f32[4,64,256]{2,1,0:T(8,128)S(1)}, f32[4,64,256]{2,1,0:T(8,128)S(1)}, u32[]{:S(2)}, u32[]{:S(2)}) collective-permute-start(f32[4,64,256]{2,1,0:T(8,128)S(1)} %get-tuple-element.15), channel_id=1, source_target_pairs={{0,1},{1,0},{2,3},{3,2},{4,5},{5,4},{6,7},{7,6},{8,9},{9,8},{10,11... | collective-permute-start | bytes 786440 | tf_op jit(solution)/shard_map/ppermute | solution.py:35
